TPU v7x, 256 devices: a whole 4x4x8 slice. The times are simulated.
256 devices in a mesh: lat: 16 (over x, y_hi, core), lon: 16 (over y_lo, z).
Axes of the slice: x: 4, y: 4 (y_hi: 2, y_lo: 2; y = y_hi * 2 + y_lo), z: 8, core: 2. Of those that a mesh axis runs over, the one named last changes fastest.
Arguments:
- obs_values: float32 [30, 8192], P(None, ('lat', 'lon')), may hold values from -6 to 6
- obs_lat: int32 [8192], P(('lat', 'lon')), may hold values from 0 to 255, as said below
- obs_lon: int32 [8192], P(('lat', 'lon')), may hold values from 0 to 4095, as said below
- instrument: int32 [8192], P(('lat', 'lon')), may hold values from 0 to 3
- length_scale: float32 [4], replicated, may hold values from 2 to 32
- w_first: bfloat16 [3, 3, 64, 124], replicated, may hold values from -0.1875 to 0.1875
- b_first: float32 [64], replicated, may hold values from -3 to 3
- w_second: bfloat16 [3, 3, 64, 64], replicated, may hold values from -0.25 to 0.25
- b_second: float32 [64], replicated, may hold values from -3 to 3
Outputs:
- encoded: bfloat16 [64, 256, 4096], P(None, 'lat', 'lon')
Inputs may be any that keep to these rules, and one draw needn't show every extreme that they name: `obs_lon`: the rows held by ingest device q (rows q * 32 to (q + 1) * 32 - 1, devices counted with lat slowest and lon fastest) lie in that device's longitude band: columns b * 256 to (b + 1) * 256 - 1, with b the device's lon index. `obs_lat`: the rows held by ingest device q lie in that device's latitude band: rows a * 16 to (a + 1) * 16 - 1, with a the device's lat index.
All inputs are finite; a program needn't handle non-finite values.
Results may differ from a plain program's by a relative error of at most 0.00125.
The roundings to bfloat16 on the way count: a program that leaves them out, or rounds other values in their place, can miss the bound.
Values may be sent and summed in bfloat16 or wider, within the bound.
No kernel may reach another device: no remote copies, remote signals or barrier semaphores. Data moves between devices by JAX's collectives and lax.ppermute only.
A program may use at most 64 MiB of HBM per device.

v0:
```python
import jax
import jax.numpy as jnp
from jax import lax
from jax.sharding import PartitionSpec as P

CLAT = 16
CLON = 256


def with_halo(array, sides, width, wrap):
    for axis, dim in sides:
        peers, length = (lax.axis_size(axis), array.shape[dim])
        up = [(i, (i + 1) % peers) for i in range(peers if wrap else peers - 1)]
        down = [(j, i) for i, j in up]
        last = lax.slice_in_dim(array, length - width, length, axis=dim)
        first = lax.slice_in_dim(array, 0, width, axis=dim)
        before = lax.ppermute(last, axis, up)
        after = lax.ppermute(first, axis, down)
        array = jnp.concatenate([before, array, after], axis=dim)
    return array


def features_of(sums, instruments, values):
    shaped = sums.reshape((instruments, values + 1) + sums.shape[1:])
    density = shaped[:, 0:1]
    result = jnp.concatenate([jnp.log1p(density), shaped[:, 1:] / (1.0 + density)], axis=1)
    return result.reshape(sums.shape).astype(jnp.bfloat16)


def conv_valid(source, weights):
    height = source.shape[1] - 2
    width = source.shape[2] - 2
    total = jnp.zeros((weights.shape[2], height, width), jnp.float32)
    for first in range(3):
        for second in range(3):
            total = total + jnp.einsum(
                "oc,chw->ohw",
                weights[first, second],
                source[:, first : first + height, second : second + width],
                preferred_element_type=jnp.float32,
            )
    return total


def body(
    obs_values, obs_lat, obs_lon, instrument, length_scale, w_first, b_first, w_second, b_second
):
    instruments = length_scale.shape[0]
    values_count = obs_values.shape[0]
    coords = jnp.stack(
        [obs_lat.astype(jnp.float32), obs_lon.astype(jnp.float32), instrument.astype(jnp.float32)]
    )
    values, places = (
        lax.all_gather(obs_values, ("lat", "lon"), axis=1, tiled=True),
        lax.all_gather(coords, ("lat", "lon"), axis=1, tiled=True),
    )
    count = values.shape[1]
    table = 0.5 / (length_scale * length_scale)
    onehot = (places[2][None, :] == jnp.arange(instruments, dtype=jnp.float32)[:, None]).astype(
        jnp.float32
    )
    rate = jnp.sum(onehot * table[:, None], axis=0)
    reach = jnp.sum(onehot * (4.0 * length_scale)[:, None], axis=0)
    augmented = jnp.concatenate([jnp.ones((1, count), jnp.float32), values], axis=0)
    channels = (onehot[:, None, :] * augmented[None, :, :]).reshape(
        instruments * (values_count + 1), count
    )
    total_lon = float(CLON * lax.axis_size("lon"))
    lat_first = lax.axis_index("lat") * CLAT
    lon_first = (lax.axis_index("lon") * CLON).astype(jnp.float32)
    columns = lon_first + jnp.arange(CLON).astype(jnp.float32)
    offset = jnp.mod(columns[:, None] - places[1][None, :], total_lon)
    dist = jnp.minimum(offset, total_lon - offset)
    lon_kernel = jnp.where(
        dist <= reach[None, :], jnp.exp(-dist * dist * rate[None, :]), 0.0
    ).astype(jnp.bfloat16)
    grid_rows = lat_first.astype(jnp.float32) + jnp.arange(CLAT).astype(jnp.float32)

    def one_row(row):
        gap = row - places[0]
        lat_k = jnp.where(jnp.abs(gap) <= reach, jnp.exp(-(gap * gap) * rate), 0.0)
        weighted = (lat_k[None, :] * channels).astype(jnp.bfloat16)
        sums = lax.dot_general(
            weighted, lon_kernel, (((1,), (1,)), ((), ())), preferred_element_type=jnp.float32
        )
        return features_of(sums, instruments, values_count)

    feats = jnp.transpose(lax.map(one_row, grid_rows), (1, 0, 2))
    extended = with_halo(feats, (("lon", 2),), 1, True)
    extended = with_halo(extended, (("lat", 1),), 1, False)
    hidden = jax.nn.silu(conv_valid(extended, w_first) + b_first[:, None, None]).astype(
        jnp.bfloat16
    )
    border = with_halo(hidden, (("lon", 2),), 1, True)
    border = with_halo(border, (("lat", 1),), 1, False)
    out = conv_valid(border, w_second) + b_second[:, None, None]
    return out.astype(jnp.bfloat16)


def solution(mesh):
    return jax.shard_map(
        body,
        mesh=mesh,
        in_specs=(
            P(None, ("lat", "lon")),
            P(("lat", "lon")),
            P(("lat", "lon")),
            P(("lat", "lon")),
            P(),
            P(),
            P(),
            P(),
            P(),
        ),
        out_specs=P(None, "lat", "lon"),
        check_vma=False,
    )
```

profile of v0, /device:TPU:1, one launch (start us, length us, event | category | flops | bytes accessed | tf_op | source)
XLA Modules:
  0.0 1664.8 jit_solution(7597191678812809108)
XLA Ops:
  1.4 599.4 %all-gather = f32[256,32,3]{1,2,0:T(4,128)S(1)} all-gather(f32[1,32,3]{1,2,0:T(4,128)S(1)} %maximum_bitcast_fusion), channel_id=1, replica_groups=mesh['lat'=16,'lon'=16] {'lat','lon'}, dimensions={0}, use_global_device_ids=true | all-gather | bytes 98688 | tf_op jit(solution)/shard_map/all_gather | solution.py:55
  603.5 682.0 %all_gather.7 = f32[30,8192]{0,1:T(8,128)} all-gather(f32[30,32]{0,1:T(8,128)S(1)} %copy.14), channel_id=1, replica_groups=mesh['lat'=16,'lon'=16] {'lat','lon'}, dimensions={1}, use_global_device_ids=true | all-gather | bytes 986880 | tf_op jit(solution)/shard_map/all_gather | solution.py:54
  1288.7 295.9 %while.12 = (s32[]{:T(128)}, bf16[16,124,256]{2,1,0:T(8,128)(2,1)S(1)}, f32[16]{0:T(128)S(1)}, f32[3,8192]{1,0:T(4,128)}, f32[8192]{0:T(1024)S(1)}, /*index=5*/f...) while((s32[]{:T(128)}, ...), condition=%wide.region_3.4_spmd.clone.clone, body=%wide.region_2.3_spmd.clone.clone.sunk | while | flops 554846208 | bytes 18635912 | solution.py:88
  1291.1 4.6 mul.198
  1298.0 9.0 fusion.115
  1309.6 4.6 mul.198
  1316.5 9.0 fusion.115
  1328.1 4.6 mul.198
  1335.0 9.0 fusion.115
  1346.6 4.6 mul.198
  1353.5 9.0 fusion.115
  1365.1 4.6 mul.198
  1372.0 9.0 fusion.115
  1383.6 4.6 mul.198
  1390.4 9.0 fusion.115
  1402.1 4.6 mul.198
  1408.9 9.0 fusion.115
  1420.6 4.6 mul.198
  1427.4 9.0 fusion.115
  1439.1 4.6 mul.198
  1445.9 9.0 fusion.115
  1457.6 4.6 mul.198
  1464.4 9.0 fusion.115
  1482.9 9.0 fusion.115
  1501.4 9.0 fusion.115
  1519.9 9.0 fusion.115
  1538.4 9.0 fusion.115
  1556.9 9.0 fusion.115
  1575.4 9.0 fusion.115
  1586.7 6.2 collective-permute-done.1
  1597.2 36.4 %collective-permute-start.3 = (bf16[124,1,258]{2,0,1:T(8,128)(2,1)S(1)}, bf16[124,1,258]{2,0,1:T(8,128)(2,1)S(1)}, u32[]{:S(2)}, u32[]{:S(2)}) collective-permute-start(bf16[124,1,258]{2,0,1:T(8,128)(2,1)S(1)} %get-tuple-element.145), channel_id=1, source_target_pairs={{16,0},{32,16},{48,32},{64,48},{80,64},{96,80},{112,96},{128,112},... | collective-permute-start | bytes 191960 | tf_op jit(solution)/shard_map/ppermute | solution.py:18
  1643.0 5.8 collective-permute-done.5
  (229 shorter events, 143.2 us)
Async XLA Ops:
  0.0 603.4 %copy-start.2 = (f32[30,32]{1,0:T(8,128)S(1)}, f32[30,32]{1,0:T(8,128)}, u32[]{:S(2)}) copy-start(f32[30,32]{1,0:T(8,128)} %param.11) | copy-start | bytes 11524
  1584.6 1.9 copy-start.1
  1584.8 8.1 collective-permute-start.1
  1584.9 10.2 collective-permute-start
  1595.3 38.9 %collective-permute-start.2 = (bf16[124,1,258]{2,0,1:T(8,128)(2,1)S(1)}, bf16[124,1,258]{2,0,1:T(8,128)(2,1)S(1)}, u32[]{:S(2)}, u32[]{:S(2)}) collective-permute-start(bf16[124,1,258]{2,0,1:T(8,128)(2,1)S(1)} %get-tuple-element.144), channel_id=1, source_target_pairs={{0,16},{16,32},{32,48},{48,64},{64,80},{80,96},{96,112},{112,128},... | collective-permute-start | bytes 191960 | tf_op jit(solution)/shard_map/ppermute | solution.py:17
  1597.2 37.1 %collective-permute-start.3 = (bf16[124,1,258]{2,0,1:T(8,128)(2,1)S(1)}, bf16[124,1,258]{2,0,1:T(8,128)(2,1)S(1)}, u32[]{:S(2)}, u32[]{:S(2)}) collective-permute-start(bf16[124,1,258]{2,0,1:T(8,128)(2,1)S(1)} %get-tuple-element.145), channel_id=1, source_target_pairs={{16,0},{32,16},{48,32},{64,48},{80,64},{96,80},{112,96},{128,112},... | collective-permute-start | bytes 191960 | tf_op jit(solution)/shard_map/ppermute | solution.py:18
  1639.3 0.7 copy-start.4
  1640.0 2.7 copy-start
  1641.2 7.6 collective-permute-start.5
  1641.3 9.8 collective-permute-start.4
  1651.1 4.8 collective-permute-start.6
  1653.1 6.9 collective-permute-start.7
  1662.4 0.7 copy-start.3
where the time goes:
time: 1670 us; the launch traced here: 1660 us
  blocking collectives  1280 us (77%)
  matrix products  153 us (9%)
  local copies, waits for them, and re-layouts  91.6 us (5%)
  other arithmetic  71.4 us (4%)
  starting transfers between devices  45.8 us (3%)
  waiting for transfers between devices  20.5 us (1%)
    all_gather x1, blocking collectives, body(): lax.all_gather(obs_values, ('lat', 'lon'), axis=1, tiled=True)  682 us
    all_gather x1, blocking collectives, body(): lax.all_gather(coords, ('lat', 'lon'), axis=1, tiled=True)  599 us
    dot_general x16, matrix products, one_row(): lax.dot_general(weighted, lon_kernel, (((1,), (1,)), ((), ())), preferred...  144 us
    mul x16, local copies, waits for them, and re-layouts, body(): onehot[:, None, :] * augmented[None, :, :]  74.1 us
    ppermute x4, starting transfers between devices, with_halo(): after = lax.ppermute(first, axis, down)  39 us
    mul x16, other arithmetic, body(): onehot[:, None, :] * augmented[None, :, :]  38.8 us
  transfers between devices with their start and end apart: 8, of which 6 were waited for; matrix products, arithmetic and copies ran while one was open for 0% of the time, Pallas kernels for 0%

commit v1 on v0

v1 whole, which is shorter than its diff:
```python
import jax
import jax.numpy as jnp
from jax import lax
from jax.experimental import pallas as pl
from jax.experimental.pallas import tpu as pltpu
from jax.sharding import PartitionSpec as P

CLAT = 16
CLON = 256
INSTR = 4
VALUES = 30
CHANNELS = 64
SLOT = 32
NLAT = 256
NLON = 4096
ROWS_DEV = 32
EXT = CLAT + 4
HID = CLAT + 2
WIDE = 384
BAND = 512
LOG2E = 1.4426950408889634
NT = (((1,), (1,)), ((), ()))
NN = (((1,), (0,)), ((), ()))


def dot(a, b, dims=NN):
    return lax.dot_general(a, b, dims, preferred_element_type=jnp.float32)


def encode_kernel(
    scale_ref, first_ref, minus_ref, own_ref, plus_ref, w1_ref, b1_ref, w2_ref, b2_ref,
    out_ref, wt, la, lb, lc, sa, sb, sc, feat, hid, stage,
):
    lat_first = first_ref[0]
    lon_first = first_ref[1]
    lat_first_f = lat_first.astype(jnp.float32)
    lon_first_f = lon_first.astype(jnp.float32)
    grid_row = lax.broadcasted_iota(jnp.int32, (24, 128), 0) + (lat_first - 2)
    row_ok = (grid_row >= 0) & (grid_row < NLAT)
    grid_row = grid_row.astype(jnp.float32)
    sub = lax.broadcasted_iota(jnp.int32, (128, 128), 0)
    col_a = sub.astype(jnp.float32)
    col_b = (sub + 128).astype(jnp.float32)
    inst_c = ((sub + 16) // 32) % 4
    edge = sub - 32 * inst_c
    edge = jnp.where(edge > 64, edge - 128, edge)
    col_c = jnp.where(edge >= 0, edge + 256, edge).astype(jnp.float32)
    inst_c = inst_c.astype(jnp.float32)

    for part, ref in enumerate((minus_ref, own_ref, plus_ref)):
        for block in range(4):
            at = part * BAND + block * 128
            data = ref[block]
            lat = data[0:1]
            lon = data[31:32]
            inst = data[32:33]
            scale = jnp.zeros_like(lat)
            for k in range(INSTR):
                scale = jnp.where(inst == float(k), scale_ref[k], scale)
            rate = -LOG2E * (0.5 / (scale * scale))
            reach = 4.0 * scale
            rel = lon - lon_first_f
            rel = jnp.where(rel > NLON / 2, rel - NLON, rel)
            rel = jnp.where(rel < -NLON / 2, rel + NLON, rel)
            gap = grid_row - lat
            lat_k = jnp.where(
                (jnp.abs(gap) <= reach) & row_ok, jnp.exp2(gap * gap * rate), 0.0
            )
            which = lax.broadcasted_iota(jnp.int32, (SLOT, 128), 0)
            aug = jnp.where(which == 0, 1.0, jnp.where(which == 31, 0.0, data[0:SLOT]))
            for i in range(EXT):
                wt[i * SLOT : (i + 1) * SLOT, at : at + 128] = (lat_k[i : i + 1] * aug).astype(
                    jnp.bfloat16
                )

            def lon_k(col):
                dist = jnp.abs(col - rel)
                return jnp.where(dist <= reach, jnp.exp2(dist * dist * rate), 0.0)

            for use, col, ref_l, base in (
                (part < 2, col_a, la, at),
                (part > 0, col_b, lb, at - BAND),
            ):
                if use:
                    ker = lon_k(col)
                    for k in range(INSTR):
                        ref_l[k * 128 : (k + 1) * 128, base : base + 128] = jnp.where(
                            inst == float(k), ker, 0.0
                        ).astype(jnp.bfloat16)
            lc[:, at : at + 128] = jnp.where(inst == inst_c, lon_k(col_c), 0.0).astype(
                jnp.bfloat16
            )

    for pair in range(2):
        rows = slice(pair * 256, (pair + 1) * 256)
        sa[:, rows] = dot(wt[:, 0 : 2 * BAND], la[rows, :], NT)
        sb[:, rows] = dot(wt[:, BAND : 3 * BAND], lb[rows, :], NT)
    sc[...] = dot(wt[...], lc[...], NT)

    slot_row = lax.broadcasted_iota(jnp.int32, (SLOT, WIDE), 0)
    for i in range(EXT):
        rows = slice(i * SLOT, (i + 1) * SLOT)
        edges = sc[rows, :]
        for k in range(INSTR):
            lanes = slice(k * 128, (k + 1) * 128)
            edge_k = edges if k == 0 else pltpu.roll(edges, 128 - 32 * k, 1)
            sums = jnp.concatenate([sa[rows, lanes], sb[rows, lanes], edge_k], axis=1)
            density = sums[0:1]
            inverse = 1.0 / (1.0 + density)
            value = jnp.where(slot_row == 0, jnp.log1p(density), sums * inverse)
            feat[i * 128 + k * SLOT : i * 128 + (k + 1) * SLOT, :] = value.astype(jnp.bfloat16)

    w1 = w1_ref[...]
    b1 = b1_ref[...]
    for pair in range(HID // 2):
        h = 2 * pair
        x = jnp.concatenate(
            [feat[h * 128 : (h + 3) * 128, :], feat[(h + 1) * 128 : (h + 4) * 128, :]], axis=1
        )
        y = dot(w1, x)
        for n in range(2):
            lanes = slice(n * WIDE, (n + 1) * WIDE)
            pre = (
                y[64:128, lanes]
                + pltpu.roll(y[0:64, lanes], 1, 1)
                + pltpu.roll(y[128:192, lanes], WIDE - 1, 1)
                + b1
            )
            act = pre / (1.0 + jnp.exp(-pre))
            row = lat_first - 1 + h + n
            if h + n in (0, HID - 1):
                act = jnp.where((row >= 0) & (row < NLAT), act, 0.0)
            hid[(h + n) * 64 : (h + n + 1) * 64, :] = act.astype(jnp.bfloat16)

    w2 = w2_ref[...]
    b2 = b2_ref[...]
    for pair in range(CLAT // 2):
        r = 2 * pair
        x = jnp.concatenate(
            [hid[r * 64 : (r + 3) * 64, :], hid[(r + 1) * 64 : (r + 4) * 64, :]], axis=1
        )
        y = dot(w2, x)
        for n in range(2):
            lanes = slice(n * WIDE, (n + 1) * WIDE)
            total = (
                y[64:128, lanes]
                + pltpu.roll(y[0:64, lanes], 1, 1)
                + pltpu.roll(y[128:192, lanes], WIDE - 1, 1)
            )[:, 0:CLON] + b2
            stage[pl.ds(r + n, CHANNELS, CLAT), :] = total[:, 0:128]
            stage[pl.ds(CHANNELS * CLAT + r + n, CHANNELS, CLAT), :] = total[:, 128:256]
    half = CHANNELS * CLAT
    for n in range(2):
        out_ref[:, :, n * 128 : (n + 1) * 128] = (
            stage[n * half : (n + 1) * half, :].reshape(CHANNELS, CLAT, 128).astype(jnp.bfloat16)
        )


def encode(scale, first, minus, own, plus, w1, b1, w2, b2):
    vmem = pl.BlockSpec(memory_space=pltpu.VMEM)
    smem = pl.BlockSpec(memory_space=pltpu.SMEM)
    bf16, f32 = jnp.bfloat16, jnp.float32
    return pl.pallas_call(
        encode_kernel,
        out_shape=jax.ShapeDtypeStruct((CHANNELS, CLAT, CLON), bf16),
        in_specs=[smem, smem] + [vmem] * 7,
        out_specs=vmem,
        scratch_shapes=[
            pltpu.VMEM((EXT * SLOT, 3 * BAND), bf16),
            pltpu.VMEM((INSTR * 128, 2 * BAND), bf16),
            pltpu.VMEM((INSTR * 128, 2 * BAND), bf16),
            pltpu.VMEM((128, 3 * BAND), bf16),
            pltpu.VMEM((EXT * SLOT, INSTR * 128), f32),
            pltpu.VMEM((EXT * SLOT, INSTR * 128), f32),
            pltpu.VMEM((EXT * SLOT, 128), f32),
            pltpu.VMEM((EXT * 128, WIDE), bf16),
            pltpu.VMEM((HID * CHANNELS, WIDE), bf16),
            pltpu.VMEM((2 * CHANNELS * CLAT, 128), f32),
        ],
        compiler_params=pltpu.CompilerParams(vmem_limit_bytes=48 * 1024 * 1024),
    )(scale, first, minus, own, plus, w1, b1, w2, b2)


def send(array, axis, target):
    peers = lax.axis_size(axis)
    return lax.ppermute(array, axis, [(i, target(i) % peers) for i in range(peers)])


def body(
    obs_values, obs_lat, obs_lon, instrument, length_scale, w_first, b_first, w_second, b_second
):
    f32 = jnp.float32
    rows = jnp.concatenate(
        [
            obs_lat.astype(f32)[None],
            obs_values,
            obs_lon.astype(f32)[None],
            instrument.astype(f32)[None],
            jnp.zeros((7, ROWS_DEV), f32),
        ],
        axis=0,
    )
    rows = jnp.concatenate([rows, send(rows, "lat", lambda i: i ^ 1)], axis=1)
    rows = jnp.concatenate([rows, send(rows, "lat", lambda i: i ^ 2)], axis=1)
    rows = jnp.stack([rows] + [send(rows, "lat", lambda i, k=k: i + 4 * k) for k in (1, 2, 3)])
    minus = send(rows, "lon", lambda i: i + 1)
    plus = send(rows, "lon", lambda i: i - 1)
    first = jnp.stack([lax.axis_index("lat") * CLAT, lax.axis_index("lon") * CLON])
    w1 = jnp.pad(
        w_first.reshape(3, 3, CHANNELS, INSTR, VALUES + 1), ((0, 0),) * 4 + ((0, 1),)
    )
    w1 = jnp.transpose(w1, (1, 2, 0, 3, 4)).reshape(3 * CHANNELS, 3 * INSTR * SLOT)
    w2 = jnp.transpose(w_second, (1, 2, 0, 3)).reshape(3 * CHANNELS, 3 * CHANNELS)
    return encode(
        length_scale, first, minus, rows, plus, w1, b_first[:, None], w2, b_second[:, None]
    )


def solution(mesh):
    return jax.shard_map(
        body,
        mesh=mesh,
        in_specs=(
            P(None, ("lat", "lon")),
            P(("lat", "lon")),
            P(("lat", "lon")),
            P(("lat", "lon")),
            P(),
            P(),
            P(),
            P(),
            P(),
        ),
        out_specs=P(None, "lat", "lon"),
        check_vma=False,
    )
```

time: 1670 us -> 34 us (0.02)
  the two profiles are of different devices: /device:TPU:1 before, /device:TPU:16 now
where the time goes in v1:
time: 34 us; the launch traced here: 33.8 us
  starting transfers between devices  14.6 us (43%)
  Pallas kernels  7.63 us (22%)
  waiting for transfers between devices  5.41 us (16%)
  local copies, waits for them, and re-layouts  5.14 us (15%)
  other arithmetic  0.93 us (3%)
    ppermute x7, starting transfers between devices, send(): lax.ppermute(array, axis, [(i, target(i) % peers) for i in range(peers)])  14.6 us
    pallas_call x1, Pallas kernels, encode(): pl.pallas_call(encode_kernel, out_shape=jax.ShapeDtypeStruct((CHANNELS, C...  7.63 us
    ppermute x7, waiting for transfers between devices, send(): lax.ppermute(array, axis, [(i, target(i) % peers) for i in range(peers)])  5.41 us
    unnamed x13, local copies, waits for them, and re-layouts  3.01 us
    concatenate x1, local copies, waits for them, and re-layouts, body(): jnp.concatenate([obs_lat.astype(f32)[None], obs_values, obs_lon.astype(f3...  0.84 us
    broadcast_in_dim x1, other arithmetic, body(): obs_lat.astype(f32)[None]  0.68 us
  transfers between devices with their start and end apart: 7, of which 3 were waited for; matrix products, arithmetic and copies ran while one was open for 7% of the time, Pallas kernels for 0%

profile of v1, /device:TPU:16, one launch (start us, length us, event | category | flops | bytes accessed | tf_op | source)
XLA Modules:
  0.0 33.8 jit_solution(16276877848953786054)
XLA Ops:
  0.0 0.7 %convert_bitcast_fusion.2 = f32[1,32]{1,0:T(1,128)S(1)} fusion(s32[32]{0:T(128)} %param.10), kind=kLoop, calls=%fused_computation.7 | loop fusion | flops 32 | bytes 256 | tf_op jit(solution)/shard_map/broadcast_in_dim | solution.py:195
  0.7 0.8 %concatenate.10 = f32[40,32]{1,0:T(8,128)S(1)} concatenate(f32[1,32]{1,0:T(1,128)S(1)} %convert_bitcast_fusion.2, f32[30,32]{1,0:T(8,128)} %param.9, f32[1,32]{1,0:T(1,128)S(1)} %get-tuple-element.6, f32[1,32]{1,0:T(1,128)S(1)} %get-tuple-element.5, f32[7,32]{1,0:T(8,128)S(1)} %broadcast_in_dim.21), dimensions={0} | concatenate | bytes 10240 | tf_op jit(solution)/shard_map/concatenate | solution.py:193
  1.6 0.1 collective-permute-start
  1.6 1.2 %collective-permute-done = f32[40,32]{1,0:T(8,128)S(1)} collective-permute-done((f32[40,32]{1,0:T(8,128)S(1)}, f32[40,32]{1,0:T(8,128)S(1)}, u32[]{:S(2)}, u32[]{:S(2)}) %collective-permute-start) | collective-permute-done | bytes 5152 | tf_op jit(solution)/shard_map/ppermute | solution.py:186
  2.8 0.1 pad_maximum_fusion.1
  2.9 2.1 %collective-permute-start.1 = (f32[40,64]{1,0:T(8,128)S(1)}, f32[40,64]{1,0:T(8,128)S(1)}, u32[]{:S(2)}, u32[]{:S(2)}) collective-permute-start(f32[40,64]{1,0:T(8,128)S(1)} %pad_maximum_fusion.1), channel_id=1, source_target_pairs={{0,32},{16,48},{32,0},{48,16},{64,96},{80,112},{96,64},{112,80},{1... | collective-permute-start | bytes 30728 | tf_op jit(solution)/shard_map/ppermute | solution.py:186
  5.0 1.1 %copy.14 = bf16[3,3,64,124]{2,3,1,0:T(8,128)(2,1)S(1)} copy(bf16[3,3,64,124]{3,2,1,0:T(8,128)(2,1)} %param.14) | data formatting | bytes 285696 | tf_op args[5]
  6.1 0.1 reshape.9
  6.2 2.0 %collective-permute-done.1 = f32[40,64]{1,0:T(8,128)S(1)} collective-permute-done((f32[40,64]{1,0:T(8,128)S(1)}, f32[40,64]{1,0:T(8,128)S(1)}, u32[]{:S(2)}, u32[]{:S(2)}) %collective-permute-start.1) | collective-permute-done | bytes 10272 | tf_op jit(solution)/shard_map/ppermute | solution.py:186
  8.2 0.1 pad_maximum_fusion.2
  8.3 1.5 %collective-permute-start.2 = (f32[40,128]{1,0:T(8,128)S(1)}, f32[40,128]{1,0:T(8,128)S(1)}, u32[]{:S(2)}, u32[]{:S(2)}) collective-permute-start(f32[40,128]{1,0:T(8,128)S(1)} %pad_maximum_fusion.2), channel_id=1, source_target_pairs={{0,64},{16,80},{32,96},{48,112},{64,128},{80,144},{96,160},{112,17... | collective-permute-start | bytes 61448 | tf_op jit(solution)/shard_map/ppermute | solution.py:186
  9.8 2.7 %collective-permute-start.3 = (f32[40,128]{1,0:T(8,128)S(1)}, f32[40,128]{1,0:T(8,128)S(1)}, u32[]{:S(2)}, u32[]{:S(2)}) collective-permute-start(f32[40,128]{1,0:T(8,128)S(1)} %pad_maximum_fusion.2), channel_id=1, source_target_pairs={{0,128},{16,144},{32,160},{48,176},{64,192},{80,208},{96,224},{112... | collective-permute-start | bytes 61448 | tf_op jit(solution)/shard_map/ppermute | solution.py:186
  12.5 1.4 %collective-permute-start.4 = (f32[40,128]{1,0:T(8,128)S(1)}, f32[40,128]{1,0:T(8,128)S(1)}, u32[]{:S(2)}, u32[]{:S(2)}) collective-permute-start(f32[40,128]{1,0:T(8,128)S(1)} %pad_maximum_fusion.2), channel_id=1, source_target_pairs={{0,192},{16,208},{32,224},{48,240},{64,0},{80,16},{96,32},{112,48}... | collective-permute-start | bytes 61448 | tf_op jit(solution)/shard_map/ppermute | solution.py:186
  14.0 0.1 pad_bitcast_fusion
  14.0 0.3 copy.20
  14.3 0.0 copy-start.1
  14.3 0.3 %reshape.12.w1_ref = bf16[192,384]{1,0:T(8,128)(2,1)S(1)} reshape(bf16[3,64,3,4,32]{4,3,2,1,0:T(4,128)(2,1)S(1)} %copy.20) | data formatting | bytes 294912 | tf_op jit(solution)/shard_map/reshape | solution.py:212
  14.7 0.6 %copy-done.1 = bf16[3,3,64,64]{3,2,1,0:T(8,128)(2,1)S(1)} copy-done((bf16[3,3,64,64]{3,2,1,0:T(8,128)(2,1)S(1)}, bf16[3,3,64,64]{3,2,1,0:T(8,128)(2,1)}, u32[]{:S(2)}) %copy-start.1) | copy-done | bytes 73752
  15.2 0.1 copy.16
  15.4 0.2 reshape.11.w2_ref
  15.5 0.7 %copy-done.2 = f32[64]{0:T(128)S(1)} copy-done((f32[64]{0:T(128)S(1)}, f32[64]{0:T(128)}, u32[]{:S(2)}) %copy-start.2) | copy-done | bytes 280
  16.2 0.1 copy.18.b1_ref
  16.3 0.7 %copy-done.3 = f32[64]{0:T(128)S(1)} copy-done((f32[64]{0:T(128)S(1)}, f32[64]{0:T(128)}, u32[]{:S(2)}) %copy-start.3) | copy-done | bytes 280
  16.9 0.1 copy.19.b2_ref
  17.0 0.0 collective-permute-done.2
  17.0 0.0 collective-permute-done.3
  17.1 0.0 collective-permute-done.4
  17.1 2.0 %collective-permute-start.5 = (f32[4,40,128]{2,1,0:T(8,128)S(1)}, f32[4,40,128]{2,1,0:T(8,128)S(1)}, u32[]{:S(2)}, u32[]{:S(2)}) collective-permute-start(f32[4,40,128]{2,1,0:T(8,128)S(1)} %pad_maximum_fusion.own_ref), channel_id=1, source_target_pairs={{0,1},{1,2},{2,3},{3,4},{4,5},{5,6},{6,7},{7,8},{8,9},{9,10},{10,1... | collective-permute-start | bytes 245768 | tf_op jit(solution)/shard_map/ppermute | solution.py:186
  19.1 4.7 %collective-permute-start.6 = (f32[4,40,128]{2,1,0:T(8,128)S(1)}, f32[4,40,128]{2,1,0:T(8,128)S(1)}, u32[]{:S(2)}, u32[]{:S(2)}) collective-permute-start(f32[4,40,128]{2,1,0:T(8,128)S(1)} %pad_maximum_fusion.own_ref), channel_id=1, source_target_pairs={{0,15},{1,0},{2,1},{3,2},{4,3},{5,4},{6,5},{7,6},{8,7},{9,8},{10,9... | collective-permute-start | bytes 245768 | tf_op jit(solution)/shard_map/ppermute | solution.py:186
  23.8 0.1 pad_add_fusion.first_ref
  23.9 2.3 %collective-permute-done.5.minus_ref = f32[4,40,128]{2,1,0:T(8,128)S(1)} collective-permute-done((f32[4,40,128]{2,1,0:T(8,128)S(1)}, f32[4,40,128]{2,1,0:T(8,128)S(1)}, u32[]{:S(2)}, u32[]{:S(2)}) %collective-permute-start.5) | collective-permute-done | bytes 81952 | tf_op jit(solution)/shard_map/ppermute | solution.py:186
  26.2 7.6 %shard_map.91 = bf16[64,16,256]{2,1,0:T(8,128)(2,1)} custom-call(f32[4]{0:T(128)S(1)} %copy-done, s32[2]{0:T(128)S(1)} %pad_add_fusion.first_ref, f32[4,40,128]{2,1,0:T(8,128)S(1)} %collective-permute-done.5.minus_ref, f32[4,40,128]{2,1,0:T(8,128)S(1)} %pad_maximum_fusion.own_ref, f32[4,40,128]{2,1,0:T(8,128)S(1)} %collective-permute-done.6.plus_ref, ...), custom_call_target="tpu_custom_call" | custom-call | tf_op jit(solution)/shard_map/pallas_call | solution.py:163
  (12 shorter events, 0.0 us)
Async XLA Ops:
  0.0 0.7 %copy-start.5 = (s32[32]{0:T(128)S(1)}, s32[32]{0:T(128)}, u32[]{:S(2)}) copy-start(s32[32]{0:T(128)} %param.11) | copy-start | bytes 388
  0.0 0.7 %copy-start.4 = (s32[32]{0:T(128)S(1)}, s32[32]{0:T(128)}, u32[]{:S(2)}) copy-start(s32[32]{0:T(128)} %param.12) | copy-start | bytes 388
  1.6 1.3 %collective-permute-start = (f32[40,32]{1,0:T(8,128)S(1)}, f32[40,32]{1,0:T(8,128)S(1)}, u32[]{:S(2)}, u32[]{:S(2)}) collective-permute-start(f32[40,32]{1,0:T(8,128)S(1)} %concatenate.10), channel_id=1, source_target_pairs={{0,16},{16,0},{32,48},{48,32},{64,80},{80,64},{96,112},{112,96},{1... | collective-permute-start | bytes 15368 | tf_op jit(solution)/shard_map/ppermute | solution.py:186
  2.9 5.3 %collective-permute-start.1 = (f32[40,64]{1,0:T(8,128)S(1)}, f32[40,64]{1,0:T(8,128)S(1)}, u32[]{:S(2)}, u32[]{:S(2)}) collective-permute-start(f32[40,64]{1,0:T(8,128)S(1)} %pad_maximum_fusion.1), channel_id=1, source_target_pairs={{0,32},{16,48},{32,0},{48,16},{64,96},{80,112},{96,64},{112,80},{1... | collective-permute-start | bytes 30728 | tf_op jit(solution)/shard_map/ppermute | solution.py:186
  8.3 8.8 %collective-permute-start.2 = (f32[40,128]{1,0:T(8,128)S(1)}, f32[40,128]{1,0:T(8,128)S(1)}, u32[]{:S(2)}, u32[]{:S(2)}) collective-permute-start(f32[40,128]{1,0:T(8,128)S(1)} %pad_maximum_fusion.2), channel_id=1, source_target_pairs={{0,64},{16,80},{32,96},{48,112},{64,128},{80,144},{96,160},{112,17... | collective-permute-start | bytes 61448 | tf_op jit(solution)/shard_map/ppermute | solution.py:186
  9.8 7.3 %collective-permute-start.3 = (f32[40,128]{1,0:T(8,128)S(1)}, f32[40,128]{1,0:T(8,128)S(1)}, u32[]{:S(2)}, u32[]{:S(2)}) collective-permute-start(f32[40,128]{1,0:T(8,128)S(1)} %pad_maximum_fusion.2), channel_id=1, source_target_pairs={{0,128},{16,144},{32,160},{48,176},{64,192},{80,208},{96,224},{112... | collective-permute-start | bytes 61448 | tf_op jit(solution)/shard_map/ppermute | solution.py:186
  12.5 4.5 %collective-permute-start.4 = (f32[40,128]{1,0:T(8,128)S(1)}, f32[40,128]{1,0:T(8,128)S(1)}, u32[]{:S(2)}, u32[]{:S(2)}) collective-permute-start(f32[40,128]{1,0:T(8,128)S(1)} %pad_maximum_fusion.2), channel_id=1, source_target_pairs={{0,192},{16,208},{32,224},{48,240},{64,0},{80,16},{96,32},{112,48}... | collective-permute-start | bytes 61448 | tf_op jit(solution)/shard_map/ppermute | solution.py:186
  14.3 0.9 %copy-start.1 = (bf16[3,3,64,64]{3,2,1,0:T(8,128)(2,1)S(1)}, bf16[3,3,64,64]{3,2,1,0:T(8,128)(2,1)}, u32[]{:S(2)}) copy-start(bf16[3,3,64,64]{3,2,1,0:T(8,128)(2,1)} %param.16) | copy-start | bytes 221188
  15.5 0.7 %copy-start.2 = (f32[64]{0:T(128)S(1)}, f32[64]{0:T(128)}, u32[]{:S(2)}) copy-start(f32[64]{0:T(128)} %param.15) | copy-start | bytes 772
  16.3 0.7 %copy-start.3 = (f32[64]{0:T(128)S(1)}, f32[64]{0:T(128)}, u32[]{:S(2)}) copy-start(f32[64]{0:T(128)} %param.17) | copy-start | bytes 772
  17.1 9.1 %collective-permute-start.5 = (f32[4,40,128]{2,1,0:T(8,128)S(1)}, f32[4,40,128]{2,1,0:T(8,128)S(1)}, u32[]{:S(2)}, u32[]{:S(2)}) collective-permute-start(f32[4,40,128]{2,1,0:T(8,128)S(1)} %pad_maximum_fusion.own_ref), channel_id=1, source_target_pairs={{0,1},{1,2},{2,3},{3,4},{4,5},{5,6},{6,7},{7,8},{8,9},{9,10},{10,1... | collective-permute-start | bytes 245768 | tf_op jit(solution)/shard_map/ppermute | solution.py:186
  19.1 7.1 %collective-permute-start.6 = (f32[4,40,128]{2,1,0:T(8,128)S(1)}, f32[4,40,128]{2,1,0:T(8,128)S(1)}, u32[]{:S(2)}, u32[]{:S(2)}) collective-permute-start(f32[4,40,128]{2,1,0:T(8,128)S(1)} %pad_maximum_fusion.own_ref), channel_id=1, source_target_pairs={{0,15},{1,0},{2,1},{3,2},{4,3},{5,4},{6,5},{7,6},{8,7},{9,8},{10,9... | collective-permute-start | bytes 245768 | tf_op jit(solution)/shard_map/ppermute | solution.py:186
  23.8 2.3 %copy-start = (f32[4]{0:T(128)S(1)}, f32[4]{0:T(128)}, u32[]{:S(2)}) copy-start(f32[4]{0:T(128)} %scale_ref.1) | copy-start | bytes 52

commit v2 on v1

v2 whole, which is shorter than its diff:
```python
import jax
import jax.numpy as jnp
from jax import lax
from jax.experimental import pallas as pl
from jax.experimental.pallas import tpu as pltpu
from jax.sharding import PartitionSpec as P

CLAT = 16
CLON = 256
INSTR = 4
VALUES = 30
CHANNELS = 64
CIN = 124
SLOT = 32
NLAT = 256
NLON = 4096
ROWS_DEV = 32
EXT = CLAT + 4
HID = CLAT + 2
WIDE = 384
BAND = 512
LOG2E = 1.4426950408889634
NT = (((1,), (1,)), ((), ()))
NN = (((1,), (0,)), ((), ()))


def dot(a, b, dims=NN):
    return lax.dot_general(a, b, dims, preferred_element_type=jnp.float32)


def fetch(sources, targets, sems):
    copies = [
        pltpu.make_async_copy(source, target, sems.at[n])
        for n, (source, target) in enumerate(zip(sources, targets, strict=True))
    ]
    for copy in copies:
        copy.start()
    for copy in copies:
        copy.wait()


def weights_kernel(first, second, small, w1, w2, b1, b2, table):
    source = lax.broadcasted_iota(jnp.int32, (CIN, 128), 0)
    slot = lax.broadcasted_iota(jnp.int32, (CIN, 128), 1)
    for k in range(1, INSTR):
        slot = jnp.where(slot == SLOT * k - 1, -1, slot)
    shifted = source
    for k in range(1, INSTR):
        shifted = shifted + jnp.where(source >= k * (VALUES + 1), 1, 0)
    spread = jnp.where(shifted == slot, 1.0, 0.0).astype(jnp.bfloat16)
    for a in range(3):
        for b in range(3):
            rows = slice(b * CHANNELS, (b + 1) * CHANNELS)
            w1[rows, a * 128 : (a + 1) * 128] = dot(first[a, b], spread).astype(jnp.bfloat16)
            w2[rows, a * CHANNELS : (a + 1) * CHANNELS] = second[a, b]
    up = lax.broadcasted_iota(jnp.int32, (CHANNELS, CHANNELS), 0)
    across = lax.broadcasted_iota(jnp.int32, (CHANNELS, CHANNELS), 1)
    for n, column in enumerate((b1, b2)):
        row = small[n : n + 1, 0:CHANNELS]
        column[...] = jnp.sum(jnp.where(up == across, row, 0.0), axis=1, keepdims=True)
    for k in range(INSTR):
        length = small[2:3, k : k + 1]
        reach = jnp.floor(4.0 * length)
        table[k : k + 1] = jnp.broadcast_to(-LOG2E * (0.5 / (length * length)), (1, 128))
        table[INSTR + k : INSTR + k + 1] = jnp.broadcast_to(reach * reach, (1, 128))


def build(ref, part, shift, table, targets, wt, lc):
    lat_first = lax.axis_index("lat") * CLAT
    grid_row = lax.broadcasted_iota(jnp.int32, (24, 128), 0) + (lat_first - 2)
    row_ok = (grid_row >= 0) & (grid_row < NLAT)
    grid_row = grid_row.astype(jnp.float32)
    lane = lax.broadcasted_iota(jnp.int32, (128, 128), 0)
    edge = lax.broadcasted_iota(jnp.int32, (16, 128), 0)
    edge_inst = (edge // 4).astype(jnp.float32)
    edge = edge % 4
    edge_col = (edge - 2 + jnp.where(edge >= 2, CLON, 0)).astype(jnp.float32)
    which = lax.broadcasted_iota(jnp.int32, (SLOT, 128), 0)
    for block in range(4):
        at = part * BAND + block * 128
        data = ref[block]
        lat = data[0:1]
        lon = data[31:32]
        inst = data[32:33]
        rate = table[0:1]
        reach2 = table[INSTR : INSTR + 1]
        for k in range(1, INSTR):
            rate = jnp.where(inst == float(k), table[k : k + 1], rate)
            reach2 = jnp.where(inst == float(k), table[INSTR + k : INSTR + k + 1], reach2)
        rel = (lon.astype(jnp.int32) & (CLON - 1)).astype(jnp.float32) + shift

        def kernel_of(gap):
            gap2 = gap * gap
            return jnp.where(gap2 <= reach2, jnp.exp2(gap2 * rate), 0.0)

        lat_k = jnp.where(row_ok, kernel_of(grid_row - lat), 0.0)
        aug = jnp.where(which == 0, 1.0, jnp.where(which == 31, 0.0, data[0:SLOT]))
        for i in range(EXT):
            wt[i * SLOT : (i + 1) * SLOT, at : at + 128] = (lat_k[i : i + 1] * aug).astype(
                jnp.bfloat16
            )
        chosen = [jnp.where(inst == float(k), 1.0, 0.0).astype(jnp.bfloat16) for k in range(INSTR)]
        for target, start, base in targets:
            ker = kernel_of((lane + start).astype(jnp.float32) - rel).astype(jnp.bfloat16)
            for k in range(INSTR):
                target[k * 128 : (k + 1) * 128, base + block * 128 : base + (block + 1) * 128] = (
                    ker * chosen[k]
                )
        lc[0:16, at : at + 128] = jnp.where(
            inst == edge_inst, kernel_of(edge_col - rel), 0.0
        ).astype(jnp.bfloat16)
        lc[16:128, at : at + 128] = jnp.zeros((112, 128), jnp.bfloat16)


def own_kernel(own_ref, table, sa, sb, sc, wt, la, lb, lc):
    build(own_ref, 0, 0.0, table, ((la, 0, 0), (lb, 128, 0)), wt, lc)
    for pair in range(2):
        rows = slice(pair * 256, (pair + 1) * 256)
        sa[:, rows] = dot(wt[...], la[rows, :], NT)
        sb[:, rows] = dot(wt[...], lb[rows, :], NT)
    sc[...] = dot(wt[...], lc[...], NT)


def encode_kernel(
    minus_ref, plus_ref, table, own_a, own_b, own_c, w1_ref, b1_ref, w2_ref, b2_ref,
    out_ref, wt, la, lb, lc, sa, sb, sc, feat, hid, stage,
):
    lat_first = lax.axis_index("lat") * CLAT
    build(minus_ref, 0, -float(CLON), table, ((la, 0, 0),), wt, lc)
    build(plus_ref, 1, float(CLON), table, ((lb, 128, 0),), wt, lc)

    for pair in range(2):
        rows = slice(pair * 256, (pair + 1) * 256)
        sa[:, rows] = dot(wt[:, 0:BAND], la[rows, :], NT)
        sb[:, rows] = dot(wt[:, BAND : 2 * BAND], lb[rows, :], NT)
    sc[...] = dot(wt[...], lc[...], NT)

    slot_row = lax.broadcasted_iota(jnp.int32, (SLOT, WIDE), 0)
    for i in range(EXT):
        rows = slice(i * SLOT, (i + 1) * SLOT)
        edges = sc[rows, :] + own_c[rows, :]
        for k in range(INSTR):
            lanes = slice(k * 128, (k + 1) * 128)
            sums = jnp.concatenate(
                [
                    sa[rows, lanes] + own_a[rows, lanes],
                    sb[rows, lanes] + own_b[rows, lanes],
                    pltpu.roll(edges, 126 - 4 * k, 1),
                ],
                axis=1,
            )
            density = sums[0:1]
            inverse = 1.0 / (1.0 + density)
            value = jnp.where(slot_row == 0, jnp.log1p(density), sums * inverse)
            feat[i * 128 + k * SLOT : i * 128 + (k + 1) * SLOT, :] = value.astype(jnp.bfloat16)

    w1 = w1_ref[...]
    b1 = b1_ref[...]
    for pair in range(HID // 2):
        h = 2 * pair
        x = jnp.concatenate(
            [feat[h * 128 : (h + 3) * 128, :], feat[(h + 1) * 128 : (h + 4) * 128, :]], axis=1
        )
        y = dot(w1, x)
        for n in range(2):
            lanes = slice(n * WIDE, (n + 1) * WIDE)
            pre = (
                y[64:128, lanes]
                + pltpu.roll(y[0:64, lanes], 1, 1)
                + pltpu.roll(y[128:192, lanes], WIDE - 1, 1)
                + b1
            )
            act = pre / (1.0 + jnp.exp(-pre))
            row = lat_first - 1 + h + n
            if h + n in (0, HID - 1):
                act = jnp.where((row >= 0) & (row < NLAT), act, 0.0)
            hid[(h + n) * 64 : (h + n + 1) * 64, :] = act.astype(jnp.bfloat16)

    w2 = w2_ref[...]
    b2 = b2_ref[...]
    for pair in range(CLAT // 2):
        r = 2 * pair
        x = jnp.concatenate(
            [hid[r * 64 : (r + 3) * 64, :], hid[(r + 1) * 64 : (r + 4) * 64, :]], axis=1
        )
        y = dot(w2, x)
        for n in range(2):
            lanes = slice(n * WIDE, (n + 1) * WIDE)
            total = (
                y[64:128, lanes]
                + pltpu.roll(y[0:64, lanes], 1, 1)
                + pltpu.roll(y[128:192, lanes], WIDE - 1, 1)
            )[:, 0:CLON] + b2
            stage[pl.ds(r + n, CHANNELS, CLAT), :] = total[:, 0:128]
            stage[pl.ds(CHANNELS * CLAT + r + n, CHANNELS, CLAT), :] = total[:, 128:256]
    half = CHANNELS * CLAT
    for n in range(2):
        out_ref[:, :, n * 128 : (n + 1) * 128] = (
            stage[n * half : (n + 1) * half, :].reshape(CHANNELS, CLAT, 128).astype(jnp.bfloat16)
        )


def encode(minus, own, plus, w1, w2, b1, b2, table):
    vmem = pl.BlockSpec(memory_space=pltpu.VMEM)
    bf16, f32 = jnp.bfloat16, jnp.float32
    rows = EXT * SLOT
    partial = pl.pallas_call(
        own_kernel,
        out_shape=[
            jax.ShapeDtypeStruct((rows, INSTR * 128), f32),
            jax.ShapeDtypeStruct((rows, INSTR * 128), f32),
            jax.ShapeDtypeStruct((rows, 128), f32),
        ],
        in_specs=[vmem] * 2,
        out_specs=[vmem] * 3,
        scratch_shapes=[
            pltpu.VMEM((rows, BAND), bf16),
            pltpu.VMEM((INSTR * 128, BAND), bf16),
            pltpu.VMEM((INSTR * 128, BAND), bf16),
            pltpu.VMEM((128, BAND), bf16),
        ],
        compiler_params=pltpu.CompilerParams(vmem_limit_bytes=16 * 1024 * 1024),
        cost_estimate=pl.CostEstimate(flops=2 * rows * BAND * 1152, bytes_accessed=3000000, transcendentals=0),
    )(own, table)
    return pl.pallas_call(
        encode_kernel,
        out_shape=jax.ShapeDtypeStruct((CHANNELS, CLAT, CLON), bf16),
        in_specs=[vmem] * 10,
        out_specs=vmem,
        scratch_shapes=[
            pltpu.VMEM((rows, 2 * BAND), bf16),
            pltpu.VMEM((INSTR * 128, BAND), bf16),
            pltpu.VMEM((INSTR * 128, BAND), bf16),
            pltpu.VMEM((128, 2 * BAND), bf16),
            pltpu.VMEM((rows, INSTR * 128), f32),
            pltpu.VMEM((rows, INSTR * 128), f32),
            pltpu.VMEM((rows, 128), f32),
            pltpu.VMEM((EXT * 128, WIDE), bf16),
            pltpu.VMEM((HID * CHANNELS, WIDE), bf16),
            pltpu.VMEM((2 * CHANNELS * CLAT, 128), f32),
        ],
        compiler_params=pltpu.CompilerParams(vmem_limit_bytes=24 * 1024 * 1024),
    )(minus, plus, table, *partial, w1, b1, w2, b2)


def along(array, shape):
    return lax.broadcast_in_dim(array, shape, (len(shape) - 1,))


def pack(obs_values, obs_lat, obs_lon, instrument):
    shape = (40, ROWS_DEV)
    row = lax.broadcasted_iota(jnp.int32, shape, 0)
    ints = jnp.where(row == 32, along(instrument, shape), 0)
    ints = jnp.where(row == 31, along(obs_lon, shape), ints)
    ints = jnp.where(row == 0, along(obs_lat, shape), ints)
    return jnp.pad(obs_values, ((1, 9), (0, 0))) + ints.astype(jnp.float32)


def pack_small(b_first, b_second, length_scale):
    shape = (8, CHANNELS)
    row = lax.broadcasted_iota(jnp.int32, shape, 0)
    scale = along(jnp.pad(length_scale, (0, CHANNELS - INSTR)), shape)
    small = jnp.where(row == 2, scale, 0.0)
    small = jnp.where(row == 1, along(b_second, shape), small)
    return jnp.where(row == 0, along(b_first, shape), small)


def arrange(w_first, w_second, small):
    bf16, f32 = jnp.bfloat16, jnp.float32
    return pl.pallas_call(
        weights_kernel,
        out_shape=[
            jax.ShapeDtypeStruct((3 * CHANNELS, 3 * 128), bf16),
            jax.ShapeDtypeStruct((3 * CHANNELS, 3 * CHANNELS), bf16),
            jax.ShapeDtypeStruct((CHANNELS, 1), f32),
            jax.ShapeDtypeStruct((CHANNELS, 1), f32),
            jax.ShapeDtypeStruct((2 * INSTR, 128), f32),
        ],
        in_specs=[pl.BlockSpec(memory_space=pltpu.VMEM)] * 3,
        out_specs=[pl.BlockSpec(memory_space=pltpu.VMEM)] * 5,
        compiler_params=pltpu.CompilerParams(vmem_limit_bytes=4 * 1024 * 1024),
        cost_estimate=pl.CostEstimate(flops=20000000, bytes_accessed=1000000, transcendentals=0),
    )(w_first, w_second, small)


def send(array, axis, target):
    peers = lax.axis_size(axis)
    return lax.ppermute(array, axis, [(i, target(i) % peers) for i in range(peers)])


def body(
    obs_values, obs_lat, obs_lon, instrument, length_scale, w_first, b_first, w_second, b_second
):
    rows = pack(obs_values, obs_lat, obs_lon, instrument)
    rows = jnp.concatenate([rows, send(rows, "lat", lambda i: i ^ 1)], axis=1)
    rows, b_first, b_second, length_scale = lax.optimization_barrier(
        (rows, b_first, b_second, length_scale)
    )
    small = pack_small(b_first, b_second, length_scale)
    others = send(rows, "lat", lambda i: i ^ 2)
    rows, others, small, w_first, w_second = lax.optimization_barrier(
        (rows, others, small, w_first, w_second)
    )
    rows = jnp.concatenate([rows, others], axis=1)
    weights = arrange(w_first, w_second, small)
    others = [send(rows, "lat", lambda i, k=k: i + 4 * k) for k in (1, 2, 3)]
    rows, others, weights = lax.optimization_barrier((rows, others, weights))
    rows = jnp.stack([rows] + others)
    minus = send(rows, "lon", lambda i: i + 1)
    plus = send(rows, "lon", lambda i: i - 1)
    return encode(minus, rows, plus, *weights)


def solution(mesh):
    return jax.shard_map(
        body,
        mesh=mesh,
        in_specs=(
            P(None, ("lat", "lon")),
            P(("lat", "lon")),
            P(("lat", "lon")),
            P(("lat", "lon")),
            P(),
            P(),
            P(),
            P(),
            P(),
        ),
        out_specs=P(None, "lat", "lon"),
        check_vma=False,
    )
```

time: 34 us -> 34.9 us (1.026)
  waiting for transfers between devices: 5.41 us -> 10.3 us
  local copies, waits for them, and re-layouts: 5.14 us -> 2.48 us
  starting transfers between devices: 14.6 us -> 13.3 us
  other arithmetic: 0.93 us -> 1.75 us
  Pallas kernels: 7.63 us -> 6.86 us
    ppermute x7, waiting for transfers between devices: 5.41 us -> 10.3 us  [send(): lax.ppermute(array, axis, [(i, target(i) % peers) for i in range(peers)])]
    pallas_call x1, Pallas kernels: 7.63 us -> 5.4 us  [encode(): pl.pallas_call(encode_kernel, out_shape=jax.ShapeDtypeStruct((CHANNELS, C...]
    pallas_call x0 -> x2, Pallas kernels: none -> 1.46 us  [the longest x1 1.24 us: encode(): pl.pallas_call(own_kernel, out_shape=[jax.ShapeDtypeStruct((rows, INSTR *...]
    ppermute x7, starting transfers between devices: 14.6 us -> 13.3 us  [send(): lax.ppermute(array, axis, [(i, target(i) % peers) for i in range(peers)])]
    unnamed x13 -> x4, local copies, waits for them, and re-layouts: 3.01 us -> 1.82 us
    reshape x4 -> x0, local copies, waits for them, and re-layouts: 0.9 us -> none  [the longest x2 0.63 us: body(): jnp.transpose(w1, (1, 2, 0, 3, 4)).reshape(3 * CHANNELS, 3 * INSTR * SLOT)]
    concatenate x1 -> x0, local copies, waits for them, and re-layouts: 0.84 us -> none  [body(): jnp.concatenate([obs_lat.astype(f32)[None], obs_values, obs_lon.astype(f3...]
    add x0 -> x1, other arithmetic: none -> 0.82 us  [pack(): return jnp.pad(obs_values, ((1, 9), (0, 0))) + ints.astype(jnp.float32)]
  transfers between devices with their start and end apart: 7 -> 7, of which waited for: 3 -> 6; matrix products, arithmetic and copies ran while one was open for 7% -> 4% of each run, Pallas kernels for 0% -> 4%
where the time goes in v2:
time: 34.9 us; the launch traced here: 34.8 us
  starting transfers between devices  13.3 us (38%)
  waiting for transfers between devices  10.3 us (30%)
  Pallas kernels  6.86 us (20%)
  local copies, waits for them, and re-layouts  2.48 us (7%)
  other arithmetic  1.75 us (5%)
    ppermute x7, starting transfers between devices, send(): lax.ppermute(array, axis, [(i, target(i) % peers) for i in range(peers)])  13.3 us
    ppermute x7, waiting for transfers between devices, send(): lax.ppermute(array, axis, [(i, target(i) % peers) for i in range(peers)])  10.3 us
    pallas_call x1, Pallas kernels, encode(): pl.pallas_call(encode_kernel, out_shape=jax.ShapeDtypeStruct((CHANNELS, C...  5.4 us
    unnamed x4, local copies, waits for them, and re-layouts  1.82 us
    pallas_call x1, Pallas kernels, encode(): pl.pallas_call(own_kernel, out_shape=[jax.ShapeDtypeStruct((rows, INSTR *...  1.24 us
    add x1, other arithmetic, pack(): return jnp.pad(obs_values, ((1, 9), (0, 0))) + ints.astype(jnp.float32)  0.82 us
    select_n x1, other arithmetic, pack_small(): return jnp.where(row == 0, along(b_first, shape), small)  0.74 us
  transfers between devices with their start and end apart: 7, of which 6 were waited for; matrix products, arithmetic and copies ran while one was open for 4% of the time, Pallas kernels for 4%

profile of v2, /device:TPU:16, one launch (start us, length us, event | category | flops | bytes accessed | tf_op | source)
XLA Modules:
  0.0 34.8 jit_solution(12903711275009894371)
XLA Ops:
  0.0 0.8 %convert_add_fusion = f32[40,32]{1,0:T(8,128)S(1)} fusion(f32[30,32]{1,0:T(8,128)} %param.9, s32[32]{0:T(128)} %param.12, s32[32]{0:T(128)} %param.11, s32[32]{0:T(128)} %param.10, pred[40]{0:T(512)(128)(4,1)S(1)} %get-tuple-element.57, pred[40]{0:T(512)(128)(4,1)S(1)} %get-tuple-element.58, pred[40]{0:T(512)(128)(4,1)S(1)} %iota_compare_fusion.5), kind=kLoop, calls=%fused_computation.3 | loop fusion | flops 6400 | bytes 9464 | tf_op jit(solution)/shard_map/add | solution.py:256
  0.8 0.1 collective-permute-start
  1.0 1.2 %collective-permute-done = f32[40,32]{1,0:T(8,128)S(1)} collective-permute-done((f32[40,32]{1,0:T(8,128)S(1)}, f32[40,32]{1,0:T(8,128)S(1)}, u32[]{:S(2)}, u32[]{:S(2)}) %collective-permute-start) | collective-permute-done | bytes 5152 | tf_op jit(solution)/shard_map/ppermute | solution.py:288
  2.1 0.1 pad_maximum_fusion.1
  2.2 2.1 %collective-permute-start.1 = (f32[40,64]{1,0:T(8,128)S(1)}, f32[40,64]{1,0:T(8,128)S(1)}, u32[]{:S(2)}, u32[]{:S(2)}) collective-permute-start(f32[40,64]{1,0:T(8,128)S(1)} %pad_maximum_fusion.1), channel_id=1, source_target_pairs={{0,32},{16,48},{32,0},{48,16},{64,96},{80,112},{96,64},{112,80},{1... | collective-permute-start | bytes 30728 | tf_op jit(solution)/shard_map/ppermute | solution.py:288
  4.3 0.7 %pad.9 = f32[64]{0:T(128)S(1)} pad(f32[4]{0:T(128)} %param.13, f32[]{:T(128)} %constant.6.clone.1), padding=0_60 | pad | bytes 276 | tf_op jit(solution)/shard_map/jit(_pad)/pad | solution.py:262
  5.0 0.7 %select_select_fusion.small = f32[8,64]{1,0:T(8,128)S(1)} fusion(f32[64]{0:T(128)S(1)} %pad.9, f32[64]{0:T(128)} %param.17, f32[64]{0:T(128)} %param.15, pred[8]{0:T(512)(128)(4,1)S(1)} %get-tuple-element.59, pred[8]{0:T(512)(128)(4,1)S(1)} %get-tuple-element.60, pred[8]{0:T(512)(128)(4,1)S(1)} %iota_compare_fusion.2), kind=kLoop, calls=%fused_computation.4 | loop fusion | flops 1536 | bytes 2840 | tf_op jit(solution)/shard_map/jit(_where)/select_n | solution.py:265
  5.7 1.8 %collective-permute-done.1 = f32[40,64]{1,0:T(8,128)S(1)} collective-permute-done((f32[40,64]{1,0:T(8,128)S(1)}, f32[40,64]{1,0:T(8,128)S(1)}, u32[]{:S(2)}, u32[]{:S(2)}) %collective-permute-start.1) | collective-permute-done | bytes 10272 | tf_op jit(solution)/shard_map/ppermute | solution.py:288
  7.5 0.1 pad_maximum_fusion.2
  7.6 2.8 %collective-permute-start.4 = (f32[40,128]{1,0:T(8,128)S(1)}, f32[40,128]{1,0:T(8,128)S(1)}, u32[]{:S(2)}, u32[]{:S(2)}) collective-permute-start(f32[40,128]{1,0:T(8,128)S(1)} %pad_maximum_fusion.2), channel_id=1, source_target_pairs={{0,192},{16,208},{32,224},{48,240},{64,0},{80,16},{96,32},{112,48}... | collective-permute-start | bytes 61448 | tf_op jit(solution)/shard_map/ppermute | solution.py:288
  10.4 0.8 %collective-permute-start.3 = (f32[40,128]{1,0:T(8,128)S(1)}, f32[40,128]{1,0:T(8,128)S(1)}, u32[]{:S(2)}, u32[]{:S(2)}) collective-permute-start(f32[40,128]{1,0:T(8,128)S(1)} %pad_maximum_fusion.2), channel_id=1, source_target_pairs={{0,128},{16,144},{32,160},{48,176},{64,192},{80,208},{96,224},{112... | collective-permute-start | bytes 61448 | tf_op jit(solution)/shard_map/ppermute | solution.py:288
  11.2 0.9 %collective-permute-start.2 = (f32[40,128]{1,0:T(8,128)S(1)}, f32[40,128]{1,0:T(8,128)S(1)}, u32[]{:S(2)}, u32[]{:S(2)}) collective-permute-start(f32[40,128]{1,0:T(8,128)S(1)} %pad_maximum_fusion.2), channel_id=1, source_target_pairs={{0,64},{16,80},{32,96},{48,112},{64,128},{80,144},{96,160},{112,17... | collective-permute-start | bytes 61448 | tf_op jit(solution)/shard_map/ppermute | solution.py:288
  12.1 0.0 copy-start
  12.1 0.9 %copy-done = bf16[3,3,64,124]{3,2,1,0:T(8,128)(2,1)S(1)} copy-done((bf16[3,3,64,124]{3,2,1,0:T(8,128)(2,1)S(1)}, bf16[3,3,64,124]{3,2,1,0:T(8,128)(2,1)}, u32[]{:S(2)}) %copy-start) | copy-done | bytes 142872
  13.0 0.0 copy-start.1
  13.0 0.9 %copy-done.1 = bf16[3,3,64,64]{3,2,1,0:T(8,128)(2,1)S(1)} copy-done((bf16[3,3,64,64]{3,2,1,0:T(8,128)(2,1)S(1)}, bf16[3,3,64,64]{3,2,1,0:T(8,128)(2,1)}, u32[]{:S(2)}) %copy-start.1) | copy-done | bytes 73752
  13.9 0.2 shard_map.91
  14.1 0.0 collective-permute-done.4
  14.1 1.6 %collective-permute-done.3 = f32[40,128]{1,0:T(8,128)S(1)} collective-permute-done((f32[40,128]{1,0:T(8,128)S(1)}, f32[40,128]{1,0:T(8,128)S(1)}, u32[]{:S(2)}, u32[]{:S(2)}) %collective-permute-start.3) | collective-permute-done | bytes 20512 | tf_op jit(solution)/shard_map/ppermute | solution.py:288
  15.7 0.5 %collective-permute-done.2 = f32[40,128]{1,0:T(8,128)S(1)} collective-permute-done((f32[40,128]{1,0:T(8,128)S(1)}, f32[40,128]{1,0:T(8,128)S(1)}, u32[]{:S(2)}, u32[]{:S(2)}) %collective-permute-start.2) | collective-permute-done | bytes 20512 | tf_op jit(solution)/shard_map/ppermute | solution.py:288
  16.2 6.6 %collective-permute-start.6 = (f32[4,40,128]{2,1,0:T(8,128)S(1)}, f32[4,40,128]{2,1,0:T(8,128)S(1)}, u32[]{:S(2)}, u32[]{:S(2)}) collective-permute-start(f32[4,40,128]{2,1,0:T(8,128)S(1)} %pad_maximum_fusion.own_ref), channel_id=1, source_target_pairs={{0,15},{1,0},{2,1},{3,2},{4,3},{5,4},{6,5},{7,6},{8,7},{9,8},{10,9... | collective-permute-start | bytes 245768 | tf_op jit(solution)/shard_map/ppermute | solution.py:288
  22.8 0.0 collective-permute-start.5
  22.8 1.2 %shard_map.92 = (f32[640,512]{1,0:T(8,128)S(1)}, f32[640,512]{1,0:T(8,128)S(1)}, f32[640,128]{1,0:T(8,128)S(1)}) custom-call(f32[4,40,128]{2,1,0:T(8,128)S(1)} %pad_maximum_fusion.own_ref, f32[8,128]{1,0:T(8,128)S(1)} %get-tuple-element.49.table), custom_call_target="tpu_custom_call" | custom-call | flops 754974720 | bytes 3000000 | tf_op jit(solution)/shard_map/pallas_call | solution.py:207
  24.1 0.8 %collective-permute-done.6.plus_ref = f32[4,40,128]{2,1,0:T(8,128)S(1)} collective-permute-done((f32[4,40,128]{2,1,0:T(8,128)S(1)}, f32[4,40,128]{2,1,0:T(8,128)S(1)}, u32[]{:S(2)}, u32[]{:S(2)}) %collective-permute-start.6) | collective-permute-done | bytes 81952 | tf_op jit(solution)/shard_map/ppermute | solution.py:288
  24.9 4.5 %collective-permute-done.5.minus_ref = f32[4,40,128]{2,1,0:T(8,128)S(1)} collective-permute-done((f32[4,40,128]{2,1,0:T(8,128)S(1)}, f32[4,40,128]{2,1,0:T(8,128)S(1)}, u32[]{:S(2)}, u32[]{:S(2)}) %collective-permute-start.5) | collective-permute-done | bytes 81952 | tf_op jit(solution)/shard_map/ppermute | solution.py:288
  29.4 5.4 %shard_map.93 = bf16[64,16,256]{2,1,0:T(8,128)(2,1)} custom-call(f32[4,40,128]{2,1,0:T(8,128)S(1)} %collective-permute-done.5.minus_ref, f32[4,40,128]{2,1,0:T(8,128)S(1)} %collective-permute-done.6.plus_ref, f32[8,128]{1,0:T(8,128)S(1)} %get-tuple-element.49.table, f32[640,512]{1,0:T(8,128)S(1)} %get-tuple-element.50.own_a, ...), custom_call_target="tpu_custom_call" | custom-call | tf_op jit(solution)/shard_map/pallas_call | solution.py:225
  (5 shorter events, 0.0 us)
Async XLA Ops:
  0.8 1.3 %collective-permute-start = (f32[40,32]{1,0:T(8,128)S(1)}, f32[40,32]{1,0:T(8,128)S(1)}, u32[]{:S(2)}, u32[]{:S(2)}) collective-permute-start(f32[40,32]{1,0:T(8,128)S(1)} %convert_add_fusion), channel_id=1, source_target_pairs={{0,16},{16,0},{32,48},{48,32},{64,80},{80,64},{96,112},{112,96},{1... | collective-permute-start | bytes 15368 | tf_op jit(solution)/shard_map/ppermute | solution.py:288
  2.2 5.3 %collective-permute-start.1 = (f32[40,64]{1,0:T(8,128)S(1)}, f32[40,64]{1,0:T(8,128)S(1)}, u32[]{:S(2)}, u32[]{:S(2)}) collective-permute-start(f32[40,64]{1,0:T(8,128)S(1)} %pad_maximum_fusion.1), channel_id=1, source_target_pairs={{0,32},{16,48},{32,0},{48,16},{64,96},{80,112},{96,64},{112,80},{1... | collective-permute-start | bytes 30728 | tf_op jit(solution)/shard_map/ppermute | solution.py:288
  7.6 6.5 %collective-permute-start.4 = (f32[40,128]{1,0:T(8,128)S(1)}, f32[40,128]{1,0:T(8,128)S(1)}, u32[]{:S(2)}, u32[]{:S(2)}) collective-permute-start(f32[40,128]{1,0:T(8,128)S(1)} %pad_maximum_fusion.2), channel_id=1, source_target_pairs={{0,192},{16,208},{32,224},{48,240},{64,0},{80,16},{96,32},{112,48}... | collective-permute-start | bytes 61448 | tf_op jit(solution)/shard_map/ppermute | solution.py:288
  10.4 5.3 %collective-permute-start.3 = (f32[40,128]{1,0:T(8,128)S(1)}, f32[40,128]{1,0:T(8,128)S(1)}, u32[]{:S(2)}, u32[]{:S(2)}) collective-permute-start(f32[40,128]{1,0:T(8,128)S(1)} %pad_maximum_fusion.2), channel_id=1, source_target_pairs={{0,128},{16,144},{32,160},{48,176},{64,192},{80,208},{96,224},{112... | collective-permute-start | bytes 61448 | tf_op jit(solution)/shard_map/ppermute | solution.py:288
  11.2 5.0 %collective-permute-start.2 = (f32[40,128]{1,0:T(8,128)S(1)}, f32[40,128]{1,0:T(8,128)S(1)}, u32[]{:S(2)}, u32[]{:S(2)}) collective-permute-start(f32[40,128]{1,0:T(8,128)S(1)} %pad_maximum_fusion.2), channel_id=1, source_target_pairs={{0,64},{16,80},{32,96},{48,112},{64,128},{80,144},{96,160},{112,17... | collective-permute-start | bytes 61448 | tf_op jit(solution)/shard_map/ppermute | solution.py:288
  12.1 0.9 %copy-start = (bf16[3,3,64,124]{3,2,1,0:T(8,128)(2,1)S(1)}, bf16[3,3,64,124]{3,2,1,0:T(8,128)(2,1)}, u32[]{:S(2)}) copy-start(bf16[3,3,64,124]{3,2,1,0:T(8,128)(2,1)} %first) | copy-start | bytes 428548
  13.0 0.9 %copy-start.1 = (bf16[3,3,64,64]{3,2,1,0:T(8,128)(2,1)S(1)}, bf16[3,3,64,64]{3,2,1,0:T(8,128)(2,1)}, u32[]{:S(2)}) copy-start(bf16[3,3,64,64]{3,2,1,0:T(8,128)(2,1)} %second) | copy-start | bytes 221188
  16.2 8.7 %collective-permute-start.6 = (f32[4,40,128]{2,1,0:T(8,128)S(1)}, f32[4,40,128]{2,1,0:T(8,128)S(1)}, u32[]{:S(2)}, u32[]{:S(2)}) collective-permute-start(f32[4,40,128]{2,1,0:T(8,128)S(1)} %pad_maximum_fusion.own_ref), channel_id=1, source_target_pairs={{0,15},{1,0},{2,1},{3,2},{4,3},{5,4},{6,5},{7,6},{8,7},{9,8},{10,9... | collective-permute-start | bytes 245768 | tf_op jit(solution)/shard_map/ppermute | solution.py:288
  22.8 6.6 %collective-permute-start.5 = (f32[4,40,128]{2,1,0:T(8,128)S(1)}, f32[4,40,128]{2,1,0:T(8,128)S(1)}, u32[]{:S(2)}, u32[]{:S(2)}) collective-permute-start(f32[4,40,128]{2,1,0:T(8,128)S(1)} %pad_maximum_fusion.own_ref), channel_id=1, source_target_pairs={{0,1},{1,2},{2,3},{3,4},{4,5},{5,6},{6,7},{7,8},{8,9},{9,10},{10,1... | collective-permute-start | bytes 245768 | tf_op jit(solution)/shard_map/ppermute | solution.py:288

commit v3 on v2

v3 whole, which is shorter than its diff:
```python
import jax
import jax.numpy as jnp
from jax import lax
from jax.experimental import pallas as pl
from jax.experimental.pallas import tpu as pltpu
from jax.sharding import PartitionSpec as P

CLAT = 16
CLON = 256
INSTR = 4
VALUES = 30
CHANNELS = 64
CIN = 124
SLOT = 32
NLAT = 256
NLON = 4096
ROWS_DEV = 32
PARTS = 4
EXT = CLAT + 4
HID = CLAT + 2
EDGE = 6
BAND = 512
LOG2E = 1.4426950408889634
NT = (((1,), (1,)), ((), ()))
NN = (((1,), (0,)), ((), ()))


def dot(a, b, dims=NN):
    return lax.dot_general(a, b, dims, preferred_element_type=jnp.float32)


def fetch(sources, targets, sems):
    copies = [
        pltpu.make_async_copy(source, target, sems.at[n])
        for n, (source, target) in enumerate(zip(sources, targets, strict=True))
    ]
    for copy in copies:
        copy.start()
    for copy in copies:
        copy.wait()


def weights_kernel(first, second, small, w1, w2, w2_taps, b1, b2, table):
    source = lax.broadcasted_iota(jnp.int32, (CIN, 128), 0)
    slot = lax.broadcasted_iota(jnp.int32, (CIN, 128), 1)
    for k in range(1, INSTR):
        slot = jnp.where(slot == SLOT * k - 1, -1, slot)
    shifted = source
    for k in range(1, INSTR):
        shifted = shifted + jnp.where(source >= k * (VALUES + 1), 1, 0)
    spread = jnp.where(shifted == slot, 1.0, 0.0).astype(jnp.bfloat16)
    for a in range(3):
        for b in range(3):
            rows = slice(b * CHANNELS, (b + 1) * CHANNELS)
            w1[rows, a * 128 : (a + 1) * 128] = dot(first[a, b], spread).astype(jnp.bfloat16)
            w2[rows, a * CHANNELS : (a + 1) * CHANNELS] = second[a, b]
            w2_taps[a, rows, :] = second[a, b]
    up = lax.broadcasted_iota(jnp.int32, (CHANNELS, CHANNELS), 0)
    across = lax.broadcasted_iota(jnp.int32, (CHANNELS, CHANNELS), 1)
    for n, column in enumerate((b1, b2)):
        row = small[n : n + 1, 0:CHANNELS]
        column[...] = jnp.sum(jnp.where(up == across, row, 0.0), axis=1, keepdims=True)
    for k in range(INSTR):
        length = small[2:3, k : k + 1]
        reach = jnp.floor(4.0 * length)
        table[k : k + 1] = jnp.broadcast_to(-LOG2E * (0.5 / (length * length)), (1, 128))
        table[INSTR + k : INSTR + k + 1] = jnp.broadcast_to(reach * reach, (1, 128))


def lon_side():
    return 1 - lax.axis_index("lon") % 2


def build(ref, shift, halves, table, wt, ln, lc):
    lat_first = lax.axis_index("lat") * CLAT
    grid_row = lax.broadcasted_iota(jnp.int32, (24, 128), 0) + (lat_first - 2)
    row_ok = (grid_row >= 0) & (grid_row < NLAT)
    grid_row = grid_row.astype(jnp.float32)
    lane = lax.broadcasted_iota(jnp.int32, (128, 128), 0)
    edge = lax.broadcasted_iota(jnp.int32, (32, 128), 0)
    edge_inst = (edge // EDGE).astype(jnp.float32)
    edge = edge % EDGE
    edge_col = (edge - 2 + jnp.where(edge >= 3, CLON - 2, 0)).astype(jnp.float32)
    which = lax.broadcasted_iota(jnp.int32, (SLOT, 128), 0)
    for block in range(4):
        cols = slice(block * 128, (block + 1) * 128)
        data = ref[block]
        lat = data[0:1]
        lon = data[31:32]
        inst = data[32:33]
        rate = table[0:1]
        reach2 = table[INSTR : INSTR + 1]
        for k in range(1, INSTR):
            rate = jnp.where(inst == float(k), table[k : k + 1], rate)
            reach2 = jnp.where(inst == float(k), table[INSTR + k : INSTR + k + 1], reach2)
        rel = ((lon.astype(jnp.int32) & (CLON - 1)) + shift).astype(jnp.float32)

        def kernel_of(gap):
            gap2 = gap * gap
            return jnp.where(gap2 <= reach2, jnp.exp2(gap2 * rate), 0.0)

        lat_k = jnp.where(row_ok, kernel_of(grid_row - lat), 0.0)
        aug = jnp.where(which == 0, 1.0, jnp.where(which == 31, 0.0, data[0:SLOT]))
        for i in range(EXT):
            wt[i * SLOT : (i + 1) * SLOT, cols] = (lat_k[i : i + 1] * aug).astype(jnp.bfloat16)
        chosen = [jnp.where(inst == float(k), 1.0, 0.0).astype(jnp.bfloat16) for k in range(INSTR)]
        for n, half in enumerate(halves):
            ker = kernel_of((lane + half * 128).astype(jnp.float32) - rel).astype(jnp.bfloat16)
            for k in range(INSTR):
                ln[n, k * 128 : (k + 1) * 128, cols] = ker * chosen[k]
        lc[0:32, cols] = jnp.where(inst == edge_inst, kernel_of(edge_col - rel), 0.0).astype(
            jnp.bfloat16
        )
        lc[32:128, cols] = jnp.zeros((96, 128), jnp.bfloat16)


def features_of(sums):
    density = sums[0:1]
    row = lax.broadcasted_iota(jnp.int32, sums.shape, 0)
    inverse = 1.0 / (1.0 + density)
    return jnp.where(row == 0, jnp.log1p(density), sums * inverse).astype(jnp.bfloat16)


def own_kernel(own_ref, table, s_own, s_edge, wt, ln, lc):
    build(own_ref, 0, (0, 1), table, wt, ln, lc)
    for half in range(2):
        for pair in range(2):
            rows = slice(pair * 256, (pair + 1) * 256)
            s_own[half, :, rows] = dot(wt[...], ln[half, rows, :], NT)
    s_edge[...] = dot(wt[...], lc[...], NT)


def near_kernel(near_ref, table, s_own, s_edge, f_near, edge_out, wt, ln, lc, s_near):
    side = lon_side()
    build(near_ref, (2 * side - 1) * CLON, (side,), table, wt, ln, lc)
    for pair in range(2):
        rows = slice(pair * 256, (pair + 1) * 256)
        s_near[:, rows] = dot(wt[...], ln[0, rows, :], NT)
    edge_out[...] = s_edge[...] + dot(wt[...], lc[...], NT)
    for i in range(EXT):
        rows = slice(i * SLOT, (i + 1) * SLOT)
        for k in range(INSTR):
            lanes = slice(k * 128, (k + 1) * 128)
            f_near[i * 128 + k * SLOT : i * 128 + (k + 1) * SLOT, :] = features_of(
                s_near[rows, lanes] + s_own[side, rows, lanes]
            )


def edge_features(sums):
    lane = lax.broadcasted_iota(jnp.int32, (SLOT, 128), 1)
    parts = [jnp.zeros((SLOT, 128), jnp.float32)] * INSTR
    for i in range(EXT):
        moved = sums[i * SLOT : (i + 1) * SLOT]
        if i > 0:
            moved = pltpu.roll(moved, EDGE * i, 1)
        for k in range(INSTR):
            place = lax.rem(lane - EDGE * (i + k) + 256, 128)
            parts[k] = jnp.where(place < EDGE, moved, parts[k])
    for k in range(1, INSTR):
        parts[k] = pltpu.roll(parts[k], 128 - EDGE * k, 1)
    return jnp.concatenate([features_of(part) for part in parts], axis=0)


def edge_terms(products):
    left = products[0][0:CHANNELS]
    right = products[0][2 * CHANNELS : 3 * CHANNELS]
    for a in (1, 2):
        left += pltpu.roll(products[a][0:CHANNELS], 128 - EDGE * a, 1)
        right += pltpu.roll(products[a][2 * CHANNELS : 3 * CHANNELS], 128 - EDGE * a, 1)
    lane = lax.broadcasted_iota(jnp.int32, left.shape, 1)
    return jnp.where(lax.rem(lane, EDGE) == 1, left, pltpu.roll(right, 128 - 4, 1))


def row_total(y, terms, row, bias):
    left = pltpu.roll(y[0:CHANNELS], 1, 1)
    right = pltpu.roll(y[2 * CHANNELS : 3 * CHANNELS], CLON - 1, 1)
    here = pltpu.roll(terms, 128 - (EDGE * row + 1), 1)
    lane = lax.broadcasted_iota(jnp.int32, here.shape, 1)
    middle = y[CHANNELS : 2 * CHANNELS] + bias
    return (
        middle[:, 0:128] + jnp.where(lane == 0, here, left[:, 0:128]) + right[:, 0:128],
        middle[:, 128:256] + left[:, 128:256] + jnp.where(lane == 127, here, right[:, 128:256]),
    )


def silu(x):
    return x / (1.0 + jnp.exp(-x))


def encode_kernel(
    far_ref, table, s_own, s_edge, f_near, w1_ref, w2_ref, w2_taps, b1_ref, b2_ref,
    out_ref, wt, ln, lc, s_far, feat, hid, stage, result, sems,
):
    lat_first = lax.axis_index("lat") * CLAT
    near_side = lon_side()
    side = 1 - near_side
    build(far_ref, (2 * side - 1) * CLON, (side,), table, wt, ln, lc)
    edge_sums = s_edge[...] + dot(wt[...], lc[...], NT)
    for pair in range(2):
        rows = slice(pair * 256, (pair + 1) * 256)
        s_far[:, rows] = dot(wt[...], ln[0, rows, :], NT)
    for i in range(EXT):
        rows = slice(i * SLOT, (i + 1) * SLOT)
        for k in range(INSTR):
            lanes = slice(k * 128, (k + 1) * 128)
            slot = slice(i * 128 + k * SLOT, i * 128 + (k + 1) * SLOT)
            far = features_of(s_far[rows, lanes] + s_own[side, rows, lanes])
            near = f_near[slot, :]
            feat[slot, 0:128] = jnp.where(near_side == 0, near, far)
            feat[slot, 128:256] = jnp.where(near_side == 0, far, near)

    w1 = w1_ref[...]
    b1 = b1_ref[...]
    edge_feat = edge_features(edge_sums)
    products = [dot(w1[:, a * 128 : (a + 1) * 128], edge_feat) for a in range(3)]
    terms = edge_terms(products)
    pre = b1
    for a in range(3):
        for b in range(3):
            part = products[a][b * CHANNELS : (b + 1) * CHANNELS]
            shift = (EDGE * a + b - 1) % 128
            pre = pre + (part if shift == 0 else pltpu.roll(part, 128 - shift, 1))
    lane_row = lax.broadcasted_iota(jnp.int32, (CHANNELS, 128), 1) // EDGE + lat_first - 1
    inside = (lane_row >= 0) & (lane_row < NLAT)
    edge_hid = jnp.where(inside, silu(pre), 0.0).astype(jnp.bfloat16)
    for h in range(HID):
        y = dot(w1, feat[h * 128 : (h + 3) * 128, :])
        row = lat_first - 1 + h
        for n, half in enumerate(row_total(y, terms, h, b1)):
            act = silu(half)
            if h in (0, HID - 1):
                act = jnp.where((row >= 0) & (row < NLAT), act, 0.0)
            hid[h * CHANNELS : (h + 1) * CHANNELS, n * 128 : (n + 1) * 128] = act.astype(jnp.bfloat16)

    w2 = w2_ref[...]
    b2 = b2_ref[...]
    terms = edge_terms([dot(w2_taps[a], edge_hid) for a in range(3)])
    size = CHANNELS * CLAT
    for r in range(CLAT):
        y = dot(w2, hid[r * CHANNELS : (r + 3) * CHANNELS, :])
        for n, half in enumerate(row_total(y, terms, r, b2)):
            stage[pl.ds(n * size + r, CHANNELS, CLAT), :] = half

    copies = []
    step = CHANNELS // PARTS
    for part in range(PARTS):
        channels = slice(part * step, (part + 1) * step)
        for n in range(2):
            result[channels, :, n * 128 : (n + 1) * 128] = (
                stage[n * size + part * step * CLAT : n * size + (part + 1) * step * CLAT, :]
                .reshape(step, CLAT, 128)
                .astype(jnp.bfloat16)
            )
        copies.append(
            pltpu.make_async_copy(result.at[channels], out_ref.at[channels], sems.at[part])
        )
        copies[-1].start()
    for copy in copies:
        copy.wait()


def encode(near, own, far, w1, w2, w2_taps, b1, b2, table):
    vmem = pl.BlockSpec(memory_space=pltpu.VMEM)
    bf16, f32 = jnp.bfloat16, jnp.float32
    rows = EXT * SLOT
    s_own, s_edge = pl.pallas_call(
        own_kernel,
        out_shape=[
            jax.ShapeDtypeStruct((2, rows, INSTR * 128), f32),
            jax.ShapeDtypeStruct((rows, 128), f32),
        ],
        in_specs=[vmem] * 2,
        out_specs=[vmem] * 2,
        scratch_shapes=[
            pltpu.VMEM((rows, BAND), bf16),
            pltpu.VMEM((2, INSTR * 128, BAND), bf16),
            pltpu.VMEM((128, BAND), bf16),
        ],
        compiler_params=pltpu.CompilerParams(vmem_limit_bytes=16 * 1024 * 1024),
        cost_estimate=pl.CostEstimate(flops=2 * rows * BAND * 1152, bytes_accessed=3000000, transcendentals=0),
    )(own, table)
    f_near, s_edge = pl.pallas_call(
        near_kernel,
        out_shape=[
            jax.ShapeDtypeStruct((EXT * 128, 128), bf16),
            jax.ShapeDtypeStruct((rows, 128), f32),
        ],
        in_specs=[vmem] * 4,
        out_specs=[vmem] * 2,
        scratch_shapes=[
            pltpu.VMEM((rows, BAND), bf16),
            pltpu.VMEM((1, INSTR * 128, BAND), bf16),
            pltpu.VMEM((128, BAND), bf16),
            pltpu.VMEM((rows, INSTR * 128), f32),
        ],
        compiler_params=pltpu.CompilerParams(vmem_limit_bytes=16 * 1024 * 1024),
        cost_estimate=pl.CostEstimate(flops=2 * rows * BAND * 640, bytes_accessed=3000000, transcendentals=0),
    )(near, table, s_own, s_edge)
    return pl.pallas_call(
        encode_kernel,
        out_shape=jax.ShapeDtypeStruct((CHANNELS, CLAT, CLON), bf16),
        in_specs=[vmem] * 10,
        out_specs=pl.BlockSpec(memory_space=pl.ANY),
        scratch_shapes=[
            pltpu.VMEM((rows, BAND), bf16),
            pltpu.VMEM((1, INSTR * 128, BAND), bf16),
            pltpu.VMEM((128, BAND), bf16),
            pltpu.VMEM((rows, INSTR * 128), f32),
            pltpu.VMEM((EXT * 128, CLON), bf16),
            pltpu.VMEM((HID * CHANNELS, CLON), bf16),
            pltpu.VMEM((2 * CHANNELS * CLAT, 128), f32),
            pltpu.VMEM((CHANNELS, CLAT, CLON), bf16),
            pltpu.SemaphoreType.DMA((PARTS,)),
        ],
        compiler_params=pltpu.CompilerParams(vmem_limit_bytes=24 * 1024 * 1024),
    )(far, table, s_own, s_edge, f_near, w1, w2, w2_taps, b1, b2)


def along(array, shape):
    return lax.broadcast_in_dim(array, shape, (len(shape) - 1,))


def pack(obs_values, obs_lat, obs_lon, instrument):
    shape = (40, ROWS_DEV)
    row = lax.broadcasted_iota(jnp.int32, shape, 0)
    ints = jnp.where(row == 32, along(instrument, shape), 0)
    ints = jnp.where(row == 31, along(obs_lon, shape), ints)
    ints = jnp.where(row == 0, along(obs_lat, shape), ints)
    return jnp.pad(obs_values, ((1, 9), (0, 0))) + ints.astype(jnp.float32)


def pack_small(b_first, b_second, length_scale):
    shape = (8, CHANNELS)
    row = lax.broadcasted_iota(jnp.int32, shape, 0)
    scale = along(jnp.pad(length_scale, (0, CHANNELS - INSTR)), shape)
    small = jnp.where(row == 2, scale, 0.0)
    small = jnp.where(row == 1, along(b_second, shape), small)
    return jnp.where(row == 0, along(b_first, shape), small)


def arrange(w_first, w_second, small):
    bf16, f32 = jnp.bfloat16, jnp.float32
    return pl.pallas_call(
        weights_kernel,
        out_shape=[
            jax.ShapeDtypeStruct((3 * CHANNELS, 3 * 128), bf16),
            jax.ShapeDtypeStruct((3 * CHANNELS, 3 * CHANNELS), bf16),
            jax.ShapeDtypeStruct((3, 3 * CHANNELS, CHANNELS), bf16),
            jax.ShapeDtypeStruct((CHANNELS, 1), f32),
            jax.ShapeDtypeStruct((CHANNELS, 1), f32),
            jax.ShapeDtypeStruct((2 * INSTR, 128), f32),
        ],
        in_specs=[pl.BlockSpec(memory_space=pltpu.VMEM)] * 3,
        out_specs=[pl.BlockSpec(memory_space=pltpu.VMEM)] * 6,
        compiler_params=pltpu.CompilerParams(vmem_limit_bytes=4 * 1024 * 1024),
        cost_estimate=pl.CostEstimate(flops=20000000, bytes_accessed=1000000, transcendentals=0),
    )(w_first, w_second, small)


def send(array, axis, target):
    peers = lax.axis_size(axis)
    return lax.ppermute(array, axis, [(i, target(i) % peers) for i in range(peers)])


def body(
    obs_values, obs_lat, obs_lon, instrument, length_scale, w_first, b_first, w_second, b_second
):
    rows = pack(obs_values, obs_lat, obs_lon, instrument)
    rows = jnp.concatenate([rows, send(rows, "lat", lambda i: i ^ 1)], axis=1)
    rows, b_first, b_second, length_scale = lax.optimization_barrier(
        (rows, b_first, b_second, length_scale)
    )
    small = pack_small(b_first, b_second, length_scale)
    others = send(rows, "lat", lambda i: i ^ 2)
    rows, others, small, w_first, w_second = lax.optimization_barrier(
        (rows, others, small, w_first, w_second)
    )
    rows = jnp.concatenate([rows, others], axis=1)
    weights = arrange(w_first, w_second, small)
    others = [send(rows, "lat", lambda i, k=k: i + 4 * k) for k in (3, 2, 1)]
    rows, others, weights = lax.optimization_barrier((rows, others, weights))
    rows = jnp.stack([rows] + others)
    near = send(rows, "lon", lambda i: i ^ 1)
    far = send(rows, "lon", lambda i: ((i + 1) ^ 1) - 1)
    return encode(near, rows, far, *weights)


def solution(mesh):
    return jax.shard_map(
        body,
        mesh=mesh,
        in_specs=(
            P(None, ("lat", "lon")),
            P(("lat", "lon")),
            P(("lat", "lon")),
            P(("lat", "lon")),
            P(),
            P(),
            P(),
            P(),
            P(),
        ),
        out_specs=P(None, "lat", "lon"),
        check_vma=False,
    )
```

time: 34.9 us -> 30.1 us (0.86)
  the two profiles are of different devices: /device:TPU:16 before, /device:TPU:6 now
where the time goes in v3:
time: 30.1 us; the launch traced here: 29.9 us
  starting transfers between devices  14.5 us (48%)
  Pallas kernels  6.36 us (21%)
  waiting for transfers between devices  4.79 us (16%)
  local copies, waits for them, and re-layouts  2.48 us (8%)
  other arithmetic  1.75 us (6%)
    ppermute x7, starting transfers between devices, send(): lax.ppermute(array, axis, [(i, target(i) % peers) for i in range(peers)])  14.5 us
    ppermute x7, waiting for transfers between devices, send(): lax.ppermute(array, axis, [(i, target(i) % peers) for i in range(peers)])  4.79 us
    pallas_call x1, Pallas kernels, encode(): pl.pallas_call(encode_kernel, out_shape=jax.ShapeDtypeStruct((CHANNELS, C...  4.02 us
    unnamed x4, local copies, waits for them, and re-layouts  1.82 us
    pallas_call x1, Pallas kernels, encode(): pl.pallas_call(own_kernel, out_shape=[jax.ShapeDtypeStruct((2, rows, INST...  1.24 us
    pallas_call x1, Pallas kernels, encode(): pl.pallas_call(near_kernel, out_shape=[jax.ShapeDtypeStruct((EXT * 128, 1...  0.87 us
    add x1, other arithmetic, pack(): return jnp.pad(obs_values, ((1, 9), (0, 0))) + ints.astype(jnp.float32)  0.82 us
    select_n x1, other arithmetic, pack_small(): return jnp.where(row == 0, along(b_first, shape), small)  0.74 us
  transfers between devices with their start and end apart: 7, of which 5 were waited for; matrix products, arithmetic and copies ran while one was open for 5% of the time, Pallas kernels for 8%

profile of v3, /device:TPU:6, one launch (start us, length us, event | category | flops | bytes accessed | tf_op | source)
XLA Modules:
  0.0 29.9 jit_solution(6522030265855353614)
XLA Ops:
  0.0 0.8 %convert_add_fusion = f32[40,32]{1,0:T(8,128)S(1)} fusion(f32[30,32]{1,0:T(8,128)} %param.9, s32[32]{0:T(128)} %param.12, s32[32]{0:T(128)} %param.11, s32[32]{0:T(128)} %param.10, pred[40]{0:T(512)(128)(4,1)S(1)} %get-tuple-element.63, pred[40]{0:T(512)(128)(4,1)S(1)} %get-tuple-element.64, pred[40]{0:T(512)(128)(4,1)S(1)} %iota_compare_fusion.5), kind=kLoop, calls=%fused_computation.3 | loop fusion | flops 6400 | bytes 9464 | tf_op jit(solution)/shard_map/add | solution.py:329
  0.8 0.1 collective-permute-start
  1.0 1.2 %collective-permute-done = f32[40,32]{1,0:T(8,128)S(1)} collective-permute-done((f32[40,32]{1,0:T(8,128)S(1)}, f32[40,32]{1,0:T(8,128)S(1)}, u32[]{:S(2)}, u32[]{:S(2)}) %collective-permute-start) | collective-permute-done | bytes 5152 | tf_op jit(solution)/shard_map/ppermute | solution.py:362
  2.1 0.1 pad_maximum_fusion.1
  2.2 3.2 %collective-permute-start.1 = (f32[40,64]{1,0:T(8,128)S(1)}, f32[40,64]{1,0:T(8,128)S(1)}, u32[]{:S(2)}, u32[]{:S(2)}) collective-permute-start(f32[40,64]{1,0:T(8,128)S(1)} %pad_maximum_fusion.1), channel_id=1, source_target_pairs={{0,32},{16,48},{32,0},{48,16},{64,96},{80,112},{96,64},{112,80},{1... | collective-permute-start | bytes 30728 | tf_op jit(solution)/shard_map/ppermute | solution.py:362
  5.4 0.7 %pad.9 = f32[64]{0:T(128)S(1)} pad(f32[4]{0:T(128)} %param.13, f32[]{:T(128)} %constant.6.clone.1), padding=0_60 | pad | bytes 276 | tf_op jit(solution)/shard_map/jit(_pad)/pad | solution.py:335
  6.1 0.7 %select_select_fusion.small = f32[8,64]{1,0:T(8,128)S(1)} fusion(f32[64]{0:T(128)S(1)} %pad.9, f32[64]{0:T(128)} %param.17, f32[64]{0:T(128)} %param.15, pred[8]{0:T(512)(128)(4,1)S(1)} %get-tuple-element.65, pred[8]{0:T(512)(128)(4,1)S(1)} %get-tuple-element.66, pred[8]{0:T(512)(128)(4,1)S(1)} %iota_compare_fusion.2), kind=kLoop, calls=%fused_computation.4 | loop fusion | flops 1536 | bytes 2840 | tf_op jit(solution)/shard_map/jit(_where)/select_n | solution.py:338
  6.8 0.7 %collective-permute-done.1 = f32[40,64]{1,0:T(8,128)S(1)} collective-permute-done((f32[40,64]{1,0:T(8,128)S(1)}, f32[40,64]{1,0:T(8,128)S(1)}, u32[]{:S(2)}, u32[]{:S(2)}) %collective-permute-start.1) | collective-permute-done | bytes 10272 | tf_op jit(solution)/shard_map/ppermute | solution.py:362
  7.5 0.1 pad_maximum_fusion.2
  7.6 2.2 %collective-permute-start.4 = (f32[40,128]{1,0:T(8,128)S(1)}, f32[40,128]{1,0:T(8,128)S(1)}, u32[]{:S(2)}, u32[]{:S(2)}) collective-permute-start(f32[40,128]{1,0:T(8,128)S(1)} %pad_maximum_fusion.2), channel_id=1, source_target_pairs={{0,64},{16,80},{32,96},{48,112},{64,128},{80,144},{96,160},{112,17... | collective-permute-start | bytes 61448 | tf_op jit(solution)/shard_map/ppermute | solution.py:362
  9.8 0.7 %collective-permute-start.3 = (f32[40,128]{1,0:T(8,128)S(1)}, f32[40,128]{1,0:T(8,128)S(1)}, u32[]{:S(2)}, u32[]{:S(2)}) collective-permute-start(f32[40,128]{1,0:T(8,128)S(1)} %pad_maximum_fusion.2), channel_id=1, source_target_pairs={{0,128},{16,144},{32,160},{48,176},{64,192},{80,208},{96,224},{112... | collective-permute-start | bytes 61448 | tf_op jit(solution)/shard_map/ppermute | solution.py:362
  10.5 0.3 collective-permute-start.2
  10.8 0.0 copy-start
  10.8 0.9 %copy-done = bf16[3,3,64,124]{3,2,1,0:T(8,128)(2,1)S(1)} copy-done((bf16[3,3,64,124]{3,2,1,0:T(8,128)(2,1)S(1)}, bf16[3,3,64,124]{3,2,1,0:T(8,128)(2,1)}, u32[]{:S(2)}) %copy-start) | copy-done | bytes 142872
  11.7 0.0 copy-start.1
  11.7 0.9 %copy-done.1 = bf16[3,3,64,64]{3,2,1,0:T(8,128)(2,1)S(1)} copy-done((bf16[3,3,64,64]{3,2,1,0:T(8,128)(2,1)S(1)}, bf16[3,3,64,64]{3,2,1,0:T(8,128)(2,1)}, u32[]{:S(2)}) %copy-start.1) | copy-done | bytes 73752
  12.6 0.2 shard_map.91
  12.8 0.0 collective-permute-done.4
  12.8 2.3 %collective-permute-done.3 = f32[40,128]{1,0:T(8,128)S(1)} collective-permute-done((f32[40,128]{1,0:T(8,128)S(1)}, f32[40,128]{1,0:T(8,128)S(1)}, u32[]{:S(2)}, u32[]{:S(2)}) %collective-permute-start.3) | collective-permute-done | bytes 20512 | tf_op jit(solution)/shard_map/ppermute | solution.py:362
  15.1 0.4 %collective-permute-done.2 = f32[40,128]{1,0:T(8,128)S(1)} collective-permute-done((f32[40,128]{1,0:T(8,128)S(1)}, f32[40,128]{1,0:T(8,128)S(1)}, u32[]{:S(2)}, u32[]{:S(2)}) %collective-permute-start.2) | collective-permute-done | bytes 20512 | tf_op jit(solution)/shard_map/ppermute | solution.py:362
  15.5 2.0 %collective-permute-start.6 = (f32[4,40,128]{2,1,0:T(8,128)S(1)}, f32[4,40,128]{2,1,0:T(8,128)S(1)}, u32[]{:S(2)}, u32[]{:S(2)}) collective-permute-start(f32[4,40,128]{2,1,0:T(8,128)S(1)} %pad_maximum_fusion.own_ref), channel_id=1, source_target_pairs={{0,1},{1,0},{2,3},{3,2},{4,5},{5,4},{6,7},{7,6},{8,9},{9,8},{10,11... | collective-permute-start | bytes 245768 | tf_op jit(solution)/shard_map/ppermute | solution.py:362
  17.5 6.0 %collective-permute-start.5 = (f32[4,40,128]{2,1,0:T(8,128)S(1)}, f32[4,40,128]{2,1,0:T(8,128)S(1)}, u32[]{:S(2)}, u32[]{:S(2)}) collective-permute-start(f32[4,40,128]{2,1,0:T(8,128)S(1)} %pad_maximum_fusion.own_ref), channel_id=1, source_target_pairs={{0,15},{1,2},{2,1},{3,4},{4,3},{5,6},{6,5},{7,8},{8,7},{9,10},{10,... | collective-permute-start | bytes 245768 | tf_op jit(solution)/shard_map/ppermute | solution.py:362
  23.5 1.2 %shard_map.92 = (f32[2,640,512]{2,1,0:T(8,128)S(1)}, f32[640,128]{1,0:T(8,128)S(1)}) custom-call(f32[4,40,128]{2,1,0:T(8,128)S(1)} %pad_maximum_fusion.own_ref, f32[8,128]{1,0:T(8,128)S(1)} %get-tuple-element.53.table), custom_call_target="tpu_custom_call" | custom-call | flops 754974720 | bytes 3000000 | tf_op jit(solution)/shard_map/pallas_call | solution.py:266
  24.7 0.0 collective-permute-done.6.near_ref
  24.7 0.9 %shard_map.93 = (bf16[2560,128]{1,0:T(8,128)(2,1)S(1)}, f32[640,128]{1,0:T(8,128)S(1)}) custom-call(f32[4,40,128]{2,1,0:T(8,128)S(1)} %collective-permute-done.6.near_ref, f32[8,128]{1,0:T(8,128)S(1)} %get-tuple-element.53.table, f32[2,640,512]{2,1,0:T(8,128)S(1)} %get-tuple-element.54.s_own, f32[640,128]{1,0:T(8,128)S(1)} %get-tuple-element.55.s_edge), custom_call_target="tpu_custom_call" | custom-call | flops 419430400 | bytes 3000000 | tf_op jit(solution)/shard_map/pallas_call | solution.py:282
  25.6 0.3 collective-permute-done.5.far_ref
  25.9 4.0 %shard_map.94 = bf16[64,16,256]{2,1,0:T(8,128)(2,1)} custom-call(f32[4,40,128]{2,1,0:T(8,128)S(1)} %collective-permute-done.5.far_ref, f32[8,128]{1,0:T(8,128)S(1)} %get-tuple-element.53.table, f32[2,640,512]{2,1,0:T(8,128)S(1)} %get-tuple-element.54.s_own, f32[640,128]{1,0:T(8,128)S(1)} %get-tuple-element.56.s_edge, ...), custom_call_target="tpu_custom_call" | custom-call | tf_op jit(solution)/shard_map/pallas_call | solution.py:299
  (5 shorter events, 0.0 us)
Async XLA Ops:
  0.8 1.3 %collective-permute-start = (f32[40,32]{1,0:T(8,128)S(1)}, f32[40,32]{1,0:T(8,128)S(1)}, u32[]{:S(2)}, u32[]{:S(2)}) collective-permute-start(f32[40,32]{1,0:T(8,128)S(1)} %convert_add_fusion), channel_id=1, source_target_pairs={{0,16},{16,0},{32,48},{48,32},{64,80},{80,64},{96,112},{112,96},{1... | collective-permute-start | bytes 15368 | tf_op jit(solution)/shard_map/ppermute | solution.py:362
  2.2 5.3 %collective-permute-start.1 = (f32[40,64]{1,0:T(8,128)S(1)}, f32[40,64]{1,0:T(8,128)S(1)}, u32[]{:S(2)}, u32[]{:S(2)}) collective-permute-start(f32[40,64]{1,0:T(8,128)S(1)} %pad_maximum_fusion.1), channel_id=1, source_target_pairs={{0,32},{16,48},{32,0},{48,16},{64,96},{80,112},{96,64},{112,80},{1... | collective-permute-start | bytes 30728 | tf_op jit(solution)/shard_map/ppermute | solution.py:362
  7.6 5.2 %collective-permute-start.4 = (f32[40,128]{1,0:T(8,128)S(1)}, f32[40,128]{1,0:T(8,128)S(1)}, u32[]{:S(2)}, u32[]{:S(2)}) collective-permute-start(f32[40,128]{1,0:T(8,128)S(1)} %pad_maximum_fusion.2), channel_id=1, source_target_pairs={{0,64},{16,80},{32,96},{48,112},{64,128},{80,144},{96,160},{112,17... | collective-permute-start | bytes 61448 | tf_op jit(solution)/shard_map/ppermute | solution.py:362
  9.8 5.3 %collective-permute-start.3 = (f32[40,128]{1,0:T(8,128)S(1)}, f32[40,128]{1,0:T(8,128)S(1)}, u32[]{:S(2)}, u32[]{:S(2)}) collective-permute-start(f32[40,128]{1,0:T(8,128)S(1)} %pad_maximum_fusion.2), channel_id=1, source_target_pairs={{0,128},{16,144},{32,160},{48,176},{64,192},{80,208},{96,224},{112... | collective-permute-start | bytes 61448 | tf_op jit(solution)/shard_map/ppermute | solution.py:362
  10.5 5.0 %collective-permute-start.2 = (f32[40,128]{1,0:T(8,128)S(1)}, f32[40,128]{1,0:T(8,128)S(1)}, u32[]{:S(2)}, u32[]{:S(2)}) collective-permute-start(f32[40,128]{1,0:T(8,128)S(1)} %pad_maximum_fusion.2), channel_id=1, source_target_pairs={{0,192},{16,208},{32,224},{48,240},{64,0},{80,16},{96,32},{112,48}... | collective-permute-start | bytes 61448 | tf_op jit(solution)/shard_map/ppermute | solution.py:362
  10.8 0.9 %copy-start = (bf16[3,3,64,124]{3,2,1,0:T(8,128)(2,1)S(1)}, bf16[3,3,64,124]{3,2,1,0:T(8,128)(2,1)}, u32[]{:S(2)}) copy-start(bf16[3,3,64,124]{3,2,1,0:T(8,128)(2,1)} %first) | copy-start | bytes 428548
  11.7 0.9 %copy-start.1 = (bf16[3,3,64,64]{3,2,1,0:T(8,128)(2,1)S(1)}, bf16[3,3,64,64]{3,2,1,0:T(8,128)(2,1)}, u32[]{:S(2)}) copy-start(bf16[3,3,64,64]{3,2,1,0:T(8,128)(2,1)} %second) | copy-start | bytes 221188
  15.5 9.2 %collective-permute-start.6 = (f32[4,40,128]{2,1,0:T(8,128)S(1)}, f32[4,40,128]{2,1,0:T(8,128)S(1)}, u32[]{:S(2)}, u32[]{:S(2)}) collective-permute-start(f32[4,40,128]{2,1,0:T(8,128)S(1)} %pad_maximum_fusion.own_ref), channel_id=1, source_target_pairs={{0,1},{1,0},{2,3},{3,2},{4,5},{5,4},{6,7},{7,6},{8,9},{9,8},{10,11... | collective-permute-start | bytes 245768 | tf_op jit(solution)/shard_map/ppermute | solution.py:362
  17.5 8.4 %collective-permute-start.5 = (f32[4,40,128]{2,1,0:T(8,128)S(1)}, f32[4,40,128]{2,1,0:T(8,128)S(1)}, u32[]{:S(2)}, u32[]{:S(2)}) collective-permute-start(f32[4,40,128]{2,1,0:T(8,128)S(1)} %pad_maximum_fusion.own_ref), channel_id=1, source_target_pairs={{0,15},{1,2},{2,1},{3,4},{4,3},{5,6},{6,5},{7,8},{8,7},{9,10},{10,... | collective-permute-start | bytes 245768 | tf_op jit(solution)/shard_map/ppermute | solution.py:362

commit v4 on v3

--- a/solution.py
+++ b/solution.py
@@ -40,21 +40,22 @@
         copy.wait()
 
 
-def weights_kernel(first, second, small, w1, w2, w2_taps, b1, b2, table):
+def weights_kernel(both, small, w1, w2, w2_taps, b1, b2, table):
     source = lax.broadcasted_iota(jnp.int32, (CIN, 128), 0)
     slot = lax.broadcasted_iota(jnp.int32, (CIN, 128), 1)
+    shifted = source
     for k in range(1, INSTR):
         slot = jnp.where(slot == SLOT * k - 1, -1, slot)
-    shifted = source
-    for k in range(1, INSTR):
         shifted = shifted + jnp.where(source >= k * (VALUES + 1), 1, 0)
     spread = jnp.where(shifted == slot, 1.0, 0.0).astype(jnp.bfloat16)
     for a in range(3):
         for b in range(3):
             rows = slice(b * CHANNELS, (b + 1) * CHANNELS)
-            w1[rows, a * 128 : (a + 1) * 128] = dot(first[a, b], spread).astype(jnp.bfloat16)
-            w2[rows, a * CHANNELS : (a + 1) * CHANNELS] = second[a, b]
-            w2_taps[a, rows, :] = second[a, b]
+            first = both[a, b, 0:CHANNELS, :]
+            second = both[a, b, CHANNELS : 2 * CHANNELS, 0:CHANNELS]
+            w1[rows, a * 128 : (a + 1) * 128] = dot(first, spread).astype(jnp.bfloat16)
+            w2[rows, a * CHANNELS : (a + 1) * CHANNELS] = second
+            w2_taps[a, rows, :] = second
     up = lax.broadcasted_iota(jnp.int32, (CHANNELS, CHANNELS), 0)
     across = lax.broadcasted_iota(jnp.int32, (CHANNELS, CHANNELS), 1)
     for n, column in enumerate((b1, b2)):
@@ -85,9 +86,10 @@
     for block in range(4):
         cols = slice(block * 128, (block + 1) * 128)
         data = ref[block]
-        lat = data[0:1]
+        code = data[0:1].astype(jnp.int32)
+        lat = (code // INSTR).astype(jnp.float32)
+        inst = (code % INSTR).astype(jnp.float32)
         lon = data[31:32]
-        inst = data[32:33]
         rate = table[0:1]
         reach2 = table[INSTR : INSTR + 1]
         for k in range(1, INSTR):
@@ -321,25 +323,26 @@
 
 
 def pack(obs_values, obs_lat, obs_lon, instrument):
-    shape = (40, ROWS_DEV)
+    shape = (SLOT, ROWS_DEV)
     row = lax.broadcasted_iota(jnp.int32, shape, 0)
-    ints = jnp.where(row == 32, along(instrument, shape), 0)
-    ints = jnp.where(row == 31, along(obs_lon, shape), ints)
-    ints = jnp.where(row == 0, along(obs_lat, shape), ints)
-    return jnp.pad(obs_values, ((1, 9), (0, 0))) + ints.astype(jnp.float32)
-
-
-def pack_small(b_first, b_second, length_scale):
+    high = jnp.where(row == 0, along(obs_lat, shape), 0)
+    ints = jnp.where(row == 31, along(obs_lon, shape), 0)
+    ints = jnp.where(row == 0, along(instrument, shape), ints)
+    return jnp.pad(obs_values, ((1, 1), (0, 0))) + (high * INSTR + ints).astype(jnp.float32)
+
+
+def pack_small(b_first, b_second, scale):
     shape = (8, CHANNELS)
     row = lax.broadcasted_iota(jnp.int32, shape, 0)
-    scale = along(jnp.pad(length_scale, (0, CHANNELS - INSTR)), shape)
-    small = jnp.where(row == 2, scale, 0.0)
+    small = jnp.where(row == 2, along(scale, shape), 0.0)
     small = jnp.where(row == 1, along(b_second, shape), small)
     return jnp.where(row == 0, along(b_first, shape), small)
 
 
 def arrange(w_first, w_second, small):
     bf16, f32 = jnp.bfloat16, jnp.float32
+    wide = jnp.pad(w_second, ((0, 0), (0, 0), (CHANNELS, 0), (0, CIN - CHANNELS)))
+    both = jnp.pad(w_first, ((0, 0), (0, 0), (0, CHANNELS), (0, 0))) + wide
     return pl.pallas_call(
         weights_kernel,
         out_shape=[
@@ -350,11 +353,11 @@
             jax.ShapeDtypeStruct((CHANNELS, 1), f32),
             jax.ShapeDtypeStruct((2 * INSTR, 128), f32),
         ],
-        in_specs=[pl.BlockSpec(memory_space=pltpu.VMEM)] * 3,
+        in_specs=[pl.BlockSpec(memory_space=pltpu.VMEM)] * 2,
         out_specs=[pl.BlockSpec(memory_space=pltpu.VMEM)] * 6,
         compiler_params=pltpu.CompilerParams(vmem_limit_bytes=4 * 1024 * 1024),
         cost_estimate=pl.CostEstimate(flops=20000000, bytes_accessed=1000000, transcendentals=0),
-    )(w_first, w_second, small)
+    )(both, small)
 
 
 def send(array, axis, target):
@@ -366,19 +369,23 @@
     obs_values, obs_lat, obs_lon, instrument, length_scale, w_first, b_first, w_second, b_second
 ):
     rows = pack(obs_values, obs_lat, obs_lon, instrument)
-    rows = jnp.concatenate([rows, send(rows, "lat", lambda i: i ^ 1)], axis=1)
-    rows, b_first, b_second, length_scale = lax.optimization_barrier(
-        (rows, b_first, b_second, length_scale)
-    )
-    small = pack_small(b_first, b_second, length_scale)
-    others = send(rows, "lat", lambda i: i ^ 2)
-    rows, others, small, w_first, w_second = lax.optimization_barrier(
-        (rows, others, small, w_first, w_second)
+    rows, length_scale = lax.optimization_barrier((rows, length_scale))
+    scale = jnp.pad(length_scale, (0, CHANNELS - INSTR))
+    others = send(rows, "lat", lambda i: i ^ 1)
+    rows, others, scale, b_first, b_second, w_first, w_second = lax.optimization_barrier(
+        (rows, others, scale, b_first, b_second, w_first, w_second)
     )
     rows = jnp.concatenate([rows, others], axis=1)
-    weights = arrange(w_first, w_second, small)
-    others = [send(rows, "lat", lambda i, k=k: i + 4 * k) for k in (3, 2, 1)]
+    rows, b_first, b_second, w_first, w_second = lax.optimization_barrier(
+        (rows, b_first, b_second, w_first, w_second)
+    )
+    weights = arrange(w_first, w_second, pack_small(b_first, b_second, scale))
+    others = send(rows, "lat", lambda i: i ^ 2)
     rows, others, weights = lax.optimization_barrier((rows, others, weights))
+    rows = jnp.concatenate([rows, others], axis=1)
+    across = send(rows, "lat", lambda i: i ^ 8)
+    beside = send(rows, "lat", lambda i: i + 4 if i % 2 == 0 else i - 4)
+    others = [across, send(beside, "lat", lambda i: i ^ 1), beside]
     rows = jnp.stack([rows] + others)
     near = send(rows, "lon", lambda i: i ^ 1)
     far = send(rows, "lon", lambda i: ((i + 1) ^ 1) - 1)

time: 30.1 us -> 28.7 us (0.953)
  the two profiles are of different devices: /device:TPU:6 before, /device:TPU:1 now
where the time goes in v4:
time: 28.7 us; the launch traced here: 28.4 us
  starting transfers between devices  16.1 us (56%)
  Pallas kernels  6.44 us (22%)
  other arithmetic  2.85 us (10%)
  waiting for transfers between devices  2.3 us (8%)
  local copies, waits for them, and re-layouts  0.66 us (2%)
    ppermute x7, starting transfers between devices, send(): lax.ppermute(array, axis, [(i, target(i) % peers) for i in range(peers)])  16.1 us
    pallas_call x1, Pallas kernels, encode(): pl.pallas_call(encode_kernel, out_shape=jax.ShapeDtypeStruct((CHANNELS, C...  4.04 us
    ppermute x7, waiting for transfers between devices, send(): lax.ppermute(array, axis, [(i, target(i) % peers) for i in range(peers)])  2.3 us
    pallas_call x1, Pallas kernels, encode(): pl.pallas_call(own_kernel, out_shape=[jax.ShapeDtypeStruct((2, rows, INST...  1.28 us
    add x1, other arithmetic, arrange(): both = jnp.pad(w_first, ((0, 0), (0, 0), (0, CHANNELS), (0, 0))) + wide  1.04 us
    pallas_call x1, Pallas kernels, encode(): pl.pallas_call(near_kernel, out_shape=[jax.ShapeDtypeStruct((EXT * 128, 1...  0.89 us
    add x1, other arithmetic, pack(): jnp.pad(obs_values, ((1, 1), (0, 0)))  0.82 us
    select_n x1, other arithmetic, pack_small(): return jnp.where(row == 0, along(b_first, shape), small)  0.74 us
  transfers between devices with their start and end apart: 7, of which 4 were waited for; matrix products, arithmetic and copies ran while one was open for 9% of the time, Pallas kernels for 8%

profile of v4, /device:TPU:1, one launch (start us, length us, event | category | flops | bytes accessed | tf_op | source)
XLA Modules:
  0.0 28.4 jit_solution(7652270419302884840)
XLA Ops:
  0.0 0.8 %convert_add_fusion = f32[32,32]{1,0:T(8,128)S(1)} fusion(f32[30,32]{1,0:T(8,128)} %param.9, s32[32]{0:T(128)} %param.11, s32[32]{0:T(128)} %param.12, s32[32]{0:T(128)} %param.10, pred[32]{0:T(512)(128)(4,1)S(1)} %get-tuple-element.69, pred[32]{0:T(512)(128)(4,1)S(1)} %get-tuple-element.70), kind=kLoop, calls=%fused_computation.4 | loop fusion | flops 7168 | bytes 8384 | tf_op jit(solution)/shard_map/add | solution.py:331
  0.8 3.3 %collective-permute-start = (f32[32,32]{1,0:T(8,128)S(1)}, f32[32,32]{1,0:T(8,128)S(1)}, u32[]{:S(2)}, u32[]{:S(2)}) collective-permute-start(f32[32,32]{1,0:T(8,128)S(1)} %convert_add_fusion), channel_id=1, source_target_pairs={{0,16},{16,0},{32,48},{48,32},{64,80},{80,64},{96,112},{112,96},{1... | collective-permute-start | bytes 12296 | tf_op jit(solution)/shard_map/ppermute | solution.py:365
  4.2 0.7 %pad.17 = f32[64]{0:T(128)S(1)} pad(f32[4]{0:T(128)} %param.13, f32[]{:T(128)} %constant.7.clone.1), padding=0_60 | pad | bytes 276 | tf_op jit(solution)/shard_map/jit(_pad)/pad | solution.py:373
  4.8 0.2 collective-permute-done
  5.0 0.1 pad_maximum_fusion.1
  5.1 1.2 %collective-permute-start.1 = (f32[32,64]{1,0:T(8,128)S(1)}, f32[32,64]{1,0:T(8,128)S(1)}, u32[]{:S(2)}, u32[]{:S(2)}) collective-permute-start(f32[32,64]{1,0:T(8,128)S(1)} %pad_maximum_fusion.1), channel_id=1, source_target_pairs={{0,32},{16,48},{32,0},{48,16},{64,96},{80,112},{96,64},{112,80},{1... | collective-permute-start | bytes 24584 | tf_op jit(solution)/shard_map/ppermute | solution.py:365
  6.3 0.7 %select_select_fusion.small = f32[8,64]{1,0:T(8,128)S(1)} fusion(f32[64]{0:T(128)S(1)} %pad.17, f32[64]{0:T(128)} %param.17, f32[64]{0:T(128)} %param.15, pred[8]{0:T(512)(128)(4,1)S(1)} %get-tuple-element.71, pred[8]{0:T(512)(128)(4,1)S(1)} %get-tuple-element.72, pred[8]{0:T(512)(128)(4,1)S(1)} %iota_compare_fusion.2), kind=kLoop, calls=%fused_computation.5 | loop fusion | flops 1536 | bytes 2840 | tf_op jit(solution)/shard_map/jit(_where)/select_n | solution.py:339
  7.0 1.0 %pad_add_fusion.both = bf16[3,3,128,124]{3,2,1,0:T(8,128)(2,1)S(1)} fusion(bf16[3,3,64,64]{3,2,1,0:T(8,128)(2,1)} %param.16, bf16[3,3,64,124]{3,2,1,0:T(8,128)(2,1)} %param.14), kind=kLoop, calls=%fused_computation | loop fusion | flops 571392 | bytes 502272 | tf_op jit(solution)/shard_map/add | solution.py:345
  8.1 0.2 shard_map.91
  8.3 0.9 %collective-permute-done.1 = f32[32,64]{1,0:T(8,128)S(1)} collective-permute-done((f32[32,64]{1,0:T(8,128)S(1)}, f32[32,64]{1,0:T(8,128)S(1)}, u32[]{:S(2)}, u32[]{:S(2)}) %collective-permute-start.1) | collective-permute-done | bytes 8224 | tf_op jit(solution)/shard_map/ppermute | solution.py:365
  9.2 0.1 pad_maximum_fusion.2
  9.3 1.6 %collective-permute-start.3 = (f32[32,128]{1,0:T(8,128)S(1)}, f32[32,128]{1,0:T(8,128)S(1)}, u32[]{:S(2)}, u32[]{:S(2)}) collective-permute-start(f32[32,128]{1,0:T(8,128)S(1)} %pad_maximum_fusion.2), channel_id=1, source_target_pairs={{0,64},{16,208},{32,96},{48,240},{64,128},{80,16},{96,160},{112,48... | collective-permute-start | bytes 49160 | tf_op jit(solution)/shard_map/ppermute | solution.py:365
  10.9 0.5 %collective-permute-start.2 = (f32[32,128]{1,0:T(8,128)S(1)}, f32[32,128]{1,0:T(8,128)S(1)}, u32[]{:S(2)}, u32[]{:S(2)}) collective-permute-start(f32[32,128]{1,0:T(8,128)S(1)} %pad_maximum_fusion.2), channel_id=1, source_target_pairs={{0,128},{16,144},{32,160},{48,176},{64,192},{80,208},{96,224},{112... | collective-permute-start | bytes 49160 | tf_op jit(solution)/shard_map/ppermute | solution.py:365
  11.4 0.5 %collective-permute-done.3 = f32[32,128]{1,0:T(8,128)S(1)} collective-permute-done((f32[32,128]{1,0:T(8,128)S(1)}, f32[32,128]{1,0:T(8,128)S(1)}, u32[]{:S(2)}, u32[]{:S(2)}) %collective-permute-start.3) | collective-permute-done | bytes 16416 | tf_op jit(solution)/shard_map/ppermute | solution.py:365
  11.9 4.0 %collective-permute-start.4 = (f32[32,128]{1,0:T(8,128)S(1)}, f32[32,128]{1,0:T(8,128)S(1)}, u32[]{:S(2)}, u32[]{:S(2)}) collective-permute-start(f32[32,128]{1,0:T(8,128)S(1)} %collective-permute-done.3), channel_id=1, source_target_pairs={{0,16},{16,0},{32,48},{48,32},{64,80},{80,64},{96,112},{112,96},{1... | collective-permute-start | bytes 49160 | tf_op jit(solution)/shard_map/ppermute | solution.py:365
  15.8 0.1 fusion
  15.9 0.0 collective-permute-done.2
  15.9 0.8 %collective-permute-done.4 = f32[32,128]{1,0:T(8,128)S(1)} collective-permute-done((f32[32,128]{1,0:T(8,128)S(1)}, f32[32,128]{1,0:T(8,128)S(1)}, u32[]{:S(2)}, u32[]{:S(2)}) %collective-permute-start.4) | collective-permute-done | bytes 16416 | tf_op jit(solution)/shard_map/ppermute | solution.py:365
  16.7 0.4 %collective-permute-start.6 = (f32[4,32,128]{2,1,0:T(8,128)S(1)}, f32[4,32,128]{2,1,0:T(8,128)S(1)}, u32[]{:S(2)}, u32[]{:S(2)}) collective-permute-start(f32[4,32,128]{2,1,0:T(8,128)S(1)} %pad_maximum_fusion.own_ref), channel_id=1, source_target_pairs={{0,1},{1,0},{2,3},{3,2},{4,5},{5,4},{6,7},{7,6},{8,9},{9,8},{10,11... | collective-permute-start | bytes 196616 | tf_op jit(solution)/shard_map/ppermute | solution.py:365
  17.1 5.1 %collective-permute-start.5 = (f32[4,32,128]{2,1,0:T(8,128)S(1)}, f32[4,32,128]{2,1,0:T(8,128)S(1)}, u32[]{:S(2)}, u32[]{:S(2)}) collective-permute-start(f32[4,32,128]{2,1,0:T(8,128)S(1)} %pad_maximum_fusion.own_ref), channel_id=1, source_target_pairs={{0,15},{1,2},{2,1},{3,4},{4,3},{5,6},{6,5},{7,8},{8,7},{9,10},{10,... | collective-permute-start | bytes 196616 | tf_op jit(solution)/shard_map/ppermute | solution.py:365
  22.2 1.3 %shard_map.92 = (f32[2,640,512]{2,1,0:T(8,128)S(1)}, f32[640,128]{1,0:T(8,128)S(1)}) custom-call(f32[4,32,128]{2,1,0:T(8,128)S(1)} %pad_maximum_fusion.own_ref, f32[8,128]{1,0:T(8,128)S(1)} %get-tuple-element.59.table), custom_call_target="tpu_custom_call" | custom-call | flops 754974720 | bytes 3000000 | tf_op jit(solution)/shard_map/pallas_call | solution.py:268
  23.4 0.0 collective-permute-done.6.near_ref
  23.4 0.9 %shard_map.93 = (bf16[2560,128]{1,0:T(8,128)(2,1)S(1)}, f32[640,128]{1,0:T(8,128)S(1)}) custom-call(f32[4,32,128]{2,1,0:T(8,128)S(1)} %collective-permute-done.6.near_ref, f32[8,128]{1,0:T(8,128)S(1)} %get-tuple-element.59.table, f32[2,640,512]{2,1,0:T(8,128)S(1)} %get-tuple-element.60.s_own, f32[640,128]{1,0:T(8,128)S(1)} %get-tuple-element.61.s_edge), custom_call_target="tpu_custom_call" | custom-call | flops 419430400 | bytes 3000000 | tf_op jit(solution)/shard_map/pallas_call | solution.py:284
  24.3 0.0 collective-permute-done.5.far_ref
  24.4 4.0 %shard_map.94 = bf16[64,16,256]{2,1,0:T(8,128)(2,1)} custom-call(f32[4,32,128]{2,1,0:T(8,128)S(1)} %collective-permute-done.5.far_ref, f32[8,128]{1,0:T(8,128)S(1)} %get-tuple-element.59.table, f32[2,640,512]{2,1,0:T(8,128)S(1)} %get-tuple-element.60.s_own, f32[640,128]{1,0:T(8,128)S(1)} %get-tuple-element.62.s_edge, ...), custom_call_target="tpu_custom_call" | custom-call | tf_op jit(solution)/shard_map/pallas_call | solution.py:301
  (4 shorter events, 0.0 us)
Async XLA Ops:
  0.8 4.2 %collective-permute-start = (f32[32,32]{1,0:T(8,128)S(1)}, f32[32,32]{1,0:T(8,128)S(1)}, u32[]{:S(2)}, u32[]{:S(2)}) collective-permute-start(f32[32,32]{1,0:T(8,128)S(1)} %convert_add_fusion), channel_id=1, source_target_pairs={{0,16},{16,0},{32,48},{48,32},{64,80},{80,64},{96,112},{112,96},{1... | collective-permute-start | bytes 12296 | tf_op jit(solution)/shard_map/ppermute | solution.py:365
  5.1 4.1 %collective-permute-start.1 = (f32[32,64]{1,0:T(8,128)S(1)}, f32[32,64]{1,0:T(8,128)S(1)}, u32[]{:S(2)}, u32[]{:S(2)}) collective-permute-start(f32[32,64]{1,0:T(8,128)S(1)} %pad_maximum_fusion.1), channel_id=1, source_target_pairs={{0,32},{16,48},{32,0},{48,16},{64,96},{80,112},{96,64},{112,80},{1... | collective-permute-start | bytes 24584 | tf_op jit(solution)/shard_map/ppermute | solution.py:365
  9.3 2.6 %collective-permute-start.3 = (f32[32,128]{1,0:T(8,128)S(1)}, f32[32,128]{1,0:T(8,128)S(1)}, u32[]{:S(2)}, u32[]{:S(2)}) collective-permute-start(f32[32,128]{1,0:T(8,128)S(1)} %pad_maximum_fusion.2), channel_id=1, source_target_pairs={{0,64},{16,208},{32,96},{48,240},{64,128},{80,16},{96,160},{112,48... | collective-permute-start | bytes 49160 | tf_op jit(solution)/shard_map/ppermute | solution.py:365
  10.9 5.0 %collective-permute-start.2 = (f32[32,128]{1,0:T(8,128)S(1)}, f32[32,128]{1,0:T(8,128)S(1)}, u32[]{:S(2)}, u32[]{:S(2)}) collective-permute-start(f32[32,128]{1,0:T(8,128)S(1)} %pad_maximum_fusion.2), channel_id=1, source_target_pairs={{0,128},{16,144},{32,160},{48,176},{64,192},{80,208},{96,224},{112... | collective-permute-start | bytes 49160 | tf_op jit(solution)/shard_map/ppermute | solution.py:365
  11.9 4.8 %collective-permute-start.4 = (f32[32,128]{1,0:T(8,128)S(1)}, f32[32,128]{1,0:T(8,128)S(1)}, u32[]{:S(2)}, u32[]{:S(2)}) collective-permute-start(f32[32,128]{1,0:T(8,128)S(1)} %collective-permute-done.3), channel_id=1, source_target_pairs={{0,16},{16,0},{32,48},{48,32},{64,80},{80,64},{96,112},{112,96},{1... | collective-permute-start | bytes 49160 | tf_op jit(solution)/shard_map/ppermute | solution.py:365
  16.7 6.8 %collective-permute-start.6 = (f32[4,32,128]{2,1,0:T(8,128)S(1)}, f32[4,32,128]{2,1,0:T(8,128)S(1)}, u32[]{:S(2)}, u32[]{:S(2)}) collective-permute-start(f32[4,32,128]{2,1,0:T(8,128)S(1)} %pad_maximum_fusion.own_ref), channel_id=1, source_target_pairs={{0,1},{1,0},{2,3},{3,2},{4,5},{5,4},{6,7},{7,6},{8,9},{9,8},{10,11... | collective-permute-start | bytes 196616 | tf_op jit(solution)/shard_map/ppermute | solution.py:365
  17.1 7.3 %collective-permute-start.5 = (f32[4,32,128]{2,1,0:T(8,128)S(1)}, f32[4,32,128]{2,1,0:T(8,128)S(1)}, u32[]{:S(2)}, u32[]{:S(2)}) collective-permute-start(f32[4,32,128]{2,1,0:T(8,128)S(1)} %pad_maximum_fusion.own_ref), channel_id=1, source_target_pairs={{0,15},{1,2},{2,1},{3,4},{4,3},{5,6},{6,5},{7,8},{8,7},{9,10},{10,... | collective-permute-start | bytes 196616 | tf_op jit(solution)/shard_map/ppermute | solution.py:365

commit v5 on v4

--- a/solution.py
+++ b/solution.py
@@ -15,6 +15,7 @@
 NLAT = 256
 NLON = 4096
 ROWS_DEV = 32
+STEP = 24
 PARTS = 4
 EXT = CLAT + 4
 HID = CLAT + 2
@@ -237,22 +238,21 @@
     w2 = w2_ref[...]
     b2 = b2_ref[...]
     terms = edge_terms([dot(w2_taps[a], edge_hid) for a in range(3)])
-    size = CHANNELS * CLAT
+    size = CHANNELS * STEP
     for r in range(CLAT):
         y = dot(w2, hid[r * CHANNELS : (r + 3) * CHANNELS, :])
         for n, half in enumerate(row_total(y, terms, r, b2)):
-            stage[pl.ds(n * size + r, CHANNELS, CLAT), :] = half
+            stage[pl.ds(n * size + r, CHANNELS, STEP), :] = half
 
     copies = []
     step = CHANNELS // PARTS
     for part in range(PARTS):
         channels = slice(part * step, (part + 1) * step)
         for n in range(2):
-            result[channels, :, n * 128 : (n + 1) * 128] = (
-                stage[n * size + part * step * CLAT : n * size + (part + 1) * step * CLAT, :]
-                .reshape(step, CLAT, 128)
-                .astype(jnp.bfloat16)
-            )
+            for p in range(part * step, (part + 1) * step):
+                result[p, :, n * 128 : (n + 1) * 128] = stage[
+                    n * size + p * STEP : n * size + p * STEP + CLAT, :
+                ].astype(jnp.bfloat16)
         copies.append(
             pltpu.make_async_copy(result.at[channels], out_ref.at[channels], sems.at[part])
         )
@@ -310,7 +310,7 @@
             pltpu.VMEM((rows, INSTR * 128), f32),
             pltpu.VMEM((EXT * 128, CLON), bf16),
             pltpu.VMEM((HID * CHANNELS, CLON), bf16),
-            pltpu.VMEM((2 * CHANNELS * CLAT, 128), f32),
+            pltpu.VMEM((2 * CHANNELS * STEP, 128), f32),
             pltpu.VMEM((CHANNELS, CLAT, CLON), bf16),
             pltpu.SemaphoreType.DMA((PARTS,)),
         ],
@@ -383,7 +383,7 @@
     others = send(rows, "lat", lambda i: i ^ 2)
     rows, others, weights = lax.optimization_barrier((rows, others, weights))
     rows = jnp.concatenate([rows, others], axis=1)
-    across = send(rows, "lat", lambda i: i ^ 8)
+    across = send(rows, "lat", lambda i: i ^ 9)
     beside = send(rows, "lat", lambda i: i + 4 if i % 2 == 0 else i - 4)
     others = [across, send(beside, "lat", lambda i: i ^ 1), beside]
     rows = jnp.stack([rows] + others)

time: 28.7 us -> 28.4 us (0.990)
  starting transfers between devices: 16.1 us -> 16.6 us
  waiting for transfers between devices: 2.3 us -> 1.83 us
    ppermute x7, starting transfers between devices: 16.1 us -> 16.6 us  [send(): lax.ppermute(array, axis, [(i, target(i) % peers) for i in range(peers)])]
    ppermute x7, waiting for transfers between devices: 2.3 us -> 1.83 us  [send(): lax.ppermute(array, axis, [(i, target(i) % peers) for i in range(peers)])]
  transfers between devices with their start and end apart: 7 -> 7, of which waited for: 4 -> 3; matrix products, arithmetic and copies ran while one was open for 9% -> 9% of each run, Pallas kernels for 8% -> 8%
where the time goes in v5:
time: 28.4 us; the launch traced here: 28.2 us
  starting transfers between devices  16.6 us (58%)
  Pallas kernels  6.2 us (22%)
  other arithmetic  2.85 us (10%)
  waiting for transfers between devices  1.83 us (6%)
  local copies, waits for them, and re-layouts  0.66 us (2%)
    ppermute x7, starting transfers between devices, send(): lax.ppermute(array, axis, [(i, target(i) % peers) for i in range(peers)])  16.6 us
    pallas_call x1, Pallas kernels, encode(): pl.pallas_call(encode_kernel, out_shape=jax.ShapeDtypeStruct((CHANNELS, C...  3.81 us
    ppermute x7, waiting for transfers between devices, send(): lax.ppermute(array, axis, [(i, target(i) % peers) for i in range(peers)])  1.83 us
    pallas_call x1, Pallas kernels, encode(): pl.pallas_call(own_kernel, out_shape=[jax.ShapeDtypeStruct((2, rows, INST...  1.28 us
    add x1, other arithmetic, arrange(): both = jnp.pad(w_first, ((0, 0), (0, 0), (0, CHANNELS), (0, 0))) + wide  1.04 us
    pallas_call x1, Pallas kernels, encode(): pl.pallas_call(near_kernel, out_shape=[jax.ShapeDtypeStruct((EXT * 128, 1...  0.89 us
    add x1, other arithmetic, pack(): jnp.pad(obs_values, ((1, 1), (0, 0)))  0.82 us
    select_n x1, other arithmetic, pack_small(): return jnp.where(row == 0, along(b_first, shape), small)  0.74 us
  transfers between devices with their start and end apart: 7, of which 3 were waited for; matrix products, arithmetic and copies ran while one was open for 9% of the time, Pallas kernels for 8%

profile of v5, /device:TPU:1, one launch (start us, length us, event | category | flops | bytes accessed | tf_op | source)
XLA Modules:
  0.0 28.2 jit_solution(9202748342167139465)
XLA Ops:
  0.0 0.8 %convert_add_fusion = f32[32,32]{1,0:T(8,128)S(1)} fusion(f32[30,32]{1,0:T(8,128)} %param.9, s32[32]{0:T(128)} %param.11, s32[32]{0:T(128)} %param.12, s32[32]{0:T(128)} %param.10, pred[32]{0:T(512)(128)(4,1)S(1)} %get-tuple-element.69, pred[32]{0:T(512)(128)(4,1)S(1)} %get-tuple-element.70), kind=kLoop, calls=%fused_computation.4 | loop fusion | flops 7168 | bytes 8384 | tf_op jit(solution)/shard_map/add | solution.py:331
  0.8 3.3 %collective-permute-start = (f32[32,32]{1,0:T(8,128)S(1)}, f32[32,32]{1,0:T(8,128)S(1)}, u32[]{:S(2)}, u32[]{:S(2)}) collective-permute-start(f32[32,32]{1,0:T(8,128)S(1)} %convert_add_fusion), channel_id=1, source_target_pairs={{0,16},{16,0},{32,48},{48,32},{64,80},{80,64},{96,112},{112,96},{1... | collective-permute-start | bytes 12296 | tf_op jit(solution)/shard_map/ppermute | solution.py:365
  4.2 0.7 %pad.17 = f32[64]{0:T(128)S(1)} pad(f32[4]{0:T(128)} %param.13, f32[]{:T(128)} %constant.7.clone.1), padding=0_60 | pad | bytes 276 | tf_op jit(solution)/shard_map/jit(_pad)/pad | solution.py:373
  4.8 0.2 collective-permute-done
  5.0 0.1 pad_maximum_fusion.1
  5.1 1.2 %collective-permute-start.1 = (f32[32,64]{1,0:T(8,128)S(1)}, f32[32,64]{1,0:T(8,128)S(1)}, u32[]{:S(2)}, u32[]{:S(2)}) collective-permute-start(f32[32,64]{1,0:T(8,128)S(1)} %pad_maximum_fusion.1), channel_id=1, source_target_pairs={{0,32},{16,48},{32,0},{48,16},{64,96},{80,112},{96,64},{112,80},{1... | collective-permute-start | bytes 24584 | tf_op jit(solution)/shard_map/ppermute | solution.py:365
  6.3 0.7 %select_select_fusion.small = f32[8,64]{1,0:T(8,128)S(1)} fusion(f32[64]{0:T(128)S(1)} %pad.17, f32[64]{0:T(128)} %param.17, f32[64]{0:T(128)} %param.15, pred[8]{0:T(512)(128)(4,1)S(1)} %get-tuple-element.71, pred[8]{0:T(512)(128)(4,1)S(1)} %get-tuple-element.72, pred[8]{0:T(512)(128)(4,1)S(1)} %iota_compare_fusion.2), kind=kLoop, calls=%fused_computation.5 | loop fusion | flops 1536 | bytes 2840 | tf_op jit(solution)/shard_map/jit(_where)/select_n | solution.py:339
  7.0 1.0 %pad_add_fusion.both = bf16[3,3,128,124]{3,2,1,0:T(8,128)(2,1)S(1)} fusion(bf16[3,3,64,64]{3,2,1,0:T(8,128)(2,1)} %param.16, bf16[3,3,64,124]{3,2,1,0:T(8,128)(2,1)} %param.14), kind=kLoop, calls=%fused_computation | loop fusion | flops 571392 | bytes 502272 | tf_op jit(solution)/shard_map/add | solution.py:345
  8.1 0.2 shard_map.91
  8.3 0.9 %collective-permute-done.1 = f32[32,64]{1,0:T(8,128)S(1)} collective-permute-done((f32[32,64]{1,0:T(8,128)S(1)}, f32[32,64]{1,0:T(8,128)S(1)}, u32[]{:S(2)}, u32[]{:S(2)}) %collective-permute-start.1) | collective-permute-done | bytes 8224 | tf_op jit(solution)/shard_map/ppermute | solution.py:365
  9.2 0.1 pad_maximum_fusion.2
  9.3 1.6 %collective-permute-start.3 = (f32[32,128]{1,0:T(8,128)S(1)}, f32[32,128]{1,0:T(8,128)S(1)}, u32[]{:S(2)}, u32[]{:S(2)}) collective-permute-start(f32[32,128]{1,0:T(8,128)S(1)} %pad_maximum_fusion.2), channel_id=1, source_target_pairs={{0,64},{16,208},{32,96},{48,240},{64,128},{80,16},{96,160},{112,48... | collective-permute-start | bytes 49160 | tf_op jit(solution)/shard_map/ppermute | solution.py:365
  10.9 2.0 %collective-permute-start.2 = (f32[32,128]{1,0:T(8,128)S(1)}, f32[32,128]{1,0:T(8,128)S(1)}, u32[]{:S(2)}, u32[]{:S(2)}) collective-permute-start(f32[32,128]{1,0:T(8,128)S(1)} %pad_maximum_fusion.2), channel_id=1, source_target_pairs={{0,144},{16,128},{32,176},{48,160},{64,208},{80,192},{96,240},{112... | collective-permute-start | bytes 49160 | tf_op jit(solution)/shard_map/ppermute | solution.py:365
  12.9 0.0 collective-permute-done.3
  12.9 2.9 %collective-permute-start.4 = (f32[32,128]{1,0:T(8,128)S(1)}, f32[32,128]{1,0:T(8,128)S(1)}, u32[]{:S(2)}, u32[]{:S(2)}) collective-permute-start(f32[32,128]{1,0:T(8,128)S(1)} %collective-permute-done.3), channel_id=1, source_target_pairs={{0,16},{16,0},{32,48},{48,32},{64,80},{80,64},{96,112},{112,96},{1... | collective-permute-start | bytes 49160 | tf_op jit(solution)/shard_map/ppermute | solution.py:365
  15.7 0.1 fusion
  15.8 0.0 collective-permute-done.2
  15.8 0.8 %collective-permute-done.4 = f32[32,128]{1,0:T(8,128)S(1)} collective-permute-done((f32[32,128]{1,0:T(8,128)S(1)}, f32[32,128]{1,0:T(8,128)S(1)}, u32[]{:S(2)}, u32[]{:S(2)}) %collective-permute-start.4) | collective-permute-done | bytes 16416 | tf_op jit(solution)/shard_map/ppermute | solution.py:365
  16.6 0.7 %collective-permute-start.6 = (f32[4,32,128]{2,1,0:T(8,128)S(1)}, f32[4,32,128]{2,1,0:T(8,128)S(1)}, u32[]{:S(2)}, u32[]{:S(2)}) collective-permute-start(f32[4,32,128]{2,1,0:T(8,128)S(1)} %pad_maximum_fusion.own_ref), channel_id=1, source_target_pairs={{0,1},{1,0},{2,3},{3,2},{4,5},{5,4},{6,7},{7,6},{8,9},{9,8},{10,11... | collective-permute-start | bytes 196616 | tf_op jit(solution)/shard_map/ppermute | solution.py:365
  17.3 4.9 %collective-permute-start.5 = (f32[4,32,128]{2,1,0:T(8,128)S(1)}, f32[4,32,128]{2,1,0:T(8,128)S(1)}, u32[]{:S(2)}, u32[]{:S(2)}) collective-permute-start(f32[4,32,128]{2,1,0:T(8,128)S(1)} %pad_maximum_fusion.own_ref), channel_id=1, source_target_pairs={{0,15},{1,2},{2,1},{3,4},{4,3},{5,6},{6,5},{7,8},{8,7},{9,10},{10,... | collective-permute-start | bytes 196616 | tf_op jit(solution)/shard_map/ppermute | solution.py:365
  22.2 1.3 %shard_map.92 = (f32[2,640,512]{2,1,0:T(8,128)S(1)}, f32[640,128]{1,0:T(8,128)S(1)}) custom-call(f32[4,32,128]{2,1,0:T(8,128)S(1)} %pad_maximum_fusion.own_ref, f32[8,128]{1,0:T(8,128)S(1)} %get-tuple-element.59.table), custom_call_target="tpu_custom_call" | custom-call | flops 754974720 | bytes 3000000 | tf_op jit(solution)/shard_map/pallas_call | solution.py:268
  23.5 0.0 collective-permute-done.6.near_ref
  23.5 0.9 %shard_map.93 = (bf16[2560,128]{1,0:T(8,128)(2,1)S(1)}, f32[640,128]{1,0:T(8,128)S(1)}) custom-call(f32[4,32,128]{2,1,0:T(8,128)S(1)} %collective-permute-done.6.near_ref, f32[8,128]{1,0:T(8,128)S(1)} %get-tuple-element.59.table, f32[2,640,512]{2,1,0:T(8,128)S(1)} %get-tuple-element.60.s_own, f32[640,128]{1,0:T(8,128)S(1)} %get-tuple-element.61.s_edge), custom_call_target="tpu_custom_call" | custom-call | flops 419430400 | bytes 3000000 | tf_op jit(solution)/shard_map/pallas_call | solution.py:284
  24.4 0.0 collective-permute-done.5.far_ref
  24.4 3.8 %shard_map.94 = bf16[64,16,256]{2,1,0:T(8,128)(2,1)} custom-call(f32[4,32,128]{2,1,0:T(8,128)S(1)} %collective-permute-done.5.far_ref, f32[8,128]{1,0:T(8,128)S(1)} %get-tuple-element.59.table, f32[2,640,512]{2,1,0:T(8,128)S(1)} %get-tuple-element.60.s_own, f32[640,128]{1,0:T(8,128)S(1)} %get-tuple-element.62.s_edge, ...), custom_call_target="tpu_custom_call" | custom-call | tf_op jit(solution)/shard_map/pallas_call | solution.py:301
  (4 shorter events, 0.0 us)
Async XLA Ops:
  0.8 4.2 %collective-permute-start = (f32[32,32]{1,0:T(8,128)S(1)}, f32[32,32]{1,0:T(8,128)S(1)}, u32[]{:S(2)}, u32[]{:S(2)}) collective-permute-start(f32[32,32]{1,0:T(8,128)S(1)} %convert_add_fusion), channel_id=1, source_target_pairs={{0,16},{16,0},{32,48},{48,32},{64,80},{80,64},{96,112},{112,96},{1... | collective-permute-start | bytes 12296 | tf_op jit(solution)/shard_map/ppermute | solution.py:365
  5.1 4.1 %collective-permute-start.1 = (f32[32,64]{1,0:T(8,128)S(1)}, f32[32,64]{1,0:T(8,128)S(1)}, u32[]{:S(2)}, u32[]{:S(2)}) collective-permute-start(f32[32,64]{1,0:T(8,128)S(1)} %pad_maximum_fusion.1), channel_id=1, source_target_pairs={{0,32},{16,48},{32,0},{48,16},{64,96},{80,112},{96,64},{112,80},{1... | collective-permute-start | bytes 24584 | tf_op jit(solution)/shard_map/ppermute | solution.py:365
  9.3 3.6 %collective-permute-start.3 = (f32[32,128]{1,0:T(8,128)S(1)}, f32[32,128]{1,0:T(8,128)S(1)}, u32[]{:S(2)}, u32[]{:S(2)}) collective-permute-start(f32[32,128]{1,0:T(8,128)S(1)} %pad_maximum_fusion.2), channel_id=1, source_target_pairs={{0,64},{16,208},{32,96},{48,240},{64,128},{80,16},{96,160},{112,48... | collective-permute-start | bytes 49160 | tf_op jit(solution)/shard_map/ppermute | solution.py:365
  10.9 4.9 %collective-permute-start.2 = (f32[32,128]{1,0:T(8,128)S(1)}, f32[32,128]{1,0:T(8,128)S(1)}, u32[]{:S(2)}, u32[]{:S(2)}) collective-permute-start(f32[32,128]{1,0:T(8,128)S(1)} %pad_maximum_fusion.2), channel_id=1, source_target_pairs={{0,144},{16,128},{32,176},{48,160},{64,208},{80,192},{96,240},{112... | collective-permute-start | bytes 49160 | tf_op jit(solution)/shard_map/ppermute | solution.py:365
  12.9 3.7 %collective-permute-start.4 = (f32[32,128]{1,0:T(8,128)S(1)}, f32[32,128]{1,0:T(8,128)S(1)}, u32[]{:S(2)}, u32[]{:S(2)}) collective-permute-start(f32[32,128]{1,0:T(8,128)S(1)} %collective-permute-done.3), channel_id=1, source_target_pairs={{0,16},{16,0},{32,48},{48,32},{64,80},{80,64},{96,112},{112,96},{1... | collective-permute-start | bytes 49160 | tf_op jit(solution)/shard_map/ppermute | solution.py:365
  16.6 6.9 %collective-permute-start.6 = (f32[4,32,128]{2,1,0:T(8,128)S(1)}, f32[4,32,128]{2,1,0:T(8,128)S(1)}, u32[]{:S(2)}, u32[]{:S(2)}) collective-permute-start(f32[4,32,128]{2,1,0:T(8,128)S(1)} %pad_maximum_fusion.own_ref), channel_id=1, source_target_pairs={{0,1},{1,0},{2,3},{3,2},{4,5},{5,4},{6,7},{7,6},{8,9},{9,8},{10,11... | collective-permute-start | bytes 196616 | tf_op jit(solution)/shard_map/ppermute | solution.py:365
  17.3 7.1 %collective-permute-start.5 = (f32[4,32,128]{2,1,0:T(8,128)S(1)}, f32[4,32,128]{2,1,0:T(8,128)S(1)}, u32[]{:S(2)}, u32[]{:S(2)}) collective-permute-start(f32[4,32,128]{2,1,0:T(8,128)S(1)} %pad_maximum_fusion.own_ref), channel_id=1, source_target_pairs={{0,15},{1,2},{2,1},{3,4},{4,3},{5,6},{6,5},{7,8},{8,7},{9,10},{10,... | collective-permute-start | bytes 196616 | tf_op jit(solution)/shard_map/ppermute | solution.py:365

commit v6 on v5

--- a/solution.py
+++ b/solution.py
@@ -202,15 +202,15 @@
     for pair in range(2):
         rows = slice(pair * 256, (pair + 1) * 256)
         s_far[:, rows] = dot(wt[...], ln[0, rows, :], NT)
-    for i in range(EXT):
-        rows = slice(i * SLOT, (i + 1) * SLOT)
-        for k in range(INSTR):
-            lanes = slice(k * 128, (k + 1) * 128)
-            slot = slice(i * 128 + k * SLOT, i * 128 + (k + 1) * SLOT)
-            far = features_of(s_far[rows, lanes] + s_own[side, rows, lanes])
-            near = f_near[slot, :]
-            feat[slot, 0:128] = jnp.where(near_side == 0, near, far)
-            feat[slot, 128:256] = jnp.where(near_side == 0, far, near)
+        for i in range(EXT):
+            rows = slice(i * SLOT, (i + 1) * SLOT)
+            for k in (2 * pair, 2 * pair + 1):
+                lanes = slice(k * 128, (k + 1) * 128)
+                slot = slice(i * 128 + k * SLOT, i * 128 + (k + 1) * SLOT)
+                far = features_of(s_far[rows, lanes] + s_own[side, rows, lanes])
+                near = f_near[slot, :]
+                feat[slot, 0:128] = jnp.where(near_side == 0, near, far)
+                feat[slot, 128:256] = jnp.where(near_side == 0, far, near)
 
     w1 = w1_ref[...]
     b1 = b1_ref[...]

time: 28.4 us -> 28.4 us (level)
  no operation moved by 1% of the time
where the time goes in v6:
time: 28.4 us; the launch traced here: 28.2 us
  starting transfers between devices  16.6 us (58%)
  Pallas kernels  6.2 us (22%)
  other arithmetic  2.85 us (10%)
  waiting for transfers between devices  1.83 us (6%)
  local copies, waits for them, and re-layouts  0.66 us (2%)
    ppermute x7, starting transfers between devices, send(): lax.ppermute(array, axis, [(i, target(i) % peers) for i in range(peers)])  16.6 us
    pallas_call x1, Pallas kernels, encode(): pl.pallas_call(encode_kernel, out_shape=jax.ShapeDtypeStruct((CHANNELS, C...  3.81 us
    ppermute x7, waiting for transfers between devices, send(): lax.ppermute(array, axis, [(i, target(i) % peers) for i in range(peers)])  1.83 us
    pallas_call x1, Pallas kernels, encode(): pl.pallas_call(own_kernel, out_shape=[jax.ShapeDtypeStruct((2, rows, INST...  1.28 us
    add x1, other arithmetic, arrange(): both = jnp.pad(w_first, ((0, 0), (0, 0), (0, CHANNELS), (0, 0))) + wide  1.04 us
    pallas_call x1, Pallas kernels, encode(): pl.pallas_call(near_kernel, out_shape=[jax.ShapeDtypeStruct((EXT * 128, 1...  0.89 us
    add x1, other arithmetic, pack(): jnp.pad(obs_values, ((1, 1), (0, 0)))  0.82 us
    select_n x1, other arithmetic, pack_small(): return jnp.where(row == 0, along(b_first, shape), small)  0.74 us
  transfers between devices with their start and end apart: 7, of which 3 were waited for; matrix products, arithmetic and copies ran while one was open for 9% of the time, Pallas kernels for 8%

profile of v6, /device:TPU:1, one launch (start us, length us, event | category | flops | bytes accessed | tf_op | source)
XLA Modules:
  0.0 28.2 jit_solution(9202748342167139465)
XLA Ops:
  0.0 0.8 %convert_add_fusion = f32[32,32]{1,0:T(8,128)S(1)} fusion(f32[30,32]{1,0:T(8,128)} %param.9, s32[32]{0:T(128)} %param.11, s32[32]{0:T(128)} %param.12, s32[32]{0:T(128)} %param.10, pred[32]{0:T(512)(128)(4,1)S(1)} %get-tuple-element.69, pred[32]{0:T(512)(128)(4,1)S(1)} %get-tuple-element.70), kind=kLoop, calls=%fused_computation.4 | loop fusion | flops 7168 | bytes 8384 | tf_op jit(solution)/shard_map/add | solution.py:331
  0.8 3.3 %collective-permute-start = (f32[32,32]{1,0:T(8,128)S(1)}, f32[32,32]{1,0:T(8,128)S(1)}, u32[]{:S(2)}, u32[]{:S(2)}) collective-permute-start(f32[32,32]{1,0:T(8,128)S(1)} %convert_add_fusion), channel_id=1, source_target_pairs={{0,16},{16,0},{32,48},{48,32},{64,80},{80,64},{96,112},{112,96},{1... | collective-permute-start | bytes 12296 | tf_op jit(solution)/shard_map/ppermute | solution.py:365
  4.2 0.7 %pad.17 = f32[64]{0:T(128)S(1)} pad(f32[4]{0:T(128)} %param.13, f32[]{:T(128)} %constant.7.clone.1), padding=0_60 | pad | bytes 276 | tf_op jit(solution)/shard_map/jit(_pad)/pad | solution.py:373
  4.8 0.2 collective-permute-done
  5.0 0.1 pad_maximum_fusion.1
  5.1 1.2 %collective-permute-start.1 = (f32[32,64]{1,0:T(8,128)S(1)}, f32[32,64]{1,0:T(8,128)S(1)}, u32[]{:S(2)}, u32[]{:S(2)}) collective-permute-start(f32[32,64]{1,0:T(8,128)S(1)} %pad_maximum_fusion.1), channel_id=1, source_target_pairs={{0,32},{16,48},{32,0},{48,16},{64,96},{80,112},{96,64},{112,80},{1... | collective-permute-start | bytes 24584 | tf_op jit(solution)/shard_map/ppermute | solution.py:365
  6.3 0.7 %select_select_fusion.small = f32[8,64]{1,0:T(8,128)S(1)} fusion(f32[64]{0:T(128)S(1)} %pad.17, f32[64]{0:T(128)} %param.17, f32[64]{0:T(128)} %param.15, pred[8]{0:T(512)(128)(4,1)S(1)} %get-tuple-element.71, pred[8]{0:T(512)(128)(4,1)S(1)} %get-tuple-element.72, pred[8]{0:T(512)(128)(4,1)S(1)} %iota_compare_fusion.2), kind=kLoop, calls=%fused_computation.5 | loop fusion | flops 1536 | bytes 2840 | tf_op jit(solution)/shard_map/jit(_where)/select_n | solution.py:339
  7.0 1.0 %pad_add_fusion.both = bf16[3,3,128,124]{3,2,1,0:T(8,128)(2,1)S(1)} fusion(bf16[3,3,64,64]{3,2,1,0:T(8,128)(2,1)} %param.16, bf16[3,3,64,124]{3,2,1,0:T(8,128)(2,1)} %param.14), kind=kLoop, calls=%fused_computation | loop fusion | flops 571392 | bytes 502272 | tf_op jit(solution)/shard_map/add | solution.py:345
  8.1 0.2 shard_map.91
  8.3 0.9 %collective-permute-done.1 = f32[32,64]{1,0:T(8,128)S(1)} collective-permute-done((f32[32,64]{1,0:T(8,128)S(1)}, f32[32,64]{1,0:T(8,128)S(1)}, u32[]{:S(2)}, u32[]{:S(2)}) %collective-permute-start.1) | collective-permute-done | bytes 8224 | tf_op jit(solution)/shard_map/ppermute | solution.py:365
  9.2 0.1 pad_maximum_fusion.2
  9.3 1.6 %collective-permute-start.3 = (f32[32,128]{1,0:T(8,128)S(1)}, f32[32,128]{1,0:T(8,128)S(1)}, u32[]{:S(2)}, u32[]{:S(2)}) collective-permute-start(f32[32,128]{1,0:T(8,128)S(1)} %pad_maximum_fusion.2), channel_id=1, source_target_pairs={{0,64},{16,208},{32,96},{48,240},{64,128},{80,16},{96,160},{112,48... | collective-permute-start | bytes 49160 | tf_op jit(solution)/shard_map/ppermute | solution.py:365
  10.9 2.0 %collective-permute-start.2 = (f32[32,128]{1,0:T(8,128)S(1)}, f32[32,128]{1,0:T(8,128)S(1)}, u32[]{:S(2)}, u32[]{:S(2)}) collective-permute-start(f32[32,128]{1,0:T(8,128)S(1)} %pad_maximum_fusion.2), channel_id=1, source_target_pairs={{0,144},{16,128},{32,176},{48,160},{64,208},{80,192},{96,240},{112... | collective-permute-start | bytes 49160 | tf_op jit(solution)/shard_map/ppermute | solution.py:365
  12.9 0.0 collective-permute-done.3
  12.9 2.9 %collective-permute-start.4 = (f32[32,128]{1,0:T(8,128)S(1)}, f32[32,128]{1,0:T(8,128)S(1)}, u32[]{:S(2)}, u32[]{:S(2)}) collective-permute-start(f32[32,128]{1,0:T(8,128)S(1)} %collective-permute-done.3), channel_id=1, source_target_pairs={{0,16},{16,0},{32,48},{48,32},{64,80},{80,64},{96,112},{112,96},{1... | collective-permute-start | bytes 49160 | tf_op jit(solution)/shard_map/ppermute | solution.py:365
  15.7 0.1 fusion
  15.8 0.0 collective-permute-done.2
  15.8 0.8 %collective-permute-done.4 = f32[32,128]{1,0:T(8,128)S(1)} collective-permute-done((f32[32,128]{1,0:T(8,128)S(1)}, f32[32,128]{1,0:T(8,128)S(1)}, u32[]{:S(2)}, u32[]{:S(2)}) %collective-permute-start.4) | collective-permute-done | bytes 16416 | tf_op jit(solution)/shard_map/ppermute | solution.py:365
  16.6 0.7 %collective-permute-start.6 = (f32[4,32,128]{2,1,0:T(8,128)S(1)}, f32[4,32,128]{2,1,0:T(8,128)S(1)}, u32[]{:S(2)}, u32[]{:S(2)}) collective-permute-start(f32[4,32,128]{2,1,0:T(8,128)S(1)} %pad_maximum_fusion.own_ref), channel_id=1, source_target_pairs={{0,1},{1,0},{2,3},{3,2},{4,5},{5,4},{6,7},{7,6},{8,9},{9,8},{10,11... | collective-permute-start | bytes 196616 | tf_op jit(solution)/shard_map/ppermute | solution.py:365
  17.3 4.9 %collective-permute-start.5 = (f32[4,32,128]{2,1,0:T(8,128)S(1)}, f32[4,32,128]{2,1,0:T(8,128)S(1)}, u32[]{:S(2)}, u32[]{:S(2)}) collective-permute-start(f32[4,32,128]{2,1,0:T(8,128)S(1)} %pad_maximum_fusion.own_ref), channel_id=1, source_target_pairs={{0,15},{1,2},{2,1},{3,4},{4,3},{5,6},{6,5},{7,8},{8,7},{9,10},{10,... | collective-permute-start | bytes 196616 | tf_op jit(solution)/shard_map/ppermute | solution.py:365
  22.2 1.3 %shard_map.92 = (f32[2,640,512]{2,1,0:T(8,128)S(1)}, f32[640,128]{1,0:T(8,128)S(1)}) custom-call(f32[4,32,128]{2,1,0:T(8,128)S(1)} %pad_maximum_fusion.own_ref, f32[8,128]{1,0:T(8,128)S(1)} %get-tuple-element.59.table), custom_call_target="tpu_custom_call" | custom-call | flops 754974720 | bytes 3000000 | tf_op jit(solution)/shard_map/pallas_call | solution.py:268
  23.5 0.0 collective-permute-done.6.near_ref
  23.5 0.9 %shard_map.93 = (bf16[2560,128]{1,0:T(8,128)(2,1)S(1)}, f32[640,128]{1,0:T(8,128)S(1)}) custom-call(f32[4,32,128]{2,1,0:T(8,128)S(1)} %collective-permute-done.6.near_ref, f32[8,128]{1,0:T(8,128)S(1)} %get-tuple-element.59.table, f32[2,640,512]{2,1,0:T(8,128)S(1)} %get-tuple-element.60.s_own, f32[640,128]{1,0:T(8,128)S(1)} %get-tuple-element.61.s_edge), custom_call_target="tpu_custom_call" | custom-call | flops 419430400 | bytes 3000000 | tf_op jit(solution)/shard_map/pallas_call | solution.py:284
  24.4 0.0 collective-permute-done.5.far_ref
  24.4 3.8 %shard_map.94 = bf16[64,16,256]{2,1,0:T(8,128)(2,1)} custom-call(f32[4,32,128]{2,1,0:T(8,128)S(1)} %collective-permute-done.5.far_ref, f32[8,128]{1,0:T(8,128)S(1)} %get-tuple-element.59.table, f32[2,640,512]{2,1,0:T(8,128)S(1)} %get-tuple-element.60.s_own, f32[640,128]{1,0:T(8,128)S(1)} %get-tuple-element.62.s_edge, ...), custom_call_target="tpu_custom_call" | custom-call | tf_op jit(solution)/shard_map/pallas_call | solution.py:301
  (4 shorter events, 0.0 us)
Async XLA Ops:
  0.8 4.2 %collective-permute-start = (f32[32,32]{1,0:T(8,128)S(1)}, f32[32,32]{1,0:T(8,128)S(1)}, u32[]{:S(2)}, u32[]{:S(2)}) collective-permute-start(f32[32,32]{1,0:T(8,128)S(1)} %convert_add_fusion), channel_id=1, source_target_pairs={{0,16},{16,0},{32,48},{48,32},{64,80},{80,64},{96,112},{112,96},{1... | collective-permute-start | bytes 12296 | tf_op jit(solution)/shard_map/ppermute | solution.py:365
  5.1 4.1 %collective-permute-start.1 = (f32[32,64]{1,0:T(8,128)S(1)}, f32[32,64]{1,0:T(8,128)S(1)}, u32[]{:S(2)}, u32[]{:S(2)}) collective-permute-start(f32[32,64]{1,0:T(8,128)S(1)} %pad_maximum_fusion.1), channel_id=1, source_target_pairs={{0,32},{16,48},{32,0},{48,16},{64,96},{80,112},{96,64},{112,80},{1... | collective-permute-start | bytes 24584 | tf_op jit(solution)/shard_map/ppermute | solution.py:365
  9.3 3.6 %collective-permute-start.3 = (f32[32,128]{1,0:T(8,128)S(1)}, f32[32,128]{1,0:T(8,128)S(1)}, u32[]{:S(2)}, u32[]{:S(2)}) collective-permute-start(f32[32,128]{1,0:T(8,128)S(1)} %pad_maximum_fusion.2), channel_id=1, source_target_pairs={{0,64},{16,208},{32,96},{48,240},{64,128},{80,16},{96,160},{112,48... | collective-permute-start | bytes 49160 | tf_op jit(solution)/shard_map/ppermute | solution.py:365
  10.9 4.9 %collective-permute-start.2 = (f32[32,128]{1,0:T(8,128)S(1)}, f32[32,128]{1,0:T(8,128)S(1)}, u32[]{:S(2)}, u32[]{:S(2)}) collective-permute-start(f32[32,128]{1,0:T(8,128)S(1)} %pad_maximum_fusion.2), channel_id=1, source_target_pairs={{0,144},{16,128},{32,176},{48,160},{64,208},{80,192},{96,240},{112... | collective-permute-start | bytes 49160 | tf_op jit(solution)/shard_map/ppermute | solution.py:365
  12.9 3.7 %collective-permute-start.4 = (f32[32,128]{1,0:T(8,128)S(1)}, f32[32,128]{1,0:T(8,128)S(1)}, u32[]{:S(2)}, u32[]{:S(2)}) collective-permute-start(f32[32,128]{1,0:T(8,128)S(1)} %collective-permute-done.3), channel_id=1, source_target_pairs={{0,16},{16,0},{32,48},{48,32},{64,80},{80,64},{96,112},{112,96},{1... | collective-permute-start | bytes 49160 | tf_op jit(solution)/shard_map/ppermute | solution.py:365
  16.6 6.9 %collective-permute-start.6 = (f32[4,32,128]{2,1,0:T(8,128)S(1)}, f32[4,32,128]{2,1,0:T(8,128)S(1)}, u32[]{:S(2)}, u32[]{:S(2)}) collective-permute-start(f32[4,32,128]{2,1,0:T(8,128)S(1)} %pad_maximum_fusion.own_ref), channel_id=1, source_target_pairs={{0,1},{1,0},{2,3},{3,2},{4,5},{5,4},{6,7},{7,6},{8,9},{9,8},{10,11... | collective-permute-start | bytes 196616 | tf_op jit(solution)/shard_map/ppermute | solution.py:365
  17.3 7.1 %collective-permute-start.5 = (f32[4,32,128]{2,1,0:T(8,128)S(1)}, f32[4,32,128]{2,1,0:T(8,128)S(1)}, u32[]{:S(2)}, u32[]{:S(2)}) collective-permute-start(f32[4,32,128]{2,1,0:T(8,128)S(1)} %pad_maximum_fusion.own_ref), channel_id=1, source_target_pairs={{0,15},{1,2},{2,1},{3,4},{4,3},{5,6},{6,5},{7,8},{8,7},{9,10},{10,... | collective-permute-start | bytes 196616 | tf_op jit(solution)/shard_map/ppermute | solution.py:365

commit v7 on v5

--- a/solution.py
+++ b/solution.py
@@ -16,7 +16,7 @@
 NLON = 4096
 ROWS_DEV = 32
 STEP = 24
-PARTS = 4
+PARTS = 8
 EXT = CLAT + 4
 HID = CLAT + 2
 EDGE = 6
@@ -175,14 +175,15 @@
 
 
 def row_total(y, terms, row, bias):
-    left = pltpu.roll(y[0:CHANNELS], 1, 1)
-    right = pltpu.roll(y[2 * CHANNELS : 3 * CHANNELS], CLON - 1, 1)
+    halves = (slice(0, 128), slice(128, 256))
     here = pltpu.roll(terms, 128 - (EDGE * row + 1), 1)
     lane = lax.broadcasted_iota(jnp.int32, here.shape, 1)
-    middle = y[CHANNELS : 2 * CHANNELS] + bias
+    left = [pltpu.roll(y[0:CHANNELS, half], 1, 1) for half in halves]
+    right = [pltpu.roll(y[2 * CHANNELS : 3 * CHANNELS, half], 127, 1) for half in halves]
+    middle = [y[CHANNELS : 2 * CHANNELS, half] + bias for half in halves]
     return (
-        middle[:, 0:128] + jnp.where(lane == 0, here, left[:, 0:128]) + right[:, 0:128],
-        middle[:, 128:256] + left[:, 128:256] + jnp.where(lane == 127, here, right[:, 128:256]),
+        middle[0] + jnp.where(lane == 0, here, left[0]) + jnp.where(lane == 127, right[1], right[0]),
+        middle[1] + jnp.where(lane == 0, left[0], left[1]) + jnp.where(lane == 127, here, right[1]),
     )
 
 

time: 28.4 us -> 28.4 us (level)
  no operation moved by 1% of the time
where the time goes in v7:
time: 28.4 us; the launch traced here: 28.3 us
  starting transfers between devices  16.6 us (58%)
  Pallas kernels  6.23 us (22%)
  other arithmetic  2.85 us (10%)
  waiting for transfers between devices  1.83 us (6%)
  local copies, waits for them, and re-layouts  0.66 us (2%)
    ppermute x7, starting transfers between devices, send(): lax.ppermute(array, axis, [(i, target(i) % peers) for i in range(peers)])  16.6 us
    pallas_call x1, Pallas kernels, encode(): pl.pallas_call(encode_kernel, out_shape=jax.ShapeDtypeStruct((CHANNELS, C...  3.84 us
    ppermute x7, waiting for transfers between devices, send(): lax.ppermute(array, axis, [(i, target(i) % peers) for i in range(peers)])  1.83 us
    pallas_call x1, Pallas kernels, encode(): pl.pallas_call(own_kernel, out_shape=[jax.ShapeDtypeStruct((2, rows, INST...  1.28 us
    add x1, other arithmetic, arrange(): both = jnp.pad(w_first, ((0, 0), (0, 0), (0, CHANNELS), (0, 0))) + wide  1.04 us
    pallas_call x1, Pallas kernels, encode(): pl.pallas_call(near_kernel, out_shape=[jax.ShapeDtypeStruct((EXT * 128, 1...  0.89 us
    add x1, other arithmetic, pack(): jnp.pad(obs_values, ((1, 1), (0, 0)))  0.82 us
    select_n x1, other arithmetic, pack_small(): return jnp.where(row == 0, along(b_first, shape), small)  0.74 us
  transfers between devices with their start and end apart: 7, of which 3 were waited for; matrix products, arithmetic and copies ran while one was open for 9% of the time, Pallas kernels for 8%

profile of v7, /device:TPU:1, one launch (start us, length us, event | category | flops | bytes accessed | tf_op | source)
XLA Modules:
  0.0 28.3 jit_solution(17450618622886648450)
XLA Ops:
  0.0 0.8 %convert_add_fusion = f32[32,32]{1,0:T(8,128)S(1)} fusion(f32[30,32]{1,0:T(8,128)} %param.9, s32[32]{0:T(128)} %param.11, s32[32]{0:T(128)} %param.12, s32[32]{0:T(128)} %param.10, pred[32]{0:T(512)(128)(4,1)S(1)} %get-tuple-element.69, pred[32]{0:T(512)(128)(4,1)S(1)} %get-tuple-element.70), kind=kLoop, calls=%fused_computation.4 | loop fusion | flops 7168 | bytes 8384 | tf_op jit(solution)/shard_map/add | solution.py:332
  0.8 3.3 %collective-permute-start = (f32[32,32]{1,0:T(8,128)S(1)}, f32[32,32]{1,0:T(8,128)S(1)}, u32[]{:S(2)}, u32[]{:S(2)}) collective-permute-start(f32[32,32]{1,0:T(8,128)S(1)} %convert_add_fusion), channel_id=1, source_target_pairs={{0,16},{16,0},{32,48},{48,32},{64,80},{80,64},{96,112},{112,96},{1... | collective-permute-start | bytes 12296 | tf_op jit(solution)/shard_map/ppermute | solution.py:366
  4.2 0.7 %pad.17 = f32[64]{0:T(128)S(1)} pad(f32[4]{0:T(128)} %param.13, f32[]{:T(128)} %constant.7.clone.1), padding=0_60 | pad | bytes 276 | tf_op jit(solution)/shard_map/jit(_pad)/pad | solution.py:374
  4.8 0.2 collective-permute-done
  5.0 0.1 pad_maximum_fusion.1
  5.1 1.2 %collective-permute-start.1 = (f32[32,64]{1,0:T(8,128)S(1)}, f32[32,64]{1,0:T(8,128)S(1)}, u32[]{:S(2)}, u32[]{:S(2)}) collective-permute-start(f32[32,64]{1,0:T(8,128)S(1)} %pad_maximum_fusion.1), channel_id=1, source_target_pairs={{0,32},{16,48},{32,0},{48,16},{64,96},{80,112},{96,64},{112,80},{1... | collective-permute-start | bytes 24584 | tf_op jit(solution)/shard_map/ppermute | solution.py:366
  6.3 0.7 %select_select_fusion.small = f32[8,64]{1,0:T(8,128)S(1)} fusion(f32[64]{0:T(128)S(1)} %pad.17, f32[64]{0:T(128)} %param.17, f32[64]{0:T(128)} %param.15, pred[8]{0:T(512)(128)(4,1)S(1)} %get-tuple-element.71, pred[8]{0:T(512)(128)(4,1)S(1)} %get-tuple-element.72, pred[8]{0:T(512)(128)(4,1)S(1)} %iota_compare_fusion.2), kind=kLoop, calls=%fused_computation.5 | loop fusion | flops 1536 | bytes 2840 | tf_op jit(solution)/shard_map/jit(_where)/select_n | solution.py:340
  7.0 1.0 %pad_add_fusion.both = bf16[3,3,128,124]{3,2,1,0:T(8,128)(2,1)S(1)} fusion(bf16[3,3,64,64]{3,2,1,0:T(8,128)(2,1)} %param.16, bf16[3,3,64,124]{3,2,1,0:T(8,128)(2,1)} %param.14), kind=kLoop, calls=%fused_computation | loop fusion | flops 571392 | bytes 502272 | tf_op jit(solution)/shard_map/add | solution.py:346
  8.1 0.2 shard_map.91
  8.3 0.9 %collective-permute-done.1 = f32[32,64]{1,0:T(8,128)S(1)} collective-permute-done((f32[32,64]{1,0:T(8,128)S(1)}, f32[32,64]{1,0:T(8,128)S(1)}, u32[]{:S(2)}, u32[]{:S(2)}) %collective-permute-start.1) | collective-permute-done | bytes 8224 | tf_op jit(solution)/shard_map/ppermute | solution.py:366
  9.2 0.1 pad_maximum_fusion.2
  9.3 1.6 %collective-permute-start.3 = (f32[32,128]{1,0:T(8,128)S(1)}, f32[32,128]{1,0:T(8,128)S(1)}, u32[]{:S(2)}, u32[]{:S(2)}) collective-permute-start(f32[32,128]{1,0:T(8,128)S(1)} %pad_maximum_fusion.2), channel_id=1, source_target_pairs={{0,64},{16,208},{32,96},{48,240},{64,128},{80,16},{96,160},{112,48... | collective-permute-start | bytes 49160 | tf_op jit(solution)/shard_map/ppermute | solution.py:366
  10.9 2.0 %collective-permute-start.2 = (f32[32,128]{1,0:T(8,128)S(1)}, f32[32,128]{1,0:T(8,128)S(1)}, u32[]{:S(2)}, u32[]{:S(2)}) collective-permute-start(f32[32,128]{1,0:T(8,128)S(1)} %pad_maximum_fusion.2), channel_id=1, source_target_pairs={{0,144},{16,128},{32,176},{48,160},{64,208},{80,192},{96,240},{112... | collective-permute-start | bytes 49160 | tf_op jit(solution)/shard_map/ppermute | solution.py:366
  12.9 0.0 collective-permute-done.3
  12.9 2.9 %collective-permute-start.4 = (f32[32,128]{1,0:T(8,128)S(1)}, f32[32,128]{1,0:T(8,128)S(1)}, u32[]{:S(2)}, u32[]{:S(2)}) collective-permute-start(f32[32,128]{1,0:T(8,128)S(1)} %collective-permute-done.3), channel_id=1, source_target_pairs={{0,16},{16,0},{32,48},{48,32},{64,80},{80,64},{96,112},{112,96},{1... | collective-permute-start | bytes 49160 | tf_op jit(solution)/shard_map/ppermute | solution.py:366
  15.7 0.1 fusion
  15.8 0.0 collective-permute-done.2
  15.8 0.8 %collective-permute-done.4 = f32[32,128]{1,0:T(8,128)S(1)} collective-permute-done((f32[32,128]{1,0:T(8,128)S(1)}, f32[32,128]{1,0:T(8,128)S(1)}, u32[]{:S(2)}, u32[]{:S(2)}) %collective-permute-start.4) | collective-permute-done | bytes 16416 | tf_op jit(solution)/shard_map/ppermute | solution.py:366
  16.6 0.7 %collective-permute-start.6 = (f32[4,32,128]{2,1,0:T(8,128)S(1)}, f32[4,32,128]{2,1,0:T(8,128)S(1)}, u32[]{:S(2)}, u32[]{:S(2)}) collective-permute-start(f32[4,32,128]{2,1,0:T(8,128)S(1)} %pad_maximum_fusion.own_ref), channel_id=1, source_target_pairs={{0,1},{1,0},{2,3},{3,2},{4,5},{5,4},{6,7},{7,6},{8,9},{9,8},{10,11... | collective-permute-start | bytes 196616 | tf_op jit(solution)/shard_map/ppermute | solution.py:366
  17.3 4.9 %collective-permute-start.5 = (f32[4,32,128]{2,1,0:T(8,128)S(1)}, f32[4,32,128]{2,1,0:T(8,128)S(1)}, u32[]{:S(2)}, u32[]{:S(2)}) collective-permute-start(f32[4,32,128]{2,1,0:T(8,128)S(1)} %pad_maximum_fusion.own_ref), channel_id=1, source_target_pairs={{0,15},{1,2},{2,1},{3,4},{4,3},{5,6},{6,5},{7,8},{8,7},{9,10},{10,... | collective-permute-start | bytes 196616 | tf_op jit(solution)/shard_map/ppermute | solution.py:366
  22.2 1.3 %shard_map.92 = (f32[2,640,512]{2,1,0:T(8,128)S(1)}, f32[640,128]{1,0:T(8,128)S(1)}) custom-call(f32[4,32,128]{2,1,0:T(8,128)S(1)} %pad_maximum_fusion.own_ref, f32[8,128]{1,0:T(8,128)S(1)} %get-tuple-element.59.table), custom_call_target="tpu_custom_call" | custom-call | flops 754974720 | bytes 3000000 | tf_op jit(solution)/shard_map/pallas_call | solution.py:269
  23.5 0.0 collective-permute-done.6.near_ref
  23.5 0.9 %shard_map.93 = (bf16[2560,128]{1,0:T(8,128)(2,1)S(1)}, f32[640,128]{1,0:T(8,128)S(1)}) custom-call(f32[4,32,128]{2,1,0:T(8,128)S(1)} %collective-permute-done.6.near_ref, f32[8,128]{1,0:T(8,128)S(1)} %get-tuple-element.59.table, f32[2,640,512]{2,1,0:T(8,128)S(1)} %get-tuple-element.60.s_own, f32[640,128]{1,0:T(8,128)S(1)} %get-tuple-element.61.s_edge), custom_call_target="tpu_custom_call" | custom-call | flops 419430400 | bytes 3000000 | tf_op jit(solution)/shard_map/pallas_call | solution.py:285
  24.4 0.0 collective-permute-done.5.far_ref
  24.4 3.8 %shard_map.94 = bf16[64,16,256]{2,1,0:T(8,128)(2,1)} custom-call(f32[4,32,128]{2,1,0:T(8,128)S(1)} %collective-permute-done.5.far_ref, f32[8,128]{1,0:T(8,128)S(1)} %get-tuple-element.59.table, f32[2,640,512]{2,1,0:T(8,128)S(1)} %get-tuple-element.60.s_own, f32[640,128]{1,0:T(8,128)S(1)} %get-tuple-element.62.s_edge, ...), custom_call_target="tpu_custom_call" | custom-call | tf_op jit(solution)/shard_map/pallas_call | solution.py:302
  (4 shorter events, 0.0 us)
Async XLA Ops:
  0.8 4.2 %collective-permute-start = (f32[32,32]{1,0:T(8,128)S(1)}, f32[32,32]{1,0:T(8,128)S(1)}, u32[]{:S(2)}, u32[]{:S(2)}) collective-permute-start(f32[32,32]{1,0:T(8,128)S(1)} %convert_add_fusion), channel_id=1, source_target_pairs={{0,16},{16,0},{32,48},{48,32},{64,80},{80,64},{96,112},{112,96},{1... | collective-permute-start | bytes 12296 | tf_op jit(solution)/shard_map/ppermute | solution.py:366
  5.1 4.1 %collective-permute-start.1 = (f32[32,64]{1,0:T(8,128)S(1)}, f32[32,64]{1,0:T(8,128)S(1)}, u32[]{:S(2)}, u32[]{:S(2)}) collective-permute-start(f32[32,64]{1,0:T(8,128)S(1)} %pad_maximum_fusion.1), channel_id=1, source_target_pairs={{0,32},{16,48},{32,0},{48,16},{64,96},{80,112},{96,64},{112,80},{1... | collective-permute-start | bytes 24584 | tf_op jit(solution)/shard_map/ppermute | solution.py:366
  9.3 3.6 %collective-permute-start.3 = (f32[32,128]{1,0:T(8,128)S(1)}, f32[32,128]{1,0:T(8,128)S(1)}, u32[]{:S(2)}, u32[]{:S(2)}) collective-permute-start(f32[32,128]{1,0:T(8,128)S(1)} %pad_maximum_fusion.2), channel_id=1, source_target_pairs={{0,64},{16,208},{32,96},{48,240},{64,128},{80,16},{96,160},{112,48... | collective-permute-start | bytes 49160 | tf_op jit(solution)/shard_map/ppermute | solution.py:366
  10.9 4.9 %collective-permute-start.2 = (f32[32,128]{1,0:T(8,128)S(1)}, f32[32,128]{1,0:T(8,128)S(1)}, u32[]{:S(2)}, u32[]{:S(2)}) collective-permute-start(f32[32,128]{1,0:T(8,128)S(1)} %pad_maximum_fusion.2), channel_id=1, source_target_pairs={{0,144},{16,128},{32,176},{48,160},{64,208},{80,192},{96,240},{112... | collective-permute-start | bytes 49160 | tf_op jit(solution)/shard_map/ppermute | solution.py:366
  12.9 3.7 %collective-permute-start.4 = (f32[32,128]{1,0:T(8,128)S(1)}, f32[32,128]{1,0:T(8,128)S(1)}, u32[]{:S(2)}, u32[]{:S(2)}) collective-permute-start(f32[32,128]{1,0:T(8,128)S(1)} %collective-permute-done.3), channel_id=1, source_target_pairs={{0,16},{16,0},{32,48},{48,32},{64,80},{80,64},{96,112},{112,96},{1... | collective-permute-start | bytes 49160 | tf_op jit(solution)/shard_map/ppermute | solution.py:366
  16.6 6.9 %collective-permute-start.6 = (f32[4,32,128]{2,1,0:T(8,128)S(1)}, f32[4,32,128]{2,1,0:T(8,128)S(1)}, u32[]{:S(2)}, u32[]{:S(2)}) collective-permute-start(f32[4,32,128]{2,1,0:T(8,128)S(1)} %pad_maximum_fusion.own_ref), channel_id=1, source_target_pairs={{0,1},{1,0},{2,3},{3,2},{4,5},{5,4},{6,7},{7,6},{8,9},{9,8},{10,11... | collective-permute-start | bytes 196616 | tf_op jit(solution)/shard_map/ppermute | solution.py:366
  17.3 7.1 %collective-permute-start.5 = (f32[4,32,128]{2,1,0:T(8,128)S(1)}, f32[4,32,128]{2,1,0:T(8,128)S(1)}, u32[]{:S(2)}, u32[]{:S(2)}) collective-permute-start(f32[4,32,128]{2,1,0:T(8,128)S(1)} %pad_maximum_fusion.own_ref), channel_id=1, source_target_pairs={{0,15},{1,2},{2,1},{3,4},{4,3},{5,6},{6,5},{7,8},{8,7},{9,10},{10,... | collective-permute-start | bytes 196616 | tf_op jit(solution)/shard_map/ppermute | solution.py:366

commit v8 on v7

--- a/solution.py
+++ b/solution.py
@@ -381,10 +381,10 @@
         (rows, b_first, b_second, w_first, w_second)
     )
     weights = arrange(w_first, w_second, pack_small(b_first, b_second, scale))
-    others = send(rows, "lat", lambda i: i ^ 2)
+    others = send(rows, "lat", lambda i: i ^ 3)
     rows, others, weights = lax.optimization_barrier((rows, others, weights))
     rows = jnp.concatenate([rows, others], axis=1)
-    across = send(rows, "lat", lambda i: i ^ 9)
+    across = send(rows, "lat", lambda i: i ^ 8)
     beside = send(rows, "lat", lambda i: i + 4 if i % 2 == 0 else i - 4)
     others = [across, send(beside, "lat", lambda i: i ^ 1), beside]
     rows = jnp.stack([rows] + others)

time: 28.4 us -> 28.4 us (level)
  waiting for transfers between devices: 1.83 us -> 2.98 us
  starting transfers between devices: 16.6 us -> 15.5 us
    ppermute x7, starting transfers between devices: 16.6 us -> 15.5 us  [send(): lax.ppermute(array, axis, [(i, target(i) % peers) for i in range(peers)])]
    ppermute x7, waiting for transfers between devices: 1.83 us -> 2.98 us  [send(): lax.ppermute(array, axis, [(i, target(i) % peers) for i in range(peers)])]
  transfers between devices with their start and end apart: 7 -> 7, of which waited for: 3 -> 4; matrix products, arithmetic and copies ran while one was open for 9% -> 9% of each run, Pallas kernels for 8% -> 8%
where the time goes in v8:
time: 28.4 us; the launch traced here: 28.3 us
  starting transfers between devices  15.5 us (55%)
  Pallas kernels  6.24 us (22%)
  waiting for transfers between devices  2.98 us (10%)
  other arithmetic  2.85 us (10%)
  local copies, waits for them, and re-layouts  0.66 us (2%)
    ppermute x7, starting transfers between devices, send(): lax.ppermute(array, axis, [(i, target(i) % peers) for i in range(peers)])  15.5 us
    pallas_call x1, Pallas kernels, encode(): pl.pallas_call(encode_kernel, out_shape=jax.ShapeDtypeStruct((CHANNELS, C...  3.84 us
    ppermute x7, waiting for transfers between devices, send(): lax.ppermute(array, axis, [(i, target(i) % peers) for i in range(peers)])  2.98 us
    pallas_call x1, Pallas kernels, encode(): pl.pallas_call(own_kernel, out_shape=[jax.ShapeDtypeStruct((2, rows, INST...  1.28 us
    add x1, other arithmetic, arrange(): both = jnp.pad(w_first, ((0, 0), (0, 0), (0, CHANNELS), (0, 0))) + wide  1.04 us
    pallas_call x1, Pallas kernels, encode(): pl.pallas_call(near_kernel, out_shape=[jax.ShapeDtypeStruct((EXT * 128, 1...  0.89 us
    add x1, other arithmetic, pack(): jnp.pad(obs_values, ((1, 1), (0, 0)))  0.82 us
    select_n x1, other arithmetic, pack_small(): return jnp.where(row == 0, along(b_first, shape), small)  0.74 us
  transfers between devices with their start and end apart: 7, of which 4 were waited for; matrix products, arithmetic and copies ran while one was open for 9% of the time, Pallas kernels for 8%

profile of v8, /device:TPU:1, one launch (start us, length us, event | category | flops | bytes accessed | tf_op | source)
XLA Modules:
  0.0 28.3 jit_solution(9710616737456175287)
XLA Ops:
  0.0 0.8 %convert_add_fusion = f32[32,32]{1,0:T(8,128)S(1)} fusion(f32[30,32]{1,0:T(8,128)} %param.9, s32[32]{0:T(128)} %param.11, s32[32]{0:T(128)} %param.12, s32[32]{0:T(128)} %param.10, pred[32]{0:T(512)(128)(4,1)S(1)} %get-tuple-element.69, pred[32]{0:T(512)(128)(4,1)S(1)} %get-tuple-element.70), kind=kLoop, calls=%fused_computation.4 | loop fusion | flops 7168 | bytes 8384 | tf_op jit(solution)/shard_map/add | solution.py:332
  0.8 3.3 %collective-permute-start = (f32[32,32]{1,0:T(8,128)S(1)}, f32[32,32]{1,0:T(8,128)S(1)}, u32[]{:S(2)}, u32[]{:S(2)}) collective-permute-start(f32[32,32]{1,0:T(8,128)S(1)} %convert_add_fusion), channel_id=1, source_target_pairs={{0,16},{16,0},{32,48},{48,32},{64,80},{80,64},{96,112},{112,96},{1... | collective-permute-start | bytes 12296 | tf_op jit(solution)/shard_map/ppermute | solution.py:366
  4.2 0.7 %pad.17 = f32[64]{0:T(128)S(1)} pad(f32[4]{0:T(128)} %param.13, f32[]{:T(128)} %constant.7.clone.1), padding=0_60 | pad | bytes 276 | tf_op jit(solution)/shard_map/jit(_pad)/pad | solution.py:374
  4.8 0.2 collective-permute-done
  5.0 0.1 pad_maximum_fusion.1
  5.1 1.4 %collective-permute-start.1 = (f32[32,64]{1,0:T(8,128)S(1)}, f32[32,64]{1,0:T(8,128)S(1)}, u32[]{:S(2)}, u32[]{:S(2)}) collective-permute-start(f32[32,64]{1,0:T(8,128)S(1)} %pad_maximum_fusion.1), channel_id=1, source_target_pairs={{0,48},{16,32},{32,16},{48,0},{64,112},{80,96},{96,80},{112,64},{1... | collective-permute-start | bytes 24584 | tf_op jit(solution)/shard_map/ppermute | solution.py:366
  6.5 0.7 %select_select_fusion.small = f32[8,64]{1,0:T(8,128)S(1)} fusion(f32[64]{0:T(128)S(1)} %pad.17, f32[64]{0:T(128)} %param.17, f32[64]{0:T(128)} %param.15, pred[8]{0:T(512)(128)(4,1)S(1)} %get-tuple-element.71, pred[8]{0:T(512)(128)(4,1)S(1)} %get-tuple-element.72, pred[8]{0:T(512)(128)(4,1)S(1)} %iota_compare_fusion.2), kind=kLoop, calls=%fused_computation.5 | loop fusion | flops 1536 | bytes 2840 | tf_op jit(solution)/shard_map/jit(_where)/select_n | solution.py:340
  7.2 1.0 %pad_add_fusion.both = bf16[3,3,128,124]{3,2,1,0:T(8,128)(2,1)S(1)} fusion(bf16[3,3,64,64]{3,2,1,0:T(8,128)(2,1)} %param.16, bf16[3,3,64,124]{3,2,1,0:T(8,128)(2,1)} %param.14), kind=kLoop, calls=%fused_computation | loop fusion | flops 571392 | bytes 502272 | tf_op jit(solution)/shard_map/add | solution.py:346
  8.3 0.2 shard_map.91
  8.5 1.2 %collective-permute-done.1 = f32[32,64]{1,0:T(8,128)S(1)} collective-permute-done((f32[32,64]{1,0:T(8,128)S(1)}, f32[32,64]{1,0:T(8,128)S(1)}, u32[]{:S(2)}, u32[]{:S(2)}) %collective-permute-start.1) | collective-permute-done | bytes 8224 | tf_op jit(solution)/shard_map/ppermute | solution.py:366
  9.8 0.1 pad_maximum_fusion.2
  9.8 1.3 %collective-permute-start.3 = (f32[32,128]{1,0:T(8,128)S(1)}, f32[32,128]{1,0:T(8,128)S(1)}, u32[]{:S(2)}, u32[]{:S(2)}) collective-permute-start(f32[32,128]{1,0:T(8,128)S(1)} %pad_maximum_fusion.2), channel_id=1, source_target_pairs={{0,64},{16,208},{32,96},{48,240},{64,128},{80,16},{96,160},{112,48... | collective-permute-start | bytes 49160 | tf_op jit(solution)/shard_map/ppermute | solution.py:366
  11.1 0.5 %collective-permute-start.2 = (f32[32,128]{1,0:T(8,128)S(1)}, f32[32,128]{1,0:T(8,128)S(1)}, u32[]{:S(2)}, u32[]{:S(2)}) collective-permute-start(f32[32,128]{1,0:T(8,128)S(1)} %pad_maximum_fusion.2), channel_id=1, source_target_pairs={{0,128},{16,144},{32,160},{48,176},{64,192},{80,208},{96,224},{112... | collective-permute-start | bytes 49160 | tf_op jit(solution)/shard_map/ppermute | solution.py:366
  11.6 0.8 %collective-permute-done.3 = f32[32,128]{1,0:T(8,128)S(1)} collective-permute-done((f32[32,128]{1,0:T(8,128)S(1)}, f32[32,128]{1,0:T(8,128)S(1)}, u32[]{:S(2)}, u32[]{:S(2)}) %collective-permute-start.3) | collective-permute-done | bytes 16416 | tf_op jit(solution)/shard_map/ppermute | solution.py:366
  12.4 2.7 %collective-permute-start.4 = (f32[32,128]{1,0:T(8,128)S(1)}, f32[32,128]{1,0:T(8,128)S(1)}, u32[]{:S(2)}, u32[]{:S(2)}) collective-permute-start(f32[32,128]{1,0:T(8,128)S(1)} %collective-permute-done.3), channel_id=1, source_target_pairs={{0,16},{16,0},{32,48},{48,32},{64,80},{80,64},{96,112},{112,96},{1... | collective-permute-start | bytes 49160 | tf_op jit(solution)/shard_map/ppermute | solution.py:366
  15.2 0.1 fusion
  15.2 0.0 collective-permute-done.2
  15.2 0.8 %collective-permute-done.4 = f32[32,128]{1,0:T(8,128)S(1)} collective-permute-done((f32[32,128]{1,0:T(8,128)S(1)}, f32[32,128]{1,0:T(8,128)S(1)}, u32[]{:S(2)}, u32[]{:S(2)}) %collective-permute-start.4) | collective-permute-done | bytes 16416 | tf_op jit(solution)/shard_map/ppermute | solution.py:366
  16.0 0.9 %collective-permute-start.6 = (f32[4,32,128]{2,1,0:T(8,128)S(1)}, f32[4,32,128]{2,1,0:T(8,128)S(1)}, u32[]{:S(2)}, u32[]{:S(2)}) collective-permute-start(f32[4,32,128]{2,1,0:T(8,128)S(1)} %pad_maximum_fusion.own_ref), channel_id=1, source_target_pairs={{0,1},{1,0},{2,3},{3,2},{4,5},{5,4},{6,7},{7,6},{8,9},{9,8},{10,11... | collective-permute-start | bytes 196616 | tf_op jit(solution)/shard_map/ppermute | solution.py:366
  16.9 5.3 %collective-permute-start.5 = (f32[4,32,128]{2,1,0:T(8,128)S(1)}, f32[4,32,128]{2,1,0:T(8,128)S(1)}, u32[]{:S(2)}, u32[]{:S(2)}) collective-permute-start(f32[4,32,128]{2,1,0:T(8,128)S(1)} %pad_maximum_fusion.own_ref), channel_id=1, source_target_pairs={{0,15},{1,2},{2,1},{3,4},{4,3},{5,6},{6,5},{7,8},{8,7},{9,10},{10,... | collective-permute-start | bytes 196616 | tf_op jit(solution)/shard_map/ppermute | solution.py:366
  22.2 1.3 %shard_map.92 = (f32[2,640,512]{2,1,0:T(8,128)S(1)}, f32[640,128]{1,0:T(8,128)S(1)}) custom-call(f32[4,32,128]{2,1,0:T(8,128)S(1)} %pad_maximum_fusion.own_ref, f32[8,128]{1,0:T(8,128)S(1)} %get-tuple-element.59.table), custom_call_target="tpu_custom_call" | custom-call | flops 754974720 | bytes 3000000 | tf_op jit(solution)/shard_map/pallas_call | solution.py:269
  23.5 0.0 collective-permute-done.6.near_ref
  23.5 0.9 %shard_map.93 = (bf16[2560,128]{1,0:T(8,128)(2,1)S(1)}, f32[640,128]{1,0:T(8,128)S(1)}) custom-call(f32[4,32,128]{2,1,0:T(8,128)S(1)} %collective-permute-done.6.near_ref, f32[8,128]{1,0:T(8,128)S(1)} %get-tuple-element.59.table, f32[2,640,512]{2,1,0:T(8,128)S(1)} %get-tuple-element.60.s_own, f32[640,128]{1,0:T(8,128)S(1)} %get-tuple-element.61.s_edge), custom_call_target="tpu_custom_call" | custom-call | flops 419430400 | bytes 3000000 | tf_op jit(solution)/shard_map/pallas_call | solution.py:285
  24.4 0.0 collective-permute-done.5.far_ref
  24.4 3.8 %shard_map.94 = bf16[64,16,256]{2,1,0:T(8,128)(2,1)} custom-call(f32[4,32,128]{2,1,0:T(8,128)S(1)} %collective-permute-done.5.far_ref, f32[8,128]{1,0:T(8,128)S(1)} %get-tuple-element.59.table, f32[2,640,512]{2,1,0:T(8,128)S(1)} %get-tuple-element.60.s_own, f32[640,128]{1,0:T(8,128)S(1)} %get-tuple-element.62.s_edge, ...), custom_call_target="tpu_custom_call" | custom-call | tf_op jit(solution)/shard_map/pallas_call | solution.py:302
  (4 shorter events, 0.0 us)
Async XLA Ops:
  0.8 4.2 %collective-permute-start = (f32[32,32]{1,0:T(8,128)S(1)}, f32[32,32]{1,0:T(8,128)S(1)}, u32[]{:S(2)}, u32[]{:S(2)}) collective-permute-start(f32[32,32]{1,0:T(8,128)S(1)} %convert_add_fusion), channel_id=1, source_target_pairs={{0,16},{16,0},{32,48},{48,32},{64,80},{80,64},{96,112},{112,96},{1... | collective-permute-start | bytes 12296 | tf_op jit(solution)/shard_map/ppermute | solution.py:366
  5.1 4.7 %collective-permute-start.1 = (f32[32,64]{1,0:T(8,128)S(1)}, f32[32,64]{1,0:T(8,128)S(1)}, u32[]{:S(2)}, u32[]{:S(2)}) collective-permute-start(f32[32,64]{1,0:T(8,128)S(1)} %pad_maximum_fusion.1), channel_id=1, source_target_pairs={{0,48},{16,32},{32,16},{48,0},{64,112},{80,96},{96,80},{112,64},{1... | collective-permute-start | bytes 24584 | tf_op jit(solution)/shard_map/ppermute | solution.py:366
  9.8 2.6 %collective-permute-start.3 = (f32[32,128]{1,0:T(8,128)S(1)}, f32[32,128]{1,0:T(8,128)S(1)}, u32[]{:S(2)}, u32[]{:S(2)}) collective-permute-start(f32[32,128]{1,0:T(8,128)S(1)} %pad_maximum_fusion.2), channel_id=1, source_target_pairs={{0,64},{16,208},{32,96},{48,240},{64,128},{80,16},{96,160},{112,48... | collective-permute-start | bytes 49160 | tf_op jit(solution)/shard_map/ppermute | solution.py:366
  11.1 4.1 %collective-permute-start.2 = (f32[32,128]{1,0:T(8,128)S(1)}, f32[32,128]{1,0:T(8,128)S(1)}, u32[]{:S(2)}, u32[]{:S(2)}) collective-permute-start(f32[32,128]{1,0:T(8,128)S(1)} %pad_maximum_fusion.2), channel_id=1, source_target_pairs={{0,128},{16,144},{32,160},{48,176},{64,192},{80,208},{96,224},{112... | collective-permute-start | bytes 49160 | tf_op jit(solution)/shard_map/ppermute | solution.py:366
  12.4 3.5 %collective-permute-start.4 = (f32[32,128]{1,0:T(8,128)S(1)}, f32[32,128]{1,0:T(8,128)S(1)}, u32[]{:S(2)}, u32[]{:S(2)}) collective-permute-start(f32[32,128]{1,0:T(8,128)S(1)} %collective-permute-done.3), channel_id=1, source_target_pairs={{0,16},{16,0},{32,48},{48,32},{64,80},{80,64},{96,112},{112,96},{1... | collective-permute-start | bytes 49160 | tf_op jit(solution)/shard_map/ppermute | solution.py:366
  16.0 7.5 %collective-permute-start.6 = (f32[4,32,128]{2,1,0:T(8,128)S(1)}, f32[4,32,128]{2,1,0:T(8,128)S(1)}, u32[]{:S(2)}, u32[]{:S(2)}) collective-permute-start(f32[4,32,128]{2,1,0:T(8,128)S(1)} %pad_maximum_fusion.own_ref), channel_id=1, source_target_pairs={{0,1},{1,0},{2,3},{3,2},{4,5},{5,4},{6,7},{7,6},{8,9},{9,8},{10,11... | collective-permute-start | bytes 196616 | tf_op jit(solution)/shard_map/ppermute | solution.py:366
  16.9 7.5 %collective-permute-start.5 = (f32[4,32,128]{2,1,0:T(8,128)S(1)}, f32[4,32,128]{2,1,0:T(8,128)S(1)}, u32[]{:S(2)}, u32[]{:S(2)}) collective-permute-start(f32[4,32,128]{2,1,0:T(8,128)S(1)} %pad_maximum_fusion.own_ref), channel_id=1, source_target_pairs={{0,15},{1,2},{2,1},{3,4},{4,3},{5,6},{6,5},{7,8},{8,7},{9,10},{10,... | collective-permute-start | bytes 196616 | tf_op jit(solution)/shard_map/ppermute | solution.py:366
